TPU v7x, 32 devices: a whole 2x2x4 slice. The times are simulated.
32 devices in a mesh: group: 2 (over x), space: 8 (over z, y), rep: 2 (over core).
Axes of the slice: x: 2, y: 2, z: 4, core: 2. Of those that a mesh axis runs over, the one named last changes fastest.
Arguments:
- latent: bfloat16 [4, 128, 8, 256], P(('group', 'rep'), None, 'space'), parts along dimension 0, may hold values from -12 to 12
- first_weight: bfloat16 [64, 64, 128], replicated, may hold values from -0.1875 to 0.1875
- first_norm_gain: float32 [64], replicated, may hold values from 0.25 to 1.75
- first_norm_shift: float32 [64], replicated, may hold values from -0.5 to 0.5
- second_weight: bfloat16 [64, 32, 64], replicated, may hold values from -0.25 to 0.25
- second_norm_gain: float32 [32], replicated, may hold values from 0.25 to 1.75
- second_norm_shift: float32 [32], replicated, may hold values from -0.5 to 0.5
- cotangent: bfloat16 [4, 32, 32, 4096], P(('group', 'rep'), None, 'space'), parts along dimension 0, may hold values from -6 to 6
Outputs:
- features: bfloat16 [4, 32, 32, 4096], P(('group', 'rep'), None, 'space'), parts along dimension 0
- latent_grad: float32 [4, 128, 8, 256], P(('group', 'rep'), None, 'space'), parts along dimension 0
- first_weight_grad: float32 [128, 64, 128], P('group'), parts along dimension 0
- second_weight_grad: float32 [128, 32, 64], P('group'), parts along dimension 0
- first_batchnorm_gradients: float32 [4, 64], P('group'), parts along dimension 0
- second_batchnorm_gradients: float32 [4, 32], P('group'), parts along dimension 0
There are 2 independent parts, one for each index of `group`. A program takes and returns all parts, laid end to end along the dimension named above; an argument that names none is the same for every part. Nothing has to cross between parts.
All inputs are finite; a program needn't handle non-finite values.
Results may differ from a plain program's by a relative error of at most 0.0054.
Values may be sent and summed in bfloat16 or wider, within the bound.
No kernel may reach another device: no remote copies, remote signals or barrier semaphores. Data moves between devices by JAX's collectives and lax.ppermute only.
A program may use at most 64 MiB of HBM per device.

v0:
```python
import jax
import jax.numpy as jnp
from jax import lax
from jax.experimental import pallas as pl
from jax.experimental.pallas import tpu as pltpu
from jax.sharding import PartitionSpec as P

H0 = 4
W0 = 64
CELLS = H0 * W0
C0 = 128
C1 = 64
C2 = 32
EPSILON = 1e-05

F32 = jnp.float32
BF16 = jnp.bfloat16
GROUP = ("space", "rep")

PHASE_TAPS = (((1, 0), (3, -1)), ((2, 0), (0, 1)))
TAP_PHASES = ((1, -1), (0, 0), (1, 0), (0, 1))
FINE_STEPS = {
    (0, -1): (1, -1),
    (0, 0): (0, 0),
    (0, 1): (1, 0),
    (1, -1): (0, 0),
    (1, 0): (1, 0),
    (1, 1): (0, 1),
}


def group_size():
    return lax.axis_size("space") * lax.axis_size("rep")


def exchange_steps():
    steps = []
    for axis in ("rep", "space"):
        bit = 1
        while bit < lax.axis_size(axis):
            steps.append((axis, bit))
            bit *= 2
    return steps


def swap(block, axis, bit):
    return lax.ppermute(block, axis, [(i, i ^ bit) for i in range(lax.axis_size(axis))])


def halving_sum(values):
    steps = exchange_steps()
    part = values
    for axis, bit in steps:
        upper = (lax.axis_index(axis) // bit) % 2
        half = part.shape[0] // 2
        kept = lax.dynamic_slice_in_dim(part, upper * half, half)
        sent = lax.dynamic_slice_in_dim(part, (1 - upper) * half, half).astype(BF16)
        part = kept + swap(sent, axis, bit).astype(F32)
    part = part.astype(BF16)
    for axis, bit in reversed(steps):
        upper = (lax.axis_index(axis) // bit) % 2
        other = swap(part, axis, bit)
        part = jnp.where(
            upper == 0,
            jnp.concatenate([part, other]),
            jnp.concatenate([other, part]),
        )
    return part.astype(F32)


def exchange(copies):
    return lax.all_to_all(copies, GROUP, 0, 0)


def to_above(block):
    count = lax.axis_size("space")
    return lax.ppermute(block, "space", [(i, i + 1) for i in range(count - 1)])


def to_below(block):
    count = lax.axis_size("space")
    return lax.ppermute(block, "space", [(i + 1, i) for i in range(count - 1)])


def call(kernel, outs, args, scratch=()):
    return pl.pallas_call(
        kernel,
        out_shape=[jax.ShapeDtypeStruct(shape, dtype) for shape, dtype in outs],
        in_specs=[pl.BlockSpec(memory_space=pltpu.VMEM)] * len(args),
        out_specs=[pl.BlockSpec(memory_space=pltpu.VMEM)] * len(outs),
        scratch_shapes=list(scratch),
        compiler_params=pltpu.CompilerParams(vmem_limit_bytes=48 * 2**20),
        cost_estimate=pl.CostEstimate(flops=10**9, bytes_accessed=4 * 10**6, transcendentals=0),
    )(*args)


def matmul(a, b):
    return jnp.dot(a, b, preferred_element_type=F32)


def matmul_nt(a, b):
    return lax.dot_general(a, b, (((1,), (1,)), ((), ())), preferred_element_type=F32)


def shift_matrix(dj, dl):
    src = lax.broadcasted_iota(jnp.int32, (CELLS, CELLS), 0)
    dst = lax.broadcasted_iota(jnp.int32, (CELLS, CELLS), 1)
    col = dst % W0 + dl
    hit = (src == dst + dj * W0 + dl) & (col >= 0) & (col < W0)
    return jnp.where(hit, 1.0, 0.0).astype(BF16)


def shift_slot(dj, dl):
    return slice(((dj + 1) * 3 + dl + 1) * CELLS, ((dj + 1) * 3 + dl + 2) * CELLS)


def spread_matrix():
    src = lax.broadcasted_iota(jnp.int32, (512, 512), 0)
    dst = lax.broadcasted_iota(jnp.int32, (512, 512), 1)
    cp2, cp, jj, l = dst // 256, (dst // 128) % 2, (dst // 64) % 2, dst % 64
    return jnp.where(src == jj * 256 + 4 * l + 2 * cp + cp2, 1.0, 0.0).astype(BF16)


def columns(rows):
    return jnp.transpose(jnp.concatenate([rows, jnp.zeros((120, 128), F32)], axis=0))


def emit_rows(ref, first, second):
    lane = lax.broadcasted_iota(jnp.int32, (first.shape[0], 128), 1)
    tile = jnp.where(lane == 0, first, jnp.where(lane == 1, second, 0.0))
    tile = jnp.concatenate([tile] * (128 // first.shape[0]), axis=0)
    rows = jnp.transpose(tile)[0:8, :]
    for k in range(ref.shape[0]):
        ref[k] = rows


def fold(rows, channels):
    total = rows[0:channels]
    for k in range(1, rows.shape[0] // channels):
        total = total + rows[k * channels : (k + 1) * channels]
    return total


def moments(copies, local_count):
    count = copies.shape[0]
    sums = jnp.sum(copies, axis=0)
    mean = sums[0:1] / count
    away = copies - mean[None]
    spread = jnp.sum(away * away, axis=0)[0:1]
    variance = (sums[1:2] + local_count * spread) / (count * local_count)
    return mean, lax.rsqrt(variance + EPSILON)


def sigmoid(values):
    return 1.0 / (1.0 + jnp.exp(-values))


def prepare_kernel(w1_ref, w2_ref, a1_ref, a2_ref, b1_ref, b2_ref, sh_ref):
    for dj in (-1, 0, 1):
        for dl in (-1, 0, 1):
            sh_ref[:, shift_slot(dj, dl)] = shift_matrix(dj, dl)
    a1_ref[...] = jnp.zeros(a1_ref.shape, BF16)
    for par in range(2):
        for rp in range(2):
            for cp in range(2):
                row2 = par * 4 * C2 + (2 * rp + cp) * C2
                pieces = [jnp.zeros((C2, C1), BF16)] * 18
                for p, dp in PHASE_TAPS[par]:
                    dt = dp + 1 - par
                    for q, dr in PHASE_TAPS[rp]:
                        for r, dc in PHASE_TAPS[cp]:
                            tap = 16 * p + 4 * q + r
                            slot = dt * 9 + (dr + 1) * 3 + dc + 1
                            row = par * 4 * C1 + (2 * rp + cp) * C1
                            a1_ref[row : row + C1, slot * C0 : (slot + 1) * C0] = w1_ref[
                                tap * C1 : (tap + 1) * C1, :
                            ]
                            pieces[slot] = w2_ref[tap * C2 : (tap + 1) * C2, :]
                a2_ref[row2 : row2 + C2, :] = jnp.concatenate(pieces, axis=1)
    eye = jnp.where(
        lax.broadcasted_iota(jnp.int32, (128, 128), 0)
        == lax.broadcasted_iota(jnp.int32, (128, 128), 1),
        1.0,
        0.0,
    ).astype(BF16)

    @pl.loop(0, 8)
    def _(k):
        at = pl.multiple_of(k * 512, 512)
        b1_ref[:, pl.ds(at, 512)] = matmul_nt(eye, w1_ref[pl.ds(at, 512), :]).astype(BF16)

    @pl.loop(0, 4)
    def _(k):
        at = pl.multiple_of(k * 512, 512)
        b2_ref[:, pl.ds(at, 512)] = matmul_nt(eye[0:C1, 0:C1], w2_ref[pl.ds(at, 512), :]).astype(
            BF16
        )


def first_kernel(lat_ref, below_ref, above_ref, a1_ref, sh_ref, pre_ref, out_ref, x_ref):
    planes = jnp.concatenate([below_ref[...], lat_ref[...], above_ref[...]], axis=0)
    for k in range(9):
        moved = matmul(planes, sh_ref[:, k * CELLS : (k + 1) * CELLS]).astype(BF16)
        for z in range(3):
            at = (z * 9 + k) * C0
            x_ref[at : at + C0, :] = moved[z * C0 : (z + 1) * C0]
    for m in range(2):
        both = matmul(a1_ref[...], x_ref[m * 9 * C0 : (m + 2) * 9 * C0, :])
        pre_ref[2 * m + 1] = both[0 : 4 * C1]
        pre_ref[2 * m] = both[4 * C1 : 8 * C1]
    lower, upper = pre_ref[1], pre_ref[2]
    sums = fold(jnp.sum(lower + upper, axis=1, keepdims=True), C1)
    mean = sums / (8 * CELLS)
    wide = jnp.concatenate([mean] * 4, axis=0)
    lower, upper = lower - wide, upper - wide
    squares = fold(jnp.sum(lower * lower + upper * upper, axis=1, keepdims=True), C1)
    emit_rows(out_ref, mean, squares)


def second_kernel(got_ref, pre1_ref, p1_ref, a2_ref, sh_ref, pre_ref, act_ref, st_ref, out_ref, x_ref):
    mean, scale = moments(got_ref[...], 8 * CELLS)
    st = jnp.concatenate([mean, scale, p1_ref[0:6]], axis=0)
    st_ref[...] = st
    cols = columns(st)
    mean, scale, gain, shift = (cols[0:C1, k : k + 1] for k in range(4))
    keeps = (cols[0:C1, 4:5], None, None, cols[0:C1, 5:6])
    for q in range(4):
        for block in range(4):
            rp, cp = block // 2, block % 2
            norm = gain * ((pre1_ref[q, block * C1 : (block + 1) * C1, :] - mean) * scale) + shift
            act = norm * sigmoid(norm)
            if keeps[q] is not None:
                act = act * keeps[q]
            act = act.astype(BF16)
            if q in (1, 2):
                act_ref[q - 1, :, block * CELLS : (block + 1) * CELLS] = act
            sj, sl = 1 - 2 * rp, 1 - 2 * cp
            moved = {(0, 0): act}
            for dj, dl in ((sj, 0), (0, sl), (sj, sl)):
                moved[dj, dl] = matmul(act, sh_ref[:, shift_slot(dj, dl)]).astype(BF16)
            for (trp, dr), (srp, dj) in FINE_STEPS.items():
                if srp != rp:
                    continue
                for (tcp, dc), (scp, dl) in FINE_STEPS.items():
                    if scp != cp:
                        continue
                    at = q * 9 * C1 + ((dr + 1) * 3 + dc + 1) * C1
                    lane = (2 * trp + tcp) * CELLS
                    x_ref[at : at + C1, lane : lane + CELLS] = moved[dj, dl]

    for m in range(3):

        @pl.loop(0, 4)
        def _(block):
            lane = pl.multiple_of(block * CELLS, CELLS)
            both = matmul(a2_ref[...], x_ref[m * 9 * C1 : (m + 2) * 9 * C1, pl.ds(lane, CELLS)])
            pre_ref[2 * m + 1, :, pl.ds(lane, CELLS)] = both[0 : 4 * C2]
            pre_ref[2 * m, :, pl.ds(lane, CELLS)] = both[4 * C2 : 8 * C2]

    total = pre_ref[1] + pre_ref[2] + pre_ref[3] + pre_ref[4]
    sums = fold(jnp.sum(total, axis=1, keepdims=True), C2)
    mean = sums / (64 * CELLS)
    wide = jnp.concatenate([mean] * 4, axis=0)
    squares = jnp.zeros((4 * C2, CELLS), F32)
    for t in range(1, 5):
        for block in range(4):
            away = pre_ref[t, :, block * CELLS : (block + 1) * CELLS] - wide
            squares = squares + away * away
    emit_rows(out_ref, mean, fold(jnp.sum(squares, axis=1, keepdims=True), C2))


def spread_kernel(cot_ref, out_ref):
    matrix = spread_matrix()
    count = cot_ref.shape[0] // C2
    for rp in range(2):
        for rp2 in range(2):
            for h in range(2):
                lanes = [(4 * (2 * h + jj) + 2 * rp + rp2) * 256 for jj in range(2)]
                rows = jnp.concatenate([cot_ref[:, at : at + 256] for at in lanes], axis=1)
                moved = matmul(rows, matrix).astype(BF16)
                for cp2 in range(2):
                    for cp in range(2):
                        row = (2 * rp2 + cp2) * C2
                        lane = (2 * rp + cp) * CELLS + h * 128
                        piece = moved[:, cp2 * 256 + cp * 128 : cp2 * 256 + cp * 128 + 128]
                        for t in range(count):
                            out_ref[t, row : row + C2, lane : lane + 128] = piece[
                                t * C2 : (t + 1) * C2
                            ]


def gather_kernel(feat_ref, out_ref):
    matrix = spread_matrix()
    count = feat_ref.shape[0]
    for rp in range(2):
        for rp2 in range(2):
            for h in range(2):
                pieces = []
                for cp2 in range(2):
                    for cp in range(2):
                        row = (2 * rp2 + cp2) * C2
                        lane = (2 * rp + cp) * CELLS + h * 128
                        pieces.append(
                            jnp.concatenate(
                                [
                                    feat_ref[t, row : row + C2, lane : lane + 128]
                                    for t in range(count)
                                ],
                                axis=0,
                            )
                        )
                moved = matmul_nt(jnp.concatenate(pieces, axis=1), matrix).astype(BF16)
                for jj in range(2):
                    at = (4 * (2 * h + jj) + 2 * rp + rp2) * 256
                    out_ref[:, at : at + 256] = moved[:, jj * 256 : (jj + 1) * 256]


def third_kernel(got_ref, pre_ref, cot_ref, p2_ref, grad_ref, feat_ref, st_ref, out_ref):
    mean, scale = moments(got_ref[...], 64 * CELLS)
    st = jnp.concatenate([mean, scale, p2_ref[0:6]], axis=0)
    st_ref[...] = st
    cols = columns(st)
    mean, scale, gain, shift = (cols[:, k : k + 1] for k in range(4))

    def slope(t, lane):
        hat = (pre_ref[t, :, pl.ds(lane, CELLS)] - mean) * scale
        norm = gain * hat + shift
        gate = sigmoid(norm)
        cot = cot_ref[t, :, pl.ds(lane, CELLS)].astype(F32)
        grad = cot * (gate * (1.0 + norm * (1.0 - gate)))
        grad_ref[t, :, pl.ds(lane, CELLS)] = grad
        return hat, norm, gate, grad

    for t in (0, 5):

        @pl.loop(0, 4)
        def _(block):
            slope(t, pl.multiple_of(block * CELLS, CELLS))

    def body(k, carry):
        t = k // 4 + 1
        lane = pl.multiple_of((k % 4) * CELLS, CELLS)
        hat, norm, gate, grad = slope(t, lane)
        feat_ref[t - 1, :, pl.ds(lane, CELLS)] = (norm * gate).astype(BF16)
        return carry[0] + grad * hat, carry[1] + grad

    zero = jnp.zeros((4 * C2, CELLS), F32)
    first, second = lax.fori_loop(0, 16, body, (zero, zero))
    emit_rows(
        out_ref,
        fold(jnp.sum(first, axis=1, keepdims=True), C2),
        fold(jnp.sum(second, axis=1, keepdims=True), C2),
    )


def fourth_kernel(
    got_ref, pre_ref, grad_ref, st2_ref, b2_ref, sh_ref, act_ref, pre1_ref, st1_ref,
    g1_ref, dw_ref, sum_ref, out_ref, x_ref,
):
    sums = jnp.sum(got_ref[...], axis=0)
    sum_ref[...] = sums
    total = got_ref.shape[0] * 64 * CELLS
    cols = columns(jnp.concatenate([st2_ref[0:6], sums[0:2] / total], axis=0))
    mean, scale, gain = (cols[:, k : k + 1] for k in range(3))
    hat_part, part = cols[:, 6:7], cols[:, 7:8]
    keeps = {0: cols[:, 4:5], 5: cols[:, 5:6]}
    for t in range(6):
        factor = gain * scale
        if t in keeps:
            factor = factor * keeps[t]
        for block in range(4):
            rp, cp = block // 2, block % 2
            lanes = slice(block * CELLS, (block + 1) * CELLS)
            hat = (pre_ref[t, :, lanes] - mean) * scale
            dpre = (factor * (grad_ref[t, :, lanes] - part - hat * hat_part)).astype(BF16)
            sj, sl = 1 - 2 * rp, 1 - 2 * cp
            moved = {(0, 0): dpre}
            for dj, dl in ((sj, 0), (0, sl), (sj, sl)):
                moved[dj, dl] = matmul(dpre, sh_ref[:, shift_slot(dj, dl)]).astype(BF16)
            for q, (rp2, dr) in enumerate(TAP_PHASES):
                for r, (cp2, dc) in enumerate(TAP_PHASES):
                    row = (2 * rp2 + cp2) * C2
                    for trp in range(2):
                        for tcp in range(2):
                            srp, dj = FINE_STEPS[trp, dr]
                            scp, dl = FINE_STEPS[tcp, dc]
                            if (srp, scp) != (rp, cp):
                                continue
                            at = t * 16 * C2 + (4 * q + r) * C2
                            lane = (2 * trp + tcp) * CELLS
                            x_ref[at : at + C2, lane : lane + CELLS] = moved[dj, dl][row : row + C2]

    cols = columns(st1_ref[...])
    mean, scale, gain, shift = (cols[0:C1, k : k + 1] for k in range(4))
    first = jnp.zeros((C1, CELLS), F32)
    second = jnp.zeros((C1, CELLS), F32)
    for j in range(2):
        for block in range(4):
            lanes = slice(block * CELLS, (block + 1) * CELLS)
            act_grad = matmul(b2_ref[...], x_ref[j * 32 * C2 : (j + 2) * 32 * C2, lanes])
            hat = (pre1_ref[j + 1, block * C1 : (block + 1) * C1, :] - mean) * scale
            norm = gain * hat + shift
            gate = sigmoid(norm)
            grad = act_grad * (gate * (1.0 + norm * (1.0 - gate)))
            g1_ref[j, block * C1 : (block + 1) * C1, :] = grad
            first = first + grad * hat
            second = second + grad
    emit_rows(
        out_ref,
        jnp.sum(first, axis=1, keepdims=True),
        jnp.sum(second, axis=1, keepdims=True),
    )
    for p in range(4):
        part = matmul_nt(x_ref[p * 16 * C2 : (p + 1) * 16 * C2, :], act_ref[0])
        part = part + matmul_nt(x_ref[(p + 2) * 16 * C2 : (p + 3) * 16 * C2, :], act_ref[1])
        dw_ref[p * 16 * C2 : (p + 1) * 16 * C2, :] = part


def first_dpre(grad, pre, cols, keep):
    mean, scale, gain = (cols[0:C1, k : k + 1] for k in range(3))
    hat_part, part = cols[0:C1, 6:7], cols[0:C1, 7:8]
    factor = gain * scale
    if keep is not None:
        factor = factor * keep
    return (factor * (grad - part - (pre - mean) * scale * hat_part)).astype(BF16)


def first_windows(x_ref, base, grad_ref, pre_ref, cols, keep, sh_ref):
    for block in range(4):
        rp, cp = block // 2, block % 2
        rows = slice(block * C1, (block + 1) * C1)
        dpre = first_dpre(grad_ref[rows, :].astype(F32), pre_ref[rows, :], cols, keep)
        for q, (trp, dj) in enumerate(TAP_PHASES):
            for r, (tcp, dl) in enumerate(TAP_PHASES):
                if (trp, tcp) != (rp, cp):
                    continue
                moved = dpre
                if (dj, dl) != (0, 0):
                    moved = matmul(dpre, sh_ref[:, shift_slot(dj, dl)]).astype(BF16)
                at = base + (4 * q + r) * C1
                x_ref[at : at + C1, :] = moved


def fifth_kernel(
    got_ref, g1_ref, pre1_ref, st1_ref, sh_ref, lat_ref, below_ref, above_ref, dw_ref, sum_ref, x_ref
):
    sums = jnp.sum(got_ref[...], axis=0)
    sum_ref[...] = sums
    total = got_ref.shape[0] * 8 * CELLS
    cols = columns(jnp.concatenate([st1_ref[0:6], sums[0:2] / total], axis=0))
    for j in range(2):
        first_windows(
            x_ref, j * 16 * C1, g1_ref.at[j], pre1_ref.at[j + 1], cols, None, sh_ref
        )
    for p, j, field in ((0, 1, above_ref), (1, 0, lat_ref), (2, 1, lat_ref), (3, 0, below_ref)):
        for half in range(2):
            at = p * 16 * C1 + half * 8 * C1
            src = j * 16 * C1 + half * 8 * C1
            dw_ref[at : at + 8 * C1, :] = matmul_nt(x_ref[src : src + 8 * C1, :], field[...])


def sixth_kernel(
    sum_ref, low_ref, high_ref, pre1_ref, st1_ref, sh_ref, b1_ref, own_ref, count_ref, out_ref, x_ref
):
    total = count_ref.shape[0] * 8 * CELLS
    cols = columns(jnp.concatenate([st1_ref[0:6], sum_ref[0:2] / total], axis=0))
    keeps = (cols[0:C1, 4:5], cols[0:C1, 5:6])
    first_windows(x_ref, 0, low_ref, pre1_ref.at[0], cols, keeps[0], sh_ref)
    first_windows(x_ref, 16 * C1, high_ref, pre1_ref.at[3], cols, keeps[1], sh_ref)
    grad = matmul(b1_ref[:, 0 : 16 * C1], x_ref[0 : 16 * C1, :])
    grad = grad + matmul(b1_ref[:, 16 * C1 : 48 * C1], own_ref[...])
    out_ref[...] = grad + matmul(b1_ref[:, 48 * C1 : 64 * C1], x_ref[16 * C1 : 32 * C1, :])


def local(
    latent,
    first_weight,
    first_norm_gain,
    first_norm_shift,
    second_weight,
    second_norm_gain,
    second_norm_shift,
    cotangent,
):
    count = group_size()
    place = lax.axis_index("space")
    below_is = jnp.full((128,), place > 0, F32)
    above_is = jnp.full((128,), place < lax.axis_size("space") - 1, F32)
    blank = jnp.zeros((128,), F32)
    p1 = jnp.stack(
        [jnp.tile(first_norm_gain, 2), jnp.tile(first_norm_shift, 2), below_is, above_is]
        + [blank] * 4
    )
    p2 = jnp.stack(
        [jnp.tile(second_norm_gain, 4), jnp.tile(second_norm_shift, 4), below_is, above_is]
        + [blank] * 4
    )
    lat = latent.reshape(C0, CELLS)
    lat_below = to_above(lat)
    lat_above = to_below(lat)
    cot = cotangent.reshape(C2, 4, 16 * CELLS).transpose(1, 0, 2)
    cot_below = to_above(cot[3])
    cot_above = to_below(cot[0])
    w1 = first_weight.reshape(64 * C1, C0)
    w2 = second_weight.reshape(64 * C2, C1)
    a1, a2, b1, b2, sh = call(
        prepare_kernel,
        [
            ((8 * C1, 18 * C0), BF16),
            ((8 * C2, 18 * C1), BF16),
            ((C0, 64 * C1), BF16),
            ((C1, 64 * C2), BF16),
            ((CELLS, 9 * CELLS), BF16),
        ],
        [w1, w2],
    )
    stats = ((count, 8, 128), F32)
    pre1, out = call(
        first_kernel,
        [((4, 4 * C1, CELLS), F32), stats],
        [lat, lat_below, lat_above, a1, sh],
        [pltpu.VMEM((27 * C0, CELLS), BF16)],
    )
    (spread,) = call(
        spread_kernel,
        [((6, 4 * C2, 4 * CELLS), BF16)],
        [jnp.concatenate([cot_below[None], cot, cot_above[None]]).reshape(6 * C2, 16 * CELLS)],
    )
    got = exchange(out)
    pre2, act, st1, out = call(
        second_kernel,
        [((6, 4 * C2, 4 * CELLS), F32), ((2, C1, 4 * CELLS), BF16), ((8, 128), F32), stats],
        [got, pre1, p1, a2, sh],
        [pltpu.VMEM((36 * C1, 4 * CELLS), BF16)],
    )
    got = exchange(out)
    grad2, feat, st2, out = call(
        third_kernel,
        [
            ((6, 4 * C2, 4 * CELLS), F32),
            ((4, 4 * C2, 4 * CELLS), BF16),
            ((8, 128), F32),
            stats,
        ],
        [got, pre2, spread, p2],
    )
    got = exchange(out)
    grad1, dw2, sum2, out = call(
        fourth_kernel,
        [((2, 4 * C1, CELLS), F32), ((64 * C2, C1), F32), ((8, 128), F32), stats],
        [got, pre2, grad2, st2, b2, sh, act, pre1, st1],
        [pltpu.VMEM((96 * C2, 4 * CELLS), BF16)],
    )
    grad_below = to_above(grad1[1])
    grad_above = to_below(grad1[0])
    got = exchange(out)
    dw1, sum1, windows = call(
        fifth_kernel,
        [((64 * C1, C0), F32), ((8, 128), F32), ((32 * C1, CELLS), BF16)],
        [got, grad1, pre1, st1, sh, lat, lat_below, lat_above],
    )
    (latent_grad,) = call(
        sixth_kernel,
        [((C0, CELLS), F32)],
        [sum1, grad_below, grad_above, pre1, st1, sh, b1, windows, got],
        [pltpu.VMEM((32 * C1, CELLS), BF16)],
    )
    (features,) = call(gather_kernel, [((4 * C2, 16 * CELLS), BF16)], [feat])
    features = features.reshape(4, C2, 16 * CELLS).transpose(1, 0, 2)
    second_weight_grad = halving_sum(dw2.reshape(-1, 128)).reshape(64, C2, C1)
    first_weight_grad = halving_sum(dw1).reshape(64, C1, C0)
    return (
        features[None],
        latent_grad.reshape(1, C0, 1, CELLS),
        first_weight_grad,
        second_weight_grad,
        sum1[0:2, 0:C1],
        sum2[0:2, 0:C2],
    )


def solution(mesh):
    volume = P(("group", "rep"), None, "space", None)
    in_specs = (volume, P(), P(), P(), P(), P(), P(), volume)
    out_specs = (
        volume,
        volume,
        P("group", None, None),
        P("group", None, None),
        P("group", None),
        P("group", None),
    )
    return jax.shard_map(local, mesh=mesh, in_specs=in_specs, out_specs=out_specs, check_vma=False)
```

profile of v0, /device:TPU:0, one launch (start us, length us, event | category | flops | bytes accessed | tf_op | source)
XLA Modules:
  0.0 178.5 jit_solution(5748797672642800926)
XLA Ops:
  0.7 5.0 %collective-permute-start = (bf16[128,256]{1,0:T(8,128)(2,1)}, bf16[128,256]{1,0:T(8,128)(2,1)S(1)}, u32[]{:S(2)}, u32[]{:S(2)}) collective-permute-start(bf16[128,256]{1,0:T(8,128)(2,1)} %bitcast.31), channel_id=1, source_target_pairs={{0,2},{2,4},{4,6},{6,8},{8,10},{10,12},{12,14},{1,3},{3,5},{5,7},{... | collective-permute-start | bytes 196616 | tf_op jit(solution)/shard_map/ppermute | solution.py:77
  5.7 1.3 collective-permute-start.1
  7.0 1.8 %copy.25 = bf16[1,32,4,4096]{3,1,2,0:T(8,128)(2,1)S(1)} copy(bf16[1,32,4,4096]{3,2,1,0:T(4,128)(2,1)} %param.15) | data formatting | bytes 2097152 | tf_op args[7]
  9.7 5.4 %collective-permute-start.2 = (bf16[32,4096]{1,0:T(8,128)(2,1)}, bf16[32,4096]{1,0:T(8,128)(2,1)}, u32[]{:S(2)}, u32[]{:S(2)}) collective-permute-start(bf16[32,4096]{1,0:T(8,128)(2,1)} %get-tuple-element.62), channel_id=1, source_target_pairs={{0,2},{2,4},{4,6},{6,8},{8,10},{10,12},{12,14},{1,3},{3,5},{5,7},{... | collective-permute-start | bytes 786440 | tf_op jit(solution)/shard_map/ppermute | solution.py:77
  15.1 1.3 collective-permute-start.3
  16.4 4.0 %shard_map.127 = (bf16[512,2304]{1,0:T(8,128)(2,1)}, bf16[256,1152]{1,0:T(8,128)(2,1)S(1)}, bf16[128,4096]{1,0:T(8,128)(2,1)S(1)}, bf16[64,2048]{1,0:T(8,128)(2,1)S(1)}, bf16[256,2304]{1,0:T(8,128)(2,1)S(1)}) custom-call(bf16[4096,128]{1,0:T(8,128)(2,1)S(1)} %bitcast.35, bf16[2048,64]{1,0:T(8,128)(2,1)S(1)} %bitcast.36), custom_call_target="tpu_custom_call" | custom-call | flops 1000000000 | bytes 4000000 | tf_op jit(solution)/shard_map/pallas_call | solution.py:86
  22.0 1.7 copy-done.1
  23.6 2.2 %shard_map.128 = (f32[4,256,256]{2,1,0:T(8,128)S(1)}, f32[16,8,128]{2,1,0:T(8,128)S(1)}) custom-call(bf16[128,256]{1,0:T(8,128)(2,1)S(1)} %bitcast.33, bf16[128,256]{1,0:T(8,128)(2,1)S(1)} %collective-permute-done.below_ref, bf16[128,256]{1,0:T(8,128)(2,1)S(1)} %collective-permute-done.1.above_ref, bf16[512,2304]{1,0:T(8,128)(2,1)S(1)} %copy-done.1, ...), custom_call_target="tpu_custom_call" | custom-call | flops 1000000000 | bytes 4000000 | tf_op jit(solution)/shard_map/pallas_call | solution.py:86
  26.5 7.2 %all-to-all-start = ((f32[16,8,128]{2,1,0:T(8,128)}), f32[16,8,128]{2,1,0:T(8,128)S(1)}, u32[]{:S(2)}, u32[]{:S(2)}) async-start(f32[16,8,128]{2,1,0:T(8,128)} %copy-done.16), calls=%async_computation | async-start | bytes 131072 | tf_op jit(solution)/shard_map/all_to_all | solution.py:72
  34.3 1.3 stack_tile.12
  38.8 1.8 all-to-all-done.got_ref
  41.7 7.3 %shard_map.129 = (f32[6,128,1024]{2,1,0:T(8,128)}, bf16[2,64,1024]{2,1,0:T(8,128)(2,1)S(1)}, f32[8,128]{1,0:T(8,128)S(1)}, f32[16,8,128]{2,1,0:T(8,128)S(1)}) custom-call(f32[16,8,128]{2,1,0:T(8,128)S(1)} %all-to-all-done.got_ref, f32[4,256,256]{2,1,0:T(8,128)S(1)} %get-tuple-element.31.pre1_ref, f32[8,128]{1,0:T(8,128)S(1)} %stack.6.p1_ref, ...), custom_call_target="tpu_custom_call" | custom-call | flops 1000000000 | bytes 4000000 | tf_op jit(solution)/shard_map/pallas_call | solution.py:86
  50.3 4.2 %all-to-all-start.1 = ((f32[16,8,128]{2,1,0:T(8,128)}), f32[16,8,128]{2,1,0:T(8,128)S(1)}, u32[]{:S(2)}, u32[]{:S(2)}) async-start(f32[16,8,128]{2,1,0:T(8,128)} %copy-done.17), calls=%async_computation.1 | async-start | bytes 131072 | tf_op jit(solution)/shard_map/all_to_all | solution.py:72
  54.5 1.5 pad_maximum_fusion
  58.2 3.2 %all-to-all-done.1.got_ref = f32[16,8,128]{2,1,0:T(8,128)S(1)} async-done(((f32[16,8,128]{2,1,0:T(8,128)}), f32[16,8,128]{2,1,0:T(8,128)S(1)}, u32[]{:S(2)}, u32[]{:S(2)}) %all-to-all-start.1) | async-done | bytes 65568 | tf_op jit(solution)/shard_map/all_to_all | solution.py:72
  61.4 1.4 copy-done.3
  62.8 7.2 %shard_map.131 = (f32[6,128,1024]{2,1,0:T(8,128)S(1)}, bf16[4,128,1024]{2,1,0:T(8,128)(2,1)S(1)}, f32[8,128]{1,0:T(8,128)S(1)}, f32[16,8,128]{2,1,0:T(8,128)S(1)}) custom-call(f32[16,8,128]{2,1,0:T(8,128)S(1)} %all-to-all-done.1.got_ref, f32[6,128,1024]{2,1,0:T(8,128)} %get-tuple-element.34.pre_ref, bf16[6,128,1024]{2,1,0:T(8,128)(2,1)S(1)} %copy-done.3, ...), custom_call_target="tpu_custom_call" | custom-call | flops 1000000000 | bytes 4000000 | tf_op jit(solution)/shard_map/pallas_call | solution.py:86
  70.1 1.7 copy-done
  71.8 9.5 %all_to_all.20.got_ref = f32[16,8,128]{2,1,0:T(8,128)S(1)} all-to-all(f32[16,8,128]{2,1,0:T(8,128)S(1)} %get-tuple-element.36), channel_id=1, replica_groups=mesh['group'=2,'space'=8,'rep'=2] {'space','rep'}, dimensions={0} | all-to-all | bytes 131072 | tf_op jit(solution)/shard_map/all_to_all | solution.py:72
  81.3 8.3 %shard_map.133 = (f32[2,256,256]{2,1,0:T(8,128)S(1)}, f32[2048,64]{1,0:T(8,128)S(1)}, f32[8,128]{1,0:T(8,128)S(1)}, f32[16,8,128]{2,1,0:T(8,128)S(1)}) custom-call(f32[16,8,128]{2,1,0:T(8,128)S(1)} %all_to_all.20.got_ref, f32[6,128,1024]{2,1,0:T(8,128)} %get-tuple-element.34.pre_ref, f32[6,128,1024]{2,1,0:T(8,128)} %copy-done, ...), custom_call_target="tpu_custom_call" | custom-call | flops 1000000000 | bytes 4000000 | tf_op jit(solution)/shard_map/pallas_call | solution.py:86
  92.0 3.5 %all-to-all-start.3 = ((f32[16,8,128]{2,1,0:T(8,128)}), f32[16,8,128]{2,1,0:T(8,128)S(1)}, u32[]{:S(2)}, u32[]{:S(2)}) async-start(f32[16,8,128]{2,1,0:T(8,128)} %copy-done.15), calls=%async_computation.3 | async-start | bytes 131072 | tf_op jit(solution)/shard_map/all_to_all | solution.py:72
  95.5 6.8 %all-to-all-done.3.got_ref.count_ref = f32[16,8,128]{2,1,0:T(8,128)S(1)} async-done(((f32[16,8,128]{2,1,0:T(8,128)}), f32[16,8,128]{2,1,0:T(8,128)S(1)}, u32[]{:S(2)}, u32[]{:S(2)}) %all-to-all-start.3) | async-done | bytes 65568 | tf_op jit(solution)/shard_map/all_to_all | solution.py:72
  103.4 1.5 shard_map.134
  104.9 1.3 copy-done.4
  107.1 2.2 %reshape.61 = f32[1024,128]{1,0:T(8,128)} reshape(f32[2048,64]{1,0:T(8,128)} %copy-done.7) | data formatting | bytes 1048576 | tf_op jit(solution)/shard_map/reshape | solution.py:570
  110.9 1.5 convert_add_fusion
  112.7 2.0 %collective-permute-start.15 = (bf16[256,128]{1,0:T(8,128)(2,1)S(1)}, bf16[256,128]{1,0:T(8,128)(2,1)S(1)}, u32[]{:S(2)}, u32[]{:S(2)}) collective-permute-start(bf16[256,128]{1,0:T(8,128)(2,1)S(1)} %dynamic-slice_convert_fusion.4), channel_id=1, source_target_pairs={{0,2},{2,0},{4,6},{6,4},{8,10},{10,8},{12,14},{14,12},{1,3},{3,1},... | collective-permute-start | bytes 196616 | tf_op jit(solution)/shard_map/ppermute | solution.py:47
  114.7 6.8 %collective-permute-done.7 = bf16[1024,128]{1,0:T(8,128)(2,1)S(1)} collective-permute-done((bf16[1024,128]{1,0:T(8,128)(2,1)S(1)}, bf16[1024,128]{1,0:T(8,128)(2,1)S(1)}, u32[]{:S(2)}, u32[]{:S(2)}) %collective-permute-start.7) | collective-permute-done | bytes 262176 | tf_op jit(solution)/shard_map/ppermute | solution.py:47
  122.2 1.5 collective-permute-start.16
  123.7 2.8 %collective-permute-done.8 = bf16[512,128]{1,0:T(8,128)(2,1)S(1)} collective-permute-done((bf16[512,128]{1,0:T(8,128)(2,1)S(1)}, bf16[512,128]{1,0:T(8,128)(2,1)S(1)}, u32[]{:S(2)}, u32[]{:S(2)}) %collective-permute-start.8) | collective-permute-done | bytes 131104 | tf_op jit(solution)/shard_map/ppermute | solution.py:47
  127.0 6.7 %collective-permute-done.9 = bf16[256,128]{1,0:T(8,128)(2,1)S(1)} collective-permute-done((bf16[256,128]{1,0:T(8,128)(2,1)S(1)}, bf16[256,128]{1,0:T(8,128)(2,1)S(1)}, u32[]{:S(2)}, u32[]{:S(2)}) %collective-permute-start.9) | collective-permute-done | bytes 65568 | tf_op jit(solution)/shard_map/ppermute | solution.py:47
  133.8 2.9 %collective-permute-start.17 = (bf16[64,128]{1,0:T(8,128)(2,1)S(1)}, bf16[64,128]{1,0:T(8,128)(2,1)S(1)}, u32[]{:S(2)}, u32[]{:S(2)}) collective-permute-start(bf16[64,128]{1,0:T(8,128)(2,1)S(1)} %dynamic-slice_convert_fusion.7), channel_id=1, source_target_pairs={{0,8},{2,10},{4,12},{6,14},{8,0},{10,2},{12,4},{14,6},{1,9},{3,11}... | collective-permute-start | bytes 49160 | tf_op jit(solution)/shard_map/ppermute | solution.py:47
  136.7 2.6 %collective-permute-done.10 = bf16[256,128]{1,0:T(8,128)(2,1)S(1)} collective-permute-done((bf16[256,128]{1,0:T(8,128)(2,1)S(1)}, bf16[256,128]{1,0:T(8,128)(2,1)S(1)}, u32[]{:S(2)}, u32[]{:S(2)}) %collective-permute-start.10) | collective-permute-done | bytes 65568 | tf_op jit(solution)/shard_map/ppermute | solution.py:47
  139.5 1.9 %collective-permute-start.18 = (bf16[64,128]{1,0:T(8,128)(2,1)S(1)}, bf16[64,128]{1,0:T(8,128)(2,1)S(1)}, u32[]{:S(2)}, u32[]{:S(2)}) collective-permute-start(bf16[64,128]{1,0:T(8,128)(2,1)S(1)} %add_convert_fusion.1), channel_id=1, source_target_pairs={{0,8},{2,10},{4,12},{6,14},{8,0},{10,2},{12,4},{14,6},{1,9},{3,11}... | collective-permute-start | bytes 49160 | tf_op jit(solution)/shard_map/ppermute | solution.py:47
  141.5 3.1 %collective-permute-done.11 = bf16[512,128]{1,0:T(8,128)(2,1)S(1)} collective-permute-done((bf16[512,128]{1,0:T(8,128)(2,1)S(1)}, bf16[512,128]{1,0:T(8,128)(2,1)S(1)}, u32[]{:S(2)}, u32[]{:S(2)}) %collective-permute-start.11) | collective-permute-done | bytes 131104 | tf_op jit(solution)/shard_map/ppermute | solution.py:47
  146.3 3.7 %collective-permute-done.19 = bf16[128,128]{1,0:T(8,128)(2,1)S(1)} collective-permute-done((bf16[128,128]{1,0:T(8,128)(2,1)S(1)}, bf16[128,128]{1,0:T(8,128)(2,1)S(1)}, u32[]{:S(2)}, u32[]{:S(2)}) %collective-permute-start.19) | collective-permute-done | bytes 32800 | tf_op jit(solution)/shard_map/ppermute | solution.py:47
  150.0 1.5 collective-permute-start.20
  152.0 2.1 %maximum_select_fusion.1 = bf16[2048,128]{1,0:T(8,128)(2,1)} fusion(bf16[1024,128]{1,0:T(8,128)(2,1)} %collective-permute-done.12, bf16[1024,128]{1,0:T(8,128)(2,1)} %maximum_select_fusion.2, pred[]{:T(512)S(6)} %eq.34), kind=kLoop, calls=%fused_computation.6 | loop fusion | flops 2359296 | bytes 1048577 | tf_op jit(solution)/shard_map/jit(_where)/select_n | solution.py:63
  154.2 1.9 %slice_bitcast_fusion.2 = (f32[256,256]{1,0:T(8,128)}, f32[256,256]{1,0:T(8,128)}) fusion(f32[2,256,256]{2,1,0:T(8,128)} %copy-done.8), kind=kLoop, calls=%fused_computation.18 | loop fusion | bytes 1048576 | tf_op jit(solution)/shard_map/squeeze | solution.py:555
  156.0 3.2 %collective-permute-start.4 = (f32[256,256]{1,0:T(8,128)}, f32[256,256]{1,0:T(8,128)}, u32[]{:S(2)}, u32[]{:S(2)}) collective-permute-start(f32[256,256]{1,0:T(8,128)} %get-tuple-element.65), channel_id=1, source_target_pairs={{0,2},{2,4},{4,6},{6,8},{8,10},{10,12},{12,14},{1,3},{3,5},{5,7},{... | collective-permute-start | bytes 786440 | tf_op jit(solution)/shard_map/ppermute | solution.py:77
  159.2 1.3 collective-permute-start.5
  160.9 1.2 copy-done.20
  162.1 1.5 shard_map.132
  163.6 1.8 copy.24
  166.5 4.2 %collective-permute-done.4.low_ref = f32[256,256]{1,0:T(8,128)} collective-permute-done((f32[256,256]{1,0:T(8,128)}, f32[256,256]{1,0:T(8,128)}, u32[]{:S(2)}, u32[]{:S(2)}) %collective-permute-start.4) | collective-permute-done | bytes 262176 | tf_op jit(solution)/shard_map/ppermute | solution.py:77
  170.7 2.4 %shard_map.135 = f32[128,256]{1,0:T(8,128)S(1)} custom-call(f32[8,128]{1,0:T(8,128)S(1)} %get-tuple-element.44.sum_ref, f32[256,256]{1,0:T(8,128)} %collective-permute-done.4.low_ref, f32[256,256]{1,0:T(8,128)} %collective-permute-done.5.high_ref, f32[4,256,256]{2,1,0:T(8,128)S(1)} %get-tuple-element.31.pre1_ref, f32[8,128]{1,0:T(8,128)S(1)} %get-tuple-element.41.st1_ref, ...), custom_call_target="tpu_custom_call" | custom-call | flops 1000000000 | bytes 4000000 | tf_op jit(solution)/shard_map/pallas_call | solution.py:86
  175.1 1.8 %maximum_select_fusion = bf16[4096,128]{1,0:T(8,128)(2,1)S(1)} fusion(bf16[2048,128]{1,0:T(8,128)(2,1)} %collective-permute-done.13, bf16[2048,128]{1,0:T(8,128)(2,1)} %maximum_select_fusion.1, pred[]{:T(512)S(6)} %eq.33), kind=kLoop, calls=%fused_computation.1 | loop fusion | flops 4718592 | bytes 2097153 | tf_op jit(solution)/shard_map/jit(_where)/select_n | solution.py:63
  176.9 1.6 convert.2
  (122 shorter events, 24.9 us)
Async XLA Ops:
  0.6 15.7 %copy-start.18 = (bf16[64,64,128]{2,1,0:T(8,128)(2,1)S(1)}, bf16[64,64,128]{2,1,0:T(8,128)(2,1)}, u32[]{:S(2)}) copy-start(bf16[64,64,128]{2,1,0:T(8,128)(2,1)} %param.9) | copy-start | bytes 3145732
  0.6 15.7 %copy-start.21 = (bf16[64,32,64]{2,1,0:T(8,128)(2,1)S(1)}, bf16[64,32,64]{2,1,0:T(8,128)(2,1)}, u32[]{:S(2)}) copy-start(bf16[64,32,64]{2,1,0:T(8,128)(2,1)} %param.12) | copy-start | bytes 786436
  0.7 21.3 %collective-permute-start = (bf16[128,256]{1,0:T(8,128)(2,1)}, bf16[128,256]{1,0:T(8,128)(2,1)S(1)}, u32[]{:S(2)}, u32[]{:S(2)}) collective-permute-start(bf16[128,256]{1,0:T(8,128)(2,1)} %bitcast.31), channel_id=1, source_target_pairs={{0,2},{2,4},{4,6},{6,8},{8,10},{10,12},{12,14},{1,3},{3,5},{5,7},{... | collective-permute-start | bytes 196616 | tf_op jit(solution)/shard_map/ppermute | solution.py:77
  5.7 16.3 %collective-permute-start.1 = (bf16[128,256]{1,0:T(8,128)(2,1)}, bf16[128,256]{1,0:T(8,128)(2,1)S(1)}, u32[]{:S(2)}, u32[]{:S(2)}) collective-permute-start(bf16[128,256]{1,0:T(8,128)(2,1)} %bitcast.32), channel_id=1, source_target_pairs={{2,0},{4,2},{6,4},{8,6},{10,8},{12,10},{14,12},{3,1},{5,3},{7,5},{... | collective-permute-start | bytes 196616 | tf_op jit(solution)/shard_map/ppermute | solution.py:82
  8.8 7.6 %copy-start.24 = (bf16[1,32,4,4096]{3,1,2,0:T(8,128)(2,1)}, bf16[1,32,4,4096]{3,1,2,0:T(8,128)(2,1)S(1)}, u32[]{:S(2)}) copy-start(bf16[1,32,4,4096]{3,1,2,0:T(8,128)(2,1)S(1)} %copy.25) | copy-start | bytes 3145732
  9.7 12.3 %copy-start.14 = (bf16[1,128,1,256]{3,1,2,0:T(8,128)(2,1)S(1)}, bf16[1,128,1,256]{3,1,2,0:T(8,128)(2,1)}, u32[]{:S(2)}) copy-start(bf16[1,128,1,256]{3,1,2,0:T(8,128)(2,1)} %param.8) | copy-start | bytes 196612
  9.7 44.8 %collective-permute-start.2 = (bf16[32,4096]{1,0:T(8,128)(2,1)}, bf16[32,4096]{1,0:T(8,128)(2,1)}, u32[]{:S(2)}, u32[]{:S(2)}) collective-permute-start(bf16[32,4096]{1,0:T(8,128)(2,1)} %get-tuple-element.62), channel_id=1, source_target_pairs={{0,2},{2,4},{4,6},{6,8},{8,10},{10,12},{12,14},{1,3},{3,5},{5,7},{... | collective-permute-start | bytes 786440 | tf_op jit(solution)/shard_map/ppermute | solution.py:77
  15.1 39.5 %collective-permute-start.3 = (bf16[32,4096]{1,0:T(8,128)(2,1)}, bf16[32,4096]{1,0:T(8,128)(2,1)}, u32[]{:S(2)}, u32[]{:S(2)}) collective-permute-start(bf16[32,4096]{1,0:T(8,128)(2,1)} %get-tuple-element.63), channel_id=1, source_target_pairs={{2,0},{4,2},{6,4},{8,6},{10,8},{12,10},{14,12},{3,1},{5,3},{7,5},{... | collective-permute-start | bytes 786440 | tf_op jit(solution)/shard_map/ppermute | solution.py:82
  21.9 11.8 %copy-start.29 = (f32[64]{0:T(128)S(1)}, f32[64]{0:T(128)}, u32[]{:S(2)}) copy-start(f32[64]{0:T(128)} %param.10) | copy-start | bytes 772
  21.9 13.6 %copy-start.30 = (f32[64]{0:T(128)S(1)}, f32[64]{0:T(128)}, u32[]{:S(2)}) copy-start(f32[64]{0:T(128)} %param.11) | copy-start | bytes 772
  21.9 14.2 %copy-start.27 = (f32[32]{0:T(128)S(1)}, f32[32]{0:T(128)}, u32[]{:S(2)}) copy-start(f32[32]{0:T(128)} %param.13) | copy-start | bytes 388
  21.9 14.3 %copy-start.28 = (f32[32]{0:T(128)S(1)}, f32[32]{0:T(128)}, u32[]{:S(2)}) copy-start(f32[32]{0:T(128)} %param.14) | copy-start | bytes 388
  22.0 1.7 copy-start.1
  26.5 14.1 %all-to-all-start = ((f32[16,8,128]{2,1,0:T(8,128)}), f32[16,8,128]{2,1,0:T(8,128)S(1)}, u32[]{:S(2)}, u32[]{:S(2)}) async-start(f32[16,8,128]{2,1,0:T(8,128)} %copy-done.16), calls=%async_computation | async-start | bytes 131072 | tf_op jit(solution)/shard_map/all_to_all | solution.py:72
  40.6 1.1 copy-start.23
  50.3 11.1 %all-to-all-start.1 = ((f32[16,8,128]{2,1,0:T(8,128)}), f32[16,8,128]{2,1,0:T(8,128)S(1)}, u32[]{:S(2)}, u32[]{:S(2)}) async-start(f32[16,8,128]{2,1,0:T(8,128)} %copy-done.17), calls=%async_computation.1 | async-start | bytes 131072 | tf_op jit(solution)/shard_map/all_to_all | solution.py:72
  57.1 1.1 copy-start.2
  61.4 1.4 copy-start.3
  62.8 18.5 %copy-start.11 = (bf16[64,2048]{1,0:T(8,128)(2,1)S(1)}, bf16[64,2048]{1,0:T(8,128)(2,1)}, u32[]{:S(2)}) copy-start(bf16[64,2048]{1,0:T(8,128)(2,1)} %copy-done.10) | copy-start | bytes 786436
  62.8 18.5 %copy-start.13 = (bf16[2,64,1024]{2,1,0:T(8,128)(2,1)S(1)}, bf16[2,64,1024]{2,1,0:T(8,128)(2,1)}, u32[]{:S(2)}) copy-start(bf16[2,64,1024]{2,1,0:T(8,128)(2,1)} %copy-done.12) | copy-start | bytes 786436
  70.1 1.7 copy-start
  71.8 17.8 %copy-start.19 = (bf16[4,128,1024]{2,1,0:T(8,128)(2,1)}, bf16[4,128,1024]{2,1,0:T(8,128)(2,1)S(1)}, u32[]{:S(2)}) copy-start(bf16[4,128,1024]{2,1,0:T(8,128)(2,1)S(1)} %get-tuple-element.35.feat_ref) | copy-start | bytes 3145732
  89.6 1.0 copy-start.7
  92.0 10.4 %all-to-all-start.3 = ((f32[16,8,128]{2,1,0:T(8,128)}), f32[16,8,128]{2,1,0:T(8,128)S(1)}, u32[]{:S(2)}, u32[]{:S(2)}) async-start(f32[16,8,128]{2,1,0:T(8,128)} %copy-done.15), calls=%async_computation.3 | async-start | bytes 131072 | tf_op jit(solution)/shard_map/all_to_all | solution.py:72
  102.3 1.0 copy-start.9
  104.9 1.3 copy-start.4
  104.9 2.2 %copy-start.5 = (bf16[2048,256]{1,0:T(8,128)(2,1)}, bf16[2048,256]{1,0:T(8,128)(2,1)S(1)}, u32[]{:S(2)}) copy-start(bf16[2048,256]{1,0:T(8,128)(2,1)S(1)} %get-tuple-element.46.own_ref) | copy-start | bytes 3145732
  107.1 3.9 %collective-permute-start.6 = (bf16[2048,128]{1,0:T(8,128)(2,1)}, bf16[2048,128]{1,0:T(8,128)(2,1)}, u32[]{:S(2)}, u32[]{:S(2)}) collective-permute-start(bf16[2048,128]{1,0:T(8,128)(2,1)} %dynamic-slice_convert_fusion), channel_id=1, source_target_pairs={{0,1},{1,0},{2,3},{3,2},{4,5},{5,4},{6,7},{7,6},{8,9},{9,8},{10,11... | collective-permute-start | bytes 1572872 | tf_op jit(solution)/shard_map/ppermute | solution.py:47
  109.3 3.3 %copy-start.25 = (f32[1024,128]{1,0:T(8,128)S(1)}, f32[1024,128]{1,0:T(8,128)}, u32[]{:S(2)}) copy-start(f32[1024,128]{1,0:T(8,128)} %reshape.61) | copy-start | bytes 1572868
  110.3 2.3 %collective-permute-start.14 = (bf16[512,128]{1,0:T(8,128)(2,1)S(1)}, bf16[512,128]{1,0:T(8,128)(2,1)S(1)}, u32[]{:S(2)}, u32[]{:S(2)}) collective-permute-start(bf16[512,128]{1,0:T(8,128)(2,1)S(1)} %dynamic-slice_convert_fusion.2), channel_id=1, source_target_pairs={{0,1},{1,0},{2,3},{3,2},{4,5},{5,4},{6,7},{7,6},{8,9},{9,8},{10,11... | collective-permute-start | bytes 393224 | tf_op jit(solution)/shard_map/ppermute | solution.py:47
  112.4 9.0 %collective-permute-start.7 = (bf16[1024,128]{1,0:T(8,128)(2,1)S(1)}, bf16[1024,128]{1,0:T(8,128)(2,1)S(1)}, u32[]{:S(2)}, u32[]{:S(2)}) collective-permute-start(bf16[1024,128]{1,0:T(8,128)(2,1)S(1)} %dynamic-slice_convert_fusion.1), channel_id=1, source_target_pairs={{0,2},{2,0},{4,6},{6,4},{8,10},{10,8},{12,14},{14,12},{1,3},{3,1},... | collective-permute-start | bytes 786440 | tf_op jit(solution)/shard_map/ppermute | solution.py:47
  112.7 9.4 %collective-permute-start.15 = (bf16[256,128]{1,0:T(8,128)(2,1)S(1)}, bf16[256,128]{1,0:T(8,128)(2,1)S(1)}, u32[]{:S(2)}, u32[]{:S(2)}) collective-permute-start(bf16[256,128]{1,0:T(8,128)(2,1)S(1)} %dynamic-slice_convert_fusion.4), channel_id=1, source_target_pairs={{0,2},{2,0},{4,6},{6,4},{8,10},{10,8},{12,14},{14,12},{1,3},{3,1},... | collective-permute-start | bytes 196616 | tf_op jit(solution)/shard_map/ppermute | solution.py:47
  121.5 5.0 %collective-permute-start.8 = (bf16[512,128]{1,0:T(8,128)(2,1)S(1)}, bf16[512,128]{1,0:T(8,128)(2,1)S(1)}, u32[]{:S(2)}, u32[]{:S(2)}) collective-permute-start(bf16[512,128]{1,0:T(8,128)(2,1)S(1)} %dynamic-slice_convert_fusion.3), channel_id=1, source_target_pairs={{0,4},{2,6},{4,0},{6,2},{8,12},{10,14},{12,8},{14,10},{1,5},{3,7},... | collective-permute-start | bytes 393224 | tf_op jit(solution)/shard_map/ppermute | solution.py:47
  122.2 4.8 %collective-permute-start.16 = (bf16[128,128]{1,0:T(8,128)(2,1)S(1)}, bf16[128,128]{1,0:T(8,128)(2,1)S(1)}, u32[]{:S(2)}, u32[]{:S(2)}) collective-permute-start(bf16[128,128]{1,0:T(8,128)(2,1)S(1)} %dynamic-slice_convert_fusion.6), channel_id=1, source_target_pairs={{0,4},{2,6},{4,0},{6,2},{8,12},{10,14},{12,8},{14,10},{1,5},{3,7},... | collective-permute-start | bytes 98312 | tf_op jit(solution)/shard_map/ppermute | solution.py:47
  126.6 7.1 %collective-permute-start.9 = (bf16[256,128]{1,0:T(8,128)(2,1)S(1)}, bf16[256,128]{1,0:T(8,128)(2,1)S(1)}, u32[]{:S(2)}, u32[]{:S(2)}) collective-permute-start(bf16[256,128]{1,0:T(8,128)(2,1)S(1)} %dynamic-slice_convert_fusion.5), channel_id=1, source_target_pairs={{0,8},{2,10},{4,12},{6,14},{8,0},{10,2},{12,4},{14,6},{1,9},{3,11}... | collective-permute-start | bytes 196616 | tf_op jit(solution)/shard_map/ppermute | solution.py:47
  133.7 5.6 %collective-permute-start.10 = (bf16[256,128]{1,0:T(8,128)(2,1)S(1)}, bf16[256,128]{1,0:T(8,128)(2,1)S(1)}, u32[]{:S(2)}, u32[]{:S(2)}) collective-permute-start(bf16[256,128]{1,0:T(8,128)(2,1)S(1)} %add_convert_fusion), channel_id=1, source_target_pairs={{0,8},{2,10},{4,12},{6,14},{8,0},{10,2},{12,4},{14,6},{1,9},{3,11}... | collective-permute-start | bytes 196616 | tf_op jit(solution)/shard_map/ppermute | solution.py:47
  133.8 5.7 %collective-permute-start.17 = (bf16[64,128]{1,0:T(8,128)(2,1)S(1)}, bf16[64,128]{1,0:T(8,128)(2,1)S(1)}, u32[]{:S(2)}, u32[]{:S(2)}) collective-permute-start(bf16[64,128]{1,0:T(8,128)(2,1)S(1)} %dynamic-slice_convert_fusion.7), channel_id=1, source_target_pairs={{0,8},{2,10},{4,12},{6,14},{8,0},{10,2},{12,4},{14,6},{1,9},{3,11}... | collective-permute-start | bytes 49160 | tf_op jit(solution)/shard_map/ppermute | solution.py:47
  139.4 5.2 %collective-permute-start.11 = (bf16[512,128]{1,0:T(8,128)(2,1)S(1)}, bf16[512,128]{1,0:T(8,128)(2,1)S(1)}, u32[]{:S(2)}, u32[]{:S(2)}) collective-permute-start(bf16[512,128]{1,0:T(8,128)(2,1)S(1)} %maximum_select_fusion.4), channel_id=1, source_target_pairs={{0,4},{2,6},{4,0},{6,2},{8,12},{10,14},{12,8},{14,10},{1,5},{3,7},... | collective-permute-start | bytes 393224 | tf_op jit(solution)/shard_map/ppermute | solution.py:47
  139.5 6.4 %collective-permute-start.18 = (bf16[64,128]{1,0:T(8,128)(2,1)S(1)}, bf16[64,128]{1,0:T(8,128)(2,1)S(1)}, u32[]{:S(2)}, u32[]{:S(2)}) collective-permute-start(bf16[64,128]{1,0:T(8,128)(2,1)S(1)} %add_convert_fusion.1), channel_id=1, source_target_pairs={{0,8},{2,10},{4,12},{6,14},{8,0},{10,2},{12,4},{14,6},{1,9},{3,11}... | collective-permute-start | bytes 49160 | tf_op jit(solution)/shard_map/ppermute | solution.py:47
  145.3 6.7 %collective-permute-start.12 = (bf16[1024,128]{1,0:T(8,128)(2,1)}, bf16[1024,128]{1,0:T(8,128)(2,1)}, u32[]{:S(2)}, u32[]{:S(2)}) collective-permute-start(bf16[1024,128]{1,0:T(8,128)(2,1)} %maximum_select_fusion.2), channel_id=1, source_target_pairs={{0,2},{2,0},{4,6},{6,4},{8,10},{10,8},{12,14},{14,12},{1,3},{3,1},... | collective-permute-start | bytes 786440 | tf_op jit(solution)/shard_map/ppermute | solution.py:47
  146.0 4.0 %collective-permute-start.19 = (bf16[128,128]{1,0:T(8,128)(2,1)S(1)}, bf16[128,128]{1,0:T(8,128)(2,1)S(1)}, u32[]{:S(2)}, u32[]{:S(2)}) collective-permute-start(bf16[128,128]{1,0:T(8,128)(2,1)S(1)} %maximum_select_fusion.7), channel_id=1, source_target_pairs={{0,4},{2,6},{4,0},{6,2},{8,12},{10,14},{12,8},{14,10},{1,5},{3,7},... | collective-permute-start | bytes 98312 | tf_op jit(solution)/shard_map/ppermute | solution.py:47
  150.0 10.6 %collective-permute-start.20 = (bf16[256,128]{1,0:T(8,128)(2,1)S(1)}, bf16[256,128]{1,0:T(8,128)(2,1)S(1)}, u32[]{:S(2)}, u32[]{:S(2)}) collective-permute-start(bf16[256,128]{1,0:T(8,128)(2,1)S(1)} %maximum_select_fusion.6), channel_id=1, source_target_pairs={{0,2},{2,0},{4,6},{6,4},{8,10},{10,8},{12,14},{14,12},{1,3},{3,1},... | collective-permute-start | bytes 196616 | tf_op jit(solution)/shard_map/ppermute | solution.py:47
  154.2 21.0 %collective-permute-start.13 = (bf16[2048,128]{1,0:T(8,128)(2,1)}, bf16[2048,128]{1,0:T(8,128)(2,1)}, u32[]{:S(2)}, u32[]{:S(2)}) collective-permute-start(bf16[2048,128]{1,0:T(8,128)(2,1)} %maximum_select_fusion.1), channel_id=1, source_target_pairs={{0,1},{1,0},{2,3},{3,2},{4,5},{5,4},{6,7},{7,6},{8,9},{9,8},{10,11... | collective-permute-start | bytes 1572872 | tf_op jit(solution)/shard_map/ppermute | solution.py:47
  156.0 14.7 %collective-permute-start.4 = (f32[256,256]{1,0:T(8,128)}, f32[256,256]{1,0:T(8,128)}, u32[]{:S(2)}, u32[]{:S(2)}) collective-permute-start(f32[256,256]{1,0:T(8,128)} %get-tuple-element.65), channel_id=1, source_target_pairs={{0,2},{2,4},{4,6},{6,8},{8,10},{10,12},{12,14},{1,3},{3,5},{5,7},{... | collective-permute-start | bytes 786440 | tf_op jit(solution)/shard_map/ppermute | solution.py:77
  159.2 11.4 %collective-permute-start.5 = (f32[256,256]{1,0:T(8,128)}, f32[256,256]{1,0:T(8,128)}, u32[]{:S(2)}, u32[]{:S(2)}) collective-permute-start(f32[256,256]{1,0:T(8,128)} %get-tuple-element.64), channel_id=1, source_target_pairs={{2,0},{4,2},{6,4},{8,6},{10,8},{12,10},{14,12},{3,1},{5,3},{7,5},{... | collective-permute-start | bytes 786440 | tf_op jit(solution)/shard_map/ppermute | solution.py:82
  160.6 13.3 %collective-permute-start.21 = (bf16[512,128]{1,0:T(8,128)(2,1)S(1)}, bf16[512,128]{1,0:T(8,128)(2,1)S(1)}, u32[]{:S(2)}, u32[]{:S(2)}) collective-permute-start(bf16[512,128]{1,0:T(8,128)(2,1)S(1)} %maximum_select_fusion.5), channel_id=1, source_target_pairs={{0,1},{1,0},{2,3},{3,2},{4,5},{5,4},{6,7},{7,6},{8,9},{9,8},{10,11... | collective-permute-start | bytes 393224 | tf_op jit(solution)/shard_map/ppermute | solution.py:47
  160.9 1.2 copy-start.20
  162.1 8.6 %copy-start.6 = (bf16[2048,256]{1,0:T(8,128)(2,1)S(1)}, bf16[2048,256]{1,0:T(8,128)(2,1)}, u32[]{:S(2)}) copy-start(bf16[2048,256]{1,0:T(8,128)(2,1)} %copy-done.5) | copy-start | bytes 3145732
  (8 other events, 5.4 us)
where the time goes:
time: 180 us; the launch traced here: 178 us
  starting transfers between devices  45 us (25%)
  waiting for transfers between devices  42.6 us (24%)
  Pallas kernels  35.4 us (20%)
  local copies, waits for them, and re-layouts  35.3 us (20%)
  other arithmetic  9.58 us (5%)
  blocking collectives  9.52 us (5%)
    pallas_call x9, Pallas kernels, call(): pl.pallas_call(kernel, out_shape=[jax.ShapeDtypeStruct(shape, dtype) for...  35.4 us
    ppermute x16, waiting for transfers between devices, swap(): lax.ppermute(block, axis, [(i, i ^ bit) for i in range(lax.axis_size(axis...  26.7 us
    unnamed x64, local copies, waits for them, and re-layouts  19.1 us
    all_to_all x3, starting transfers between devices, exchange(): return lax.all_to_all(copies, GROUP, 0, 0)  15 us
    ppermute x3, starting transfers between devices, to_above(): return lax.ppermute(block, 'space', [(i, i + 1) for i in range(count - 1)])  13.6 us
    ppermute x16, starting transfers between devices, swap(): lax.ppermute(block, axis, [(i, i ^ bit) for i in range(lax.axis_size(axis...  12.6 us
    all_to_all x3, waiting for transfers between devices, exchange(): return lax.all_to_all(copies, GROUP, 0, 0)  11.8 us
    all_to_all x1, blocking collectives, exchange(): return lax.all_to_all(copies, GROUP, 0, 0)  9.52 us
  transfers between devices with their start and end apart: 25, of which 13 were waited for; matrix products, arithmetic and copies ran while one was open for 14% of the time, Pallas kernels for 10%

commit v1 on v0

--- a/solution.py
+++ b/solution.py
@@ -33,39 +33,43 @@
     return lax.axis_size("space") * lax.axis_size("rep")
 
 
-def exchange_steps():
-    steps = []
-    for axis in ("rep", "space"):
-        bit = 1
-        while bit < lax.axis_size(axis):
-            steps.append((axis, bit))
-            bit *= 2
-    return steps
-
-
 def swap(block, axis, bit):
     return lax.ppermute(block, axis, [(i, i ^ bit) for i in range(lax.axis_size(axis))])
 
 
-def halving_sum(values):
-    steps = exchange_steps()
-    part = values
-    for axis, bit in steps:
-        upper = (lax.axis_index(axis) // bit) % 2
-        half = part.shape[0] // 2
-        kept = lax.dynamic_slice_in_dim(part, upper * half, half)
-        sent = lax.dynamic_slice_in_dim(part, (1 - upper) * half, half).astype(BF16)
-        part = kept + swap(sent, axis, bit).astype(F32)
-    part = part.astype(BF16)
-    for axis, bit in reversed(steps):
-        upper = (lax.axis_index(axis) // bit) % 2
-        other = swap(part, axis, bit)
-        part = jnp.where(
-            upper == 0,
-            jnp.concatenate([part, other]),
-            jnp.concatenate([other, part]),
-        )
-    return part.astype(F32)
+def chunk_steps():
+    bits = []
+    bit = 1
+    while bit < lax.axis_size("space"):
+        bits.append(("space", bit))
+        bit *= 2
+    return bits, bits[1:2] + bits[0:1] + bits[2:]
+
+
+def halve(part, axis, bit):
+    upper = (lax.axis_index(axis) // bit) % 2
+    half = part.shape[0] // 2
+    kept = lax.dynamic_slice_in_dim(part, upper * half, half)
+    sent = lax.dynamic_slice_in_dim(part, (1 - upper) * half, half).astype(BF16)
+    return kept + swap(sent, axis, bit).astype(F32)
+
+
+def double(part, axis, bit):
+    upper = (lax.axis_index(axis) // bit) % 2
+    other = swap(part, axis, bit)
+    return jnp.where(
+        upper == 0, jnp.concatenate([part, other]), jnp.concatenate([other, part])
+    )
+
+
+def space_sums(parts):
+    orders = chunk_steps()
+    for step in range(len(orders[0])):
+        parts = [halve(part, *order[step]) for part, order in zip(parts, orders)]
+    parts = [part.astype(BF16) for part in parts]
+    for step in reversed(range(len(orders[0]))):
+        parts = [double(part, *order[step]) for part, order in zip(parts, orders)]
+    return parts
 
 
 def exchange(copies):
@@ -89,7 +93,7 @@
         in_specs=[pl.BlockSpec(memory_space=pltpu.VMEM)] * len(args),
         out_specs=[pl.BlockSpec(memory_space=pltpu.VMEM)] * len(outs),
         scratch_shapes=list(scratch),
-        compiler_params=pltpu.CompilerParams(vmem_limit_bytes=48 * 2**20),
+        compiler_params=pltpu.CompilerParams(vmem_limit_bytes=24 * 2**20),
         cost_estimate=pl.CostEstimate(flops=10**9, bytes_accessed=4 * 10**6, transcendentals=0),
     )(*args)
 
@@ -155,7 +159,43 @@
     return 1.0 / (1.0 + jnp.exp(-values))
 
 
-def prepare_kernel(w1_ref, w2_ref, a1_ref, a2_ref, b1_ref, b2_ref, sh_ref):
+def spread_planes(cot_ref, out_ref, planes):
+    matrix = spread_matrix()
+    for rp in range(2):
+        for rp2 in range(2):
+            for h in range(2):
+                lanes = [(4 * (2 * h + jj) + 2 * rp + rp2) * 256 for jj in range(2)]
+                rows = jnp.concatenate(
+                    [cot_ref[0 : len(planes) * C2, at : at + 256] for at in lanes], axis=1
+                )
+                moved = matmul(rows, matrix).astype(BF16)
+                for cp2 in range(2):
+                    for cp in range(2):
+                        row = (2 * rp2 + cp2) * C2
+                        lane = (2 * rp + cp) * CELLS + h * 128
+                        piece = moved[:, cp2 * 256 + cp * 128 : cp2 * 256 + cp * 128 + 128]
+                        for k, t in enumerate(planes):
+                            out_ref[t, row : row + C2, lane : lane + 128] = piece[
+                                k * C2 : (k + 1) * C2
+                            ]
+
+
+def prepare_kernel(
+    w1_ref, w2_ref, gain1_ref, shift1_ref, gain2_ref, shift2_ref, cot_ref,
+    a1_ref, a2_ref, b1_ref, b2_ref, sh_ref, p1_ref, p2_ref, spread_ref,
+):
+    place = lax.axis_index("space")
+    below = jnp.where(place > 0, 1.0, 0.0)
+    above = jnp.where(place < lax.axis_size("space") - 1, 1.0, 0.0)
+    edges = [jnp.full((1, 128), below, F32), jnp.full((1, 128), above, F32)]
+    blank = [jnp.zeros((4, 128), F32)]
+    p1_ref[...] = jnp.concatenate(
+        [jnp.concatenate([ref[...]] * 2, axis=1) for ref in (gain1_ref, shift1_ref)] + edges + blank
+    )
+    p2_ref[...] = jnp.concatenate(
+        [jnp.concatenate([ref[...]] * 4, axis=1) for ref in (gain2_ref, shift2_ref)] + edges + blank
+    )
+    spread_planes(cot_ref, spread_ref, range(4))
     for dj in (-1, 0, 1):
         for dl in (-1, 0, 1):
             sh_ref[:, shift_slot(dj, dl)] = shift_matrix(dj, dl)
@@ -197,8 +237,20 @@
         )
 
 
-def first_kernel(lat_ref, below_ref, above_ref, a1_ref, sh_ref, pre_ref, out_ref, x_ref):
-    planes = jnp.concatenate([below_ref[...], lat_ref[...], above_ref[...]], axis=0)
+def halo_latent(halo_ref):
+    rows = halo_ref[C2 : C2 + 8, :].astype(F32)
+    return jnp.concatenate(
+        [rows[:, m * CELLS : (m + 1) * CELLS] for m in range(C0 // 8)], axis=0
+    ).astype(BF16)
+
+
+def first_kernel(
+    lat_ref, below_ref, above_ref, a1_ref, sh_ref,
+    pre_ref, out_ref, spread_ref, near_ref, x_ref,
+):
+    near_ref[0] = halo_latent(below_ref)
+    near_ref[1] = halo_latent(above_ref)
+    planes = jnp.concatenate([near_ref[0], lat_ref[...], near_ref[1]], axis=0)
     for k in range(9):
         moved = matmul(planes, sh_ref[:, k * CELLS : (k + 1) * CELLS]).astype(BF16)
         for z in range(3):
@@ -215,6 +267,8 @@
     lower, upper = lower - wide, upper - wide
     squares = fold(jnp.sum(lower * lower + upper * upper, axis=1, keepdims=True), C1)
     emit_rows(out_ref, mean, squares)
+    spread_planes(below_ref, spread_ref, (0,))
+    spread_planes(above_ref, spread_ref, (1,))
 
 
 def second_kernel(got_ref, pre1_ref, p1_ref, a2_ref, sh_ref, pre_ref, act_ref, st_ref, out_ref, x_ref):
@@ -269,26 +323,6 @@
     emit_rows(out_ref, mean, fold(jnp.sum(squares, axis=1, keepdims=True), C2))
 
 
-def spread_kernel(cot_ref, out_ref):
-    matrix = spread_matrix()
-    count = cot_ref.shape[0] // C2
-    for rp in range(2):
-        for rp2 in range(2):
-            for h in range(2):
-                lanes = [(4 * (2 * h + jj) + 2 * rp + rp2) * 256 for jj in range(2)]
-                rows = jnp.concatenate([cot_ref[:, at : at + 256] for at in lanes], axis=1)
-                moved = matmul(rows, matrix).astype(BF16)
-                for cp2 in range(2):
-                    for cp in range(2):
-                        row = (2 * rp2 + cp2) * C2
-                        lane = (2 * rp + cp) * CELLS + h * 128
-                        piece = moved[:, cp2 * 256 + cp * 128 : cp2 * 256 + cp * 128 + 128]
-                        for t in range(count):
-                            out_ref[t, row : row + C2, lane : lane + 128] = piece[
-                                t * C2 : (t + 1) * C2
-                            ]
-
-
 def gather_kernel(feat_ref, out_ref):
     matrix = spread_matrix()
     count = feat_ref.shape[0]
@@ -315,32 +349,32 @@
                     out_ref[:, at : at + 256] = moved[:, jj * 256 : (jj + 1) * 256]
 
 
-def third_kernel(got_ref, pre_ref, cot_ref, p2_ref, grad_ref, feat_ref, st_ref, out_ref):
+def third_kernel(got_ref, pre_ref, cot_ref, edge_ref, p2_ref, grad_ref, feat_ref, st_ref, out_ref):
     mean, scale = moments(got_ref[...], 64 * CELLS)
     st = jnp.concatenate([mean, scale, p2_ref[0:6]], axis=0)
     st_ref[...] = st
     cols = columns(st)
     mean, scale, gain, shift = (cols[:, k : k + 1] for k in range(4))
 
-    def slope(t, lane):
+    def slope(t, lane, cot):
         hat = (pre_ref[t, :, pl.ds(lane, CELLS)] - mean) * scale
         norm = gain * hat + shift
         gate = sigmoid(norm)
-        cot = cot_ref[t, :, pl.ds(lane, CELLS)].astype(F32)
-        grad = cot * (gate * (1.0 + norm * (1.0 - gate)))
+        grad = cot.astype(F32) * (gate * (1.0 + norm * (1.0 - gate)))
         grad_ref[t, :, pl.ds(lane, CELLS)] = grad
         return hat, norm, gate, grad
 
-    for t in (0, 5):
+    for k in range(2):
 
         @pl.loop(0, 4)
         def _(block):
-            slope(t, pl.multiple_of(block * CELLS, CELLS))
+            lane = pl.multiple_of(block * CELLS, CELLS)
+            slope(5 * k, lane, edge_ref[k, :, pl.ds(lane, CELLS)])
 
     def body(k, carry):
         t = k // 4 + 1
         lane = pl.multiple_of((k % 4) * CELLS, CELLS)
-        hat, norm, gate, grad = slope(t, lane)
+        hat, norm, gate, grad = slope(t, lane, cot_ref[t - 1, :, pl.ds(lane, CELLS)])
         feat_ref[t - 1, :, pl.ds(lane, CELLS)] = (norm * gate).astype(BF16)
         return carry[0] + grad * hat, carry[1] + grad
 
@@ -410,10 +444,14 @@
         jnp.sum(first, axis=1, keepdims=True),
         jnp.sum(second, axis=1, keepdims=True),
     )
+    parts = []
     for p in range(4):
         part = matmul_nt(x_ref[p * 16 * C2 : (p + 1) * 16 * C2, :], act_ref[0])
-        part = part + matmul_nt(x_ref[(p + 2) * 16 * C2 : (p + 3) * 16 * C2, :], act_ref[1])
-        dw_ref[p * 16 * C2 : (p + 1) * 16 * C2, :] = part
+        parts.append(part + matmul_nt(x_ref[(p + 2) * 16 * C2 : (p + 3) * 16 * C2, :], act_ref[1]))
+    for p in range(2):
+        dw_ref[p * 16 * C2 : (p + 1) * 16 * C2, :] = jnp.concatenate(
+            [parts[p], parts[p + 2]], axis=1
+        )
 
 
 def first_dpre(grad, pre, cols, keep):
@@ -442,7 +480,8 @@
 
 
 def fifth_kernel(
-    got_ref, g1_ref, pre1_ref, st1_ref, sh_ref, lat_ref, below_ref, above_ref, dw_ref, sum_ref, x_ref
+    got_ref, g1_ref, pre1_ref, st1_ref, sh_ref, lat_ref, near_ref, dw2_ref,
+    keep_a_ref, keep_b_ref, send_a_ref, send_b_ref, sum_ref, x_ref, dw_ref,
 ):
     sums = jnp.sum(got_ref[...], axis=0)
     sum_ref[...] = sums
@@ -452,11 +491,35 @@
         first_windows(
             x_ref, j * 16 * C1, g1_ref.at[j], pre1_ref.at[j + 1], cols, None, sh_ref
         )
-    for p, j, field in ((0, 1, above_ref), (1, 0, lat_ref), (2, 1, lat_ref), (3, 0, below_ref)):
+    fields = (near_ref[1], lat_ref[...], lat_ref[...], near_ref[0])
+    for p, j, field in ((0, 1, fields[0]), (1, 0, fields[1]), (2, 1, fields[2]), (3, 0, fields[3])):
         for half in range(2):
             at = p * 16 * C1 + half * 8 * C1
             src = j * 16 * C1 + half * 8 * C1
-            dw_ref[at : at + 8 * C1, :] = matmul_nt(x_ref[src : src + 8 * C1, :], field[...])
+            dw_ref[at : at + 8 * C1, :] = matmul_nt(x_ref[src : src + 8 * C1, :], field)
+    dw_ref[64 * C1 :, :] = dw2_ref[...]
+    chunk = dw_ref.shape[0] // 4
+    core = lax.axis_index("rep")
+    mine = pl.multiple_of(core * (2 * chunk), 2 * chunk)
+    theirs = pl.multiple_of((1 - core) * (2 * chunk), 2 * chunk)
+    keep_a_ref[...] = dw_ref[pl.ds(mine, chunk), :]
+    keep_b_ref[...] = dw_ref[pl.ds(mine + chunk, chunk), :]
+    send_a_ref[...] = dw_ref[pl.ds(theirs, chunk), :].astype(BF16)
+    send_b_ref[...] = dw_ref[pl.ds(theirs + chunk, chunk), :].astype(BF16)
+
+
+def last_kernel(own_a_ref, own_b_ref, other_a_ref, other_b_ref, dw1_ref, dw2_ref, x_ref):
+    core = lax.axis_index("rep")
+    chunk = own_a_ref.shape[0]
+    mine = pl.multiple_of(core * (2 * chunk), 2 * chunk)
+    theirs = pl.multiple_of((1 - core) * (2 * chunk), 2 * chunk)
+    x_ref[pl.ds(mine, chunk), :] = own_a_ref[...].astype(F32)
+    x_ref[pl.ds(mine + chunk, chunk), :] = own_b_ref[...].astype(F32)
+    x_ref[pl.ds(theirs, chunk), :] = other_a_ref[...].astype(F32)
+    x_ref[pl.ds(theirs + chunk, chunk), :] = other_b_ref[...].astype(F32)
+    dw1_ref[...] = x_ref[0 : 64 * C1, :]
+    dw2_ref[0 : 32 * C2, :] = x_ref[64 * C1 :, 0:C1]
+    dw2_ref[32 * C2 :, :] = x_ref[64 * C1 :, C1:]
 
 
 def sixth_kernel(
@@ -483,27 +546,15 @@
     cotangent,
 ):
     count = group_size()
-    place = lax.axis_index("space")
-    below_is = jnp.full((128,), place > 0, F32)
-    above_is = jnp.full((128,), place < lax.axis_size("space") - 1, F32)
-    blank = jnp.zeros((128,), F32)
-    p1 = jnp.stack(
-        [jnp.tile(first_norm_gain, 2), jnp.tile(first_norm_shift, 2), below_is, above_is]
-        + [blank] * 4
-    )
-    p2 = jnp.stack(
-        [jnp.tile(second_norm_gain, 4), jnp.tile(second_norm_shift, 4), below_is, above_is]
-        + [blank] * 4
-    )
     lat = latent.reshape(C0, CELLS)
-    lat_below = to_above(lat)
-    lat_above = to_below(lat)
-    cot = cotangent.reshape(C2, 4, 16 * CELLS).transpose(1, 0, 2)
-    cot_below = to_above(cot[3])
-    cot_above = to_below(cot[0])
+    cot = cotangent.reshape(C2, 4, 16 * CELLS)
+    low = lat.reshape(C0 // 8, 8, CELLS).transpose(1, 0, 2).reshape(8, 16 * CELLS)
+    below = to_above(jnp.concatenate([cot[:, 3], low]))
+    above = to_below(jnp.concatenate([cot[:, 0], low]))
+    planes = cot.transpose(1, 0, 2).reshape(4 * C2, 16 * CELLS)
     w1 = first_weight.reshape(64 * C1, C0)
     w2 = second_weight.reshape(64 * C2, C1)
-    a1, a2, b1, b2, sh = call(
+    a1, a2, b1, b2, sh, p1, p2, spread = call(
         prepare_kernel,
         [
             ((8 * C1, 18 * C0), BF16),
@@ -511,20 +562,31 @@
             ((C0, 64 * C1), BF16),
             ((C1, 64 * C2), BF16),
             ((CELLS, 9 * CELLS), BF16),
+            ((8, 128), F32),
+            ((8, 128), F32),
+            ((4, 4 * C2, 4 * CELLS), BF16),
         ],
-        [w1, w2],
+        [
+            w1,
+            w2,
+            first_norm_gain.reshape(1, C1),
+            first_norm_shift.reshape(1, C1),
+            second_norm_gain.reshape(1, C2),
+            second_norm_shift.reshape(1, C2),
+            planes,
+        ],
     )
     stats = ((count, 8, 128), F32)
-    pre1, out = call(
+    pre1, out, edge, near = call(
         first_kernel,
-        [((4, 4 * C1, CELLS), F32), stats],
-        [lat, lat_below, lat_above, a1, sh],
+        [
+            ((4, 4 * C1, CELLS), F32),
+            stats,
+            ((2, 4 * C2, 4 * CELLS), BF16),
+            ((2, C0, CELLS), BF16),
+        ],
+        [lat, below, above, a1, sh],
         [pltpu.VMEM((27 * C0, CELLS), BF16)],
-    )
-    (spread,) = call(
-        spread_kernel,
-        [((6, 4 * C2, 4 * CELLS), BF16)],
-        [jnp.concatenate([cot_below[None], cot, cot_above[None]]).reshape(6 * C2, 16 * CELLS)],
     )
     got = exchange(out)
     pre2, act, st1, out = call(
@@ -542,22 +604,31 @@
             ((8, 128), F32),
             stats,
         ],
-        [got, pre2, spread, p2],
+        [got, pre2, spread, edge, p2],
     )
     got = exchange(out)
     grad1, dw2, sum2, out = call(
         fourth_kernel,
-        [((2, 4 * C1, CELLS), F32), ((64 * C2, C1), F32), ((8, 128), F32), stats],
+        [((2, 4 * C1, CELLS), F32), ((32 * C2, 2 * C1), F32), ((8, 128), F32), stats],
         [got, pre2, grad2, st2, b2, sh, act, pre1, st1],
         [pltpu.VMEM((96 * C2, 4 * CELLS), BF16)],
     )
     grad_below = to_above(grad1[1])
     grad_above = to_below(grad1[0])
     got = exchange(out)
-    dw1, sum1, windows = call(
+    rows = (64 * C1 + 32 * C2) // 4
+    keep_a, keep_b, send_a, send_b, sum1, windows = call(
         fifth_kernel,
-        [((64 * C1, C0), F32), ((8, 128), F32), ((32 * C1, CELLS), BF16)],
-        [got, grad1, pre1, st1, sh, lat, lat_below, lat_above],
+        [
+            ((rows, C0), F32),
+            ((rows, C0), F32),
+            ((rows, C0), BF16),
+            ((rows, C0), BF16),
+            ((8, 128), F32),
+            ((32 * C1, CELLS), BF16),
+        ],
+        [got, grad1, pre1, st1, sh, lat, near, dw2],
+        [pltpu.VMEM((4 * rows, C0), F32)],
     )
     (latent_grad,) = call(
         sixth_kernel,
@@ -567,13 +638,23 @@
     )
     (features,) = call(gather_kernel, [((4 * C2, 16 * CELLS), BF16)], [feat])
     features = features.reshape(4, C2, 16 * CELLS).transpose(1, 0, 2)
-    second_weight_grad = halving_sum(dw2.reshape(-1, 128)).reshape(64, C2, C1)
-    first_weight_grad = halving_sum(dw1).reshape(64, C1, C0)
+    part_a, part_b = space_sums(
+        [
+            keep_a + swap(send_a, "rep", 1).astype(F32),
+            keep_b + swap(send_b, "rep", 1).astype(F32),
+        ]
+    )
+    first_weight_grad, second_weight_grad = call(
+        last_kernel,
+        [((64 * C1, C0), F32), ((64 * C2, C1), F32)],
+        [part_a, part_b, swap(part_a, "rep", 1), swap(part_b, "rep", 1)],
+        [pltpu.VMEM((4 * rows, C0), F32)],
+    )
     return (
         features[None],
         latent_grad.reshape(1, C0, 1, CELLS),
-        first_weight_grad,
-        second_weight_grad,
+        first_weight_grad.reshape(64, C1, C0),
+        second_weight_grad.reshape(64, C2, C1),
         sum1[0:2, 0:C1],
         sum2[0:2, 0:C2],
     )

time: 180 us -> 146 us (0.81)
  blocking collectives: 9.52 us -> 42 us
  local copies, waits for them, and re-layouts: 35.3 us -> 10.2 us
  starting transfers between devices: 45 us -> 25.6 us
  waiting for transfers between devices: 42.6 us -> 31.9 us
  other arithmetic: 9.58 us -> 1.76 us
  Pallas kernels: 35.4 us -> 31.7 us
    all_to_all x1 -> x4, blocking collectives: 9.52 us -> 42 us  [exchange(): return lax.all_to_all(copies, GROUP, 0, 0)]
    all_to_all x3 -> x0, starting transfers between devices: 15 us -> none  [exchange(): return lax.all_to_all(copies, GROUP, 0, 0)]
    unnamed x64 -> x36, local copies, waits for them, and re-layouts: 19.1 us -> 7.14 us
    all_to_all x3 -> x0, waiting for transfers between devices: 11.8 us -> none  [exchange(): return lax.all_to_all(copies, GROUP, 0, 0)]
    ppermute x3 -> x2, starting transfers between devices: 13.6 us -> 7.18 us  [to_above(): return lax.ppermute(block, 'space', [(i, i + 1) for i in range(count - 1)])]
    another operation x13 -> x0, local copies, waits for them, and re-layouts: 5.09 us -> none  [the longest x5 3.05 us: local(): jnp.stack([jnp.tile(first_norm_gain, 2), jnp.tile(first_norm_shift, 2), b...]
    ppermute x3 -> x2, waiting for transfers between devices: 4.16 us -> 9.17 us  [to_above(): return lax.ppermute(block, 'space', [(i, i + 1) for i in range(count - 1)])]
    select_n x7 -> x6, other arithmetic: 4.78 us -> 0.3 us  [double(): jnp.where(upper == 0, jnp.concatenate([part, other]), jnp.concatenate([ot...]
  transfers between devices with their start and end apart: 25 -> 20, of which waited for: 13 -> 10; matrix products, arithmetic and copies ran while one was open for 14% -> 4% of each run, Pallas kernels for 10% -> 4%
where the time goes in v1:
time: 146 us; the launch traced here: 144 us
  blocking collectives  42 us (29%)
  waiting for transfers between devices  31.9 us (22%)
  Pallas kernels  31.7 us (22%)
  starting transfers between devices  25.6 us (18%)
  local copies, waits for them, and re-layouts  10.2 us (7%)
  other arithmetic  1.76 us (1%)
    all_to_all x4, blocking collectives, exchange(): return lax.all_to_all(copies, GROUP, 0, 0)  42 us
    pallas_call x9, Pallas kernels, call(): pl.pallas_call(kernel, out_shape=[jax.ShapeDtypeStruct(shape, dtype) for...  31.7 us
    ppermute x16, waiting for transfers between devices, swap(): lax.ppermute(block, axis, [(i, i ^ bit) for i in range(lax.axis_size(axis...  22.7 us
    ppermute x16, starting transfers between devices, swap(): lax.ppermute(block, axis, [(i, i ^ bit) for i in range(lax.axis_size(axis...  15.8 us
    ppermute x2, waiting for transfers between devices, to_above(): return lax.ppermute(block, 'space', [(i, i + 1) for i in range(count - 1)])  9.17 us
    ppermute x2, starting transfers between devices, to_above(): return lax.ppermute(block, 'space', [(i, i + 1) for i in range(count - 1)])  7.18 us
    unnamed x36, local copies, waits for them, and re-layouts  7.14 us
  transfers between devices with their start and end apart: 20, of which 10 were waited for; matrix products, arithmetic and copies ran while one was open for 4% of the time, Pallas kernels for 4%

profile of v1, /device:TPU:0, one launch (start us, length us, event | category | flops | bytes accessed | tf_op | source)
XLA Modules:
  0.0 144.2 jit_solution(18230463966527130490)
XLA Ops:
  0.7 1.9 %copy.21 = bf16[1,32,4,4096]{3,1,2,0:T(8,128)(2,1)S(1)} copy(bf16[1,32,4,4096]{3,2,1,0:T(4,128)(2,1)} %param.15) | data formatting | bytes 2097152 | tf_op args[7]
  2.7 4.9 %collective-permute-start = (bf16[40,4096]{1,0:T(8,128)(2,1)S(1)}, bf16[40,4096]{1,0:T(8,128)(2,1)S(1)}, u32[]{:S(2)}, u32[]{:S(2)}) collective-permute-start(bf16[40,4096]{1,0:T(8,128)(2,1)S(1)} %get-tuple-element.83), channel_id=1, source_target_pairs={{0,2},{2,4},{4,6},{6,8},{8,10},{10,12},{12,14},{1,3},{3,5},{5,7},{... | collective-permute-start | bytes 983048 | tf_op jit(solution)/shard_map/ppermute | solution.py:81
  7.6 1.3 collective-permute-start.1
  9.0 3.4 %shard_map.127 = (bf16[512,2304]{1,0:T(8,128)(2,1)S(1)}, bf16[256,1152]{1,0:T(8,128)(2,1)S(1)}, bf16[128,4096]{1,0:T(8,128)(2,1)S(1)}, bf16[64,2048]{1,0:T(8,128...) custom-call(bf16[4096,128]{1,0:T(8,128)(2,1)S(1)} %bitcast.42, ...), custom_call_target="tpu_custom_call" | custom-call | flops 1000000000 | bytes 4000000 | tf_op jit(solution)/shard_map/pallas_call | solution.py:90
  12.4 9.2 %collective-permute-done.below_ref = bf16[40,4096]{1,0:T(8,128)(2,1)S(1)} collective-permute-done((bf16[40,4096]{1,0:T(8,128)(2,1)S(1)}, bf16[40,4096]{1,0:T(8,128)(2,1)S(1)}, u32[]{:S(2)}, u32[]{:S(2)}) %collective-permute-start) | collective-permute-done | bytes 327712 | tf_op jit(solution)/shard_map/ppermute | solution.py:81
  21.6 3.3 %shard_map.128 = (f32[4,256,256]{2,1,0:T(8,128)S(1)}, f32[16,8,128]{2,1,0:T(8,128)S(1)}, bf16[2,128,1024]{2,1,0:T(8,128)(2,1)S(1)}, bf16[2,128,256]{2,1,0:T(8,128)(2,1)S(1)}) custom-call(bf16[128,256]{1,0:T(8,128)(2,1)S(1)} %bitcast.40, bf16[40,4096]{1,0:T(8,128)(2,1)S(1)} %collective-permute-done.below_ref, ...), custom_call_target="tpu_custom_call" | custom-call | flops 1000000000 | bytes 4000000 | tf_op jit(solution)/shard_map/pallas_call | solution.py:90
  24.9 13.5 %all_to_all.20.got_ref = f32[16,8,128]{2,1,0:T(8,128)S(1)} all-to-all(f32[16,8,128]{2,1,0:T(8,128)S(1)} %get-tuple-element.40), channel_id=1, replica_groups=mesh['group'=2,'space'=8,'rep'=2] {'space','rep'}, dimensions={0} | all-to-all | bytes 131072 | tf_op jit(solution)/shard_map/all_to_all | solution.py:76
  38.4 6.2 %shard_map.129 = (f32[6,128,1024]{2,1,0:T(8,128)S(1)}, bf16[2,64,1024]{2,1,0:T(8,128)(2,1)S(1)}, f32[8,128]{1,0:T(8,128)S(1)}, f32[16,8,128]{2,1,0:T(8,128)S(1)}) custom-call(f32[16,8,128]{2,1,0:T(8,128)S(1)} %all_to_all.20.got_ref, f32[4,256,256]{2,1,0:T(8,128)S(1)} %get-tuple-element.41.pre1_ref, f32[8,128]{1,0:T(8,128)S(1)} %get-tuple-element.42.p1_ref, ...), custom_call_target="tpu_custom_call" | custom-call | flops 1000000000 | bytes 4000000 | tf_op jit(solution)/shard_map/pallas_call | solution.py:90
  44.6 9.5 %all_to_all.21.got_ref = f32[16,8,128]{2,1,0:T(8,128)S(1)} all-to-all(f32[16,8,128]{2,1,0:T(8,128)S(1)} %get-tuple-element.44), channel_id=1, replica_groups=mesh['group'=2,'space'=8,'rep'=2] {'space','rep'}, dimensions={0} | all-to-all | bytes 131072 | tf_op jit(solution)/shard_map/all_to_all | solution.py:76
  54.1 5.3 %shard_map.130 = (f32[6,128,1024]{2,1,0:T(8,128)S(1)}, bf16[4,128,1024]{2,1,0:T(8,128)(2,1)S(1)}, f32[8,128]{1,0:T(8,128)S(1)}, f32[16,8,128]{2,1,0:T(8,128)S(1)}) custom-call(f32[16,8,128]{2,1,0:T(8,128)S(1)} %all_to_all.21.got_ref, f32[6,128,1024]{2,1,0:T(8,128)S(1)} %get-tuple-element.45.pre_ref, bf16[4,128,1024]{2,1,0:T(8,128)(2,1)S(1)} %get-tuple-element.46.cot_ref, ...), custom_call_target="tpu_custom_call" | custom-call | flops 1000000000 | bytes 4000000 | tf_op jit(solution)/shard_map/pallas_call | solution.py:90
  59.4 1.0 copy-done.9
  60.4 9.5 %all_to_all.22.got_ref = f32[16,8,128]{2,1,0:T(8,128)S(1)} all-to-all(f32[16,8,128]{2,1,0:T(8,128)S(1)} %get-tuple-element.50), channel_id=1, replica_groups=mesh['group'=2,'space'=8,'rep'=2] {'space','rep'}, dimensions={0} | all-to-all | bytes 131072 | tf_op jit(solution)/shard_map/all_to_all | solution.py:76
  69.8 5.9 %shard_map.132 = (f32[2,256,256]{2,1,0:T(8,128)S(1)}, f32[1024,128]{1,0:T(8,128)S(1)}, f32[8,128]{1,0:T(8,128)S(1)}, f32[16,8,128]{2,1,0:T(8,128)S(1)}) custom-call(f32[16,8,128]{2,1,0:T(8,128)S(1)} %all_to_all.22.got_ref, f32[6,128,1024]{2,1,0:T(8,128)S(1)} %get-tuple-element.45.pre_ref, f32[6,128,1024]{2,1,0:T(8,128)S(1)} %get-tuple-element.51.grad_ref, ...), custom_call_target="tpu_custom_call" | custom-call | flops 1000000000 | bytes 4000000 | tf_op jit(solution)/shard_map/pallas_call | solution.py:90
  75.7 9.5 %all_to_all.23.got_ref.count_ref = f32[16,8,128]{2,1,0:T(8,128)S(1)} all-to-all(f32[16,8,128]{2,1,0:T(8,128)S(1)} %get-tuple-element.56), channel_id=1, replica_groups=mesh['group'=2,'space'=8,'rep'=2] {'space','rep'}, dimensions={0} | all-to-all | bytes 131072 | tf_op jit(solution)/shard_map/all_to_all | solution.py:76
  85.2 2.7 %shard_map.133 = (f32[1280,128]{1,0:T(8,128)S(1)}, f32[1280,128]{1,0:T(8,128)S(1)}, bf16[1280,128]{1,0:T(8,128)(2,1)S(1)}, bf16[1280,128]{1,0:T(8,128)(2,1)}, f3...) custom-call(f32[16,8,128]{2,1,0:T(8,128)S(1)} %all_to_all.23.got_ref.count_ref, ...), custom_call_target="tpu_custom_call" | custom-call | flops 1000000000 | bytes 4000000 | tf_op jit(solution)/shard_map/pallas_call | solution.py:90
  87.9 1.0 copy-done
  88.9 0.8 copy-done.2
  89.7 0.8 copy-done.4
  90.5 0.7 copy-done.12
  91.3 0.5 collective-permute-start.4
  91.8 1.6 %collective-permute-done.11 = bf16[1280,128]{1,0:T(8,128)(2,1)} collective-permute-done((bf16[1280,128]{1,0:T(8,128)(2,1)}, bf16[1280,128]{1,0:T(8,128)(2,1)}, u32[]{:S(2)}, u32[]{:S(2)}) %collective-permute-start.11) | collective-permute-done | bytes 327712 | tf_op jit(solution)/shard_map/ppermute | solution.py:37
  93.3 1.2 convert_add_fusion
  94.8 0.7 collective-permute-start.5
  95.5 5.4 %collective-permute-done.12 = bf16[640,128]{1,0:T(8,128)(2,1)S(1)} collective-permute-done((bf16[640,128]{1,0:T(8,128)(2,1)S(1)}, bf16[640,128]{1,0:T(8,128)(2,1)S(1)}, u32[]{:S(2)}, u32[]{:S(2)}) %collective-permute-start.12) | collective-permute-done | bytes 163872 | tf_op jit(solution)/shard_map/ppermute | solution.py:37
  101.2 1.8 %collective-permute-start.6 = (bf16[320,128]{1,0:T(8,128)(2,1)S(1)}, bf16[320,128]{1,0:T(8,128)(2,1)S(1)}, u32[]{:S(2)}, u32[]{:S(2)}) collective-permute-start(bf16[320,128]{1,0:T(8,128)(2,1)S(1)} %dynamic-slice_convert_fusion.3), channel_id=1, source_target_pairs={{0,4},{2,6},{4,0},{6,2},{8,12},{10,14},{12,8},{14,10},{1,5},{3,7},... | collective-permute-start | bytes 245768 | tf_op jit(solution)/shard_map/ppermute | solution.py:37
  103.0 2.5 %collective-permute-done.13 = bf16[320,128]{1,0:T(8,128)(2,1)S(1)} collective-permute-done((bf16[320,128]{1,0:T(8,128)(2,1)S(1)}, bf16[320,128]{1,0:T(8,128)(2,1)S(1)}, u32[]{:S(2)}, u32[]{:S(2)}) %collective-permute-start.13) | collective-permute-done | bytes 81952 | tf_op jit(solution)/shard_map/ppermute | solution.py:37
  105.5 0.2 collective-permute-start.14
  105.8 2.9 %collective-permute-start.7 = (bf16[160,128]{1,0:T(8,128)(2,1)S(1)}, bf16[160,128]{1,0:T(8,128)(2,1)S(1)}, u32[]{:S(2)}, u32[]{:S(2)}) collective-permute-start(bf16[160,128]{1,0:T(8,128)(2,1)S(1)} %dynamic-slice_convert_fusion.5), channel_id=1, source_target_pairs={{0,8},{2,10},{4,12},{6,14},{8,0},{10,2},{12,4},{14,6},{1,9},{3,11}... | collective-permute-start | bytes 122888 | tf_op jit(solution)/shard_map/ppermute | solution.py:37
  108.6 2.0 %collective-permute-done.14 = bf16[160,128]{1,0:T(8,128)(2,1)S(1)} collective-permute-done((bf16[160,128]{1,0:T(8,128)(2,1)S(1)}, bf16[160,128]{1,0:T(8,128)(2,1)S(1)}, u32[]{:S(2)}, u32[]{:S(2)}) %collective-permute-start.14) | collective-permute-done | bytes 40992 | tf_op jit(solution)/shard_map/ppermute | solution.py:37
  110.7 0.3 collective-permute-start.15
  111.0 0.1 collective-permute-done.7
  111.1 2.6 %collective-permute-start.8 = (bf16[160,128]{1,0:T(8,128)(2,1)S(1)}, bf16[160,128]{1,0:T(8,128)(2,1)S(1)}, u32[]{:S(2)}, u32[]{:S(2)}) collective-permute-start(bf16[160,128]{1,0:T(8,128)(2,1)S(1)} %add_convert_fusion.1), channel_id=1, source_target_pairs={{0,8},{2,10},{4,12},{6,14},{8,0},{10,2},{12,4},{14,6},{1,9},{3,11}... | collective-permute-start | bytes 122888 | tf_op jit(solution)/shard_map/ppermute | solution.py:37
  113.7 1.9 %collective-permute-done.15 = bf16[160,128]{1,0:T(8,128)(2,1)S(1)} collective-permute-done((bf16[160,128]{1,0:T(8,128)(2,1)S(1)}, bf16[160,128]{1,0:T(8,128)(2,1)S(1)}, u32[]{:S(2)}, u32[]{:S(2)}) %collective-permute-start.15) | collective-permute-done | bytes 40992 | tf_op jit(solution)/shard_map/ppermute | solution.py:37
  115.7 0.4 collective-permute-start.16
  116.1 2.2 %collective-permute-start.9 = (bf16[320,128]{1,0:T(8,128)(2,1)S(1)}, bf16[320,128]{1,0:T(8,128)(2,1)S(1)}, u32[]{:S(2)}, u32[]{:S(2)}) collective-permute-start(bf16[320,128]{1,0:T(8,128)(2,1)S(1)} %maximum_select_fusion.4), channel_id=1, source_target_pairs={{0,4},{2,6},{4,0},{6,2},{8,12},{10,14},{12,8},{14,10},{1,5},{3,7},... | collective-permute-start | bytes 245768 | tf_op jit(solution)/shard_map/ppermute | solution.py:37
  118.4 1.8 %collective-permute-done.16 = bf16[320,128]{1,0:T(8,128)(2,1)S(1)} collective-permute-done((bf16[320,128]{1,0:T(8,128)(2,1)S(1)}, bf16[320,128]{1,0:T(8,128)(2,1)S(1)}, u32[]{:S(2)}, u32[]{:S(2)}) %collective-permute-start.16) | collective-permute-done | bytes 81952 | tf_op jit(solution)/shard_map/ppermute | solution.py:37
  120.2 0.2 collective-permute-start.17
  120.5 2.3 %collective-permute-start.2 = (f32[256,256]{1,0:T(8,128)S(1)}, f32[256,256]{1,0:T(8,128)S(1)}, u32[]{:S(2)}, u32[]{:S(2)}) collective-permute-start(f32[256,256]{1,0:T(8,128)S(1)} %get-tuple-element.81), channel_id=1, source_target_pairs={{0,2},{2,4},{4,6},{6,8},{8,10},{10,12},{12,14},{1,3},{3,5},{5,7},{... | collective-permute-start | bytes 786440 | tf_op jit(solution)/shard_map/ppermute | solution.py:81
  122.8 1.3 collective-permute-start.3
  124.1 3.7 %collective-permute-start.10 = (bf16[640,128]{1,0:T(8,128)(2,1)S(1)}, bf16[640,128]{1,0:T(8,128)(2,1)S(1)}, u32[]{:S(2)}, u32[]{:S(2)}) collective-permute-start(bf16[640,128]{1,0:T(8,128)(2,1)S(1)} %maximum_select_fusion.2), channel_id=1, source_target_pairs={{0,2},{2,0},{4,6},{6,4},{8,10},{10,8},{12,14},{14,12},{1,3},{3,1},... | collective-permute-start | bytes 491528 | tf_op jit(solution)/shard_map/ppermute | solution.py:37
  128.0 7.3 %collective-permute-done.10 = bf16[640,128]{1,0:T(8,128)(2,1)S(1)} collective-permute-done((bf16[640,128]{1,0:T(8,128)(2,1)S(1)}, bf16[640,128]{1,0:T(8,128)(2,1)S(1)}, u32[]{:S(2)}, u32[]{:S(2)}) %collective-permute-start.10) | collective-permute-done | bytes 163872 | tf_op jit(solution)/shard_map/ppermute | solution.py:37
  135.5 1.5 %shard_map.131 = bf16[128,4096]{1,0:T(8,128)(2,1)S(1)} custom-call(bf16[4,128,1024]{2,1,0:T(8,128)(2,1)S(1)} %copy-done.10), custom_call_target="tpu_custom_call" | custom-call | flops 1000000000 | bytes 4000000 | tf_op jit(solution)/shard_map/pallas_call | solution.py:90
  137.0 1.8 %copy.20 = bf16[4,32,4096]{2,0,1:T(4,128)(2,1)} copy(bf16[4,32,4096]{2,1,0:T(8,128)(2,1)S(1)} %bitcast.37) | data formatting | bytes 2097152 | tf_op jit(solution)/shard_map/reshape | solution.py:640
  138.8 0.6 slice.23
  139.3 0.6 slice.22
  139.9 1.4 shard_map.134
  141.3 0.8 copy.16
  142.1 2.1 %shard_map.135 = (f32[4096,128]{1,0:T(8,128)}, f32[2048,64]{1,0:T(8,128)}) custom-call(bf16[1280,128]{1,0:T(8,128)(2,1)S(1)} %maximum_select_fusion.own_a_ref, bf16[1280,128]{1,0:T(8,128)(2,1)S(1)} %maximum_select_fusion.1.own_b_ref, bf16[1280,128]{1,0:T(8,128)(2,1)S(1)} %collective-permute-done.18.other_a_ref, ...), custom_call_target="tpu_custom_call" | custom-call | flops 1000000000 | bytes 4000000 | tf_op jit(solution)/shard_map/pallas_call | solution.py:90
  (67 shorter events, 1.2 us)
Async XLA Ops:
  0.6 2.0 %copy-start.7 = (bf16[1,128,1,256]{3,1,2,0:T(8,128)(2,1)S(1)}, bf16[1,128,1,256]{3,1,2,0:T(8,128)(2,1)}, u32[]{:S(2)}) copy-start(bf16[1,128,1,256]{3,1,2,0:T(8,128)(2,1)} %param.8) | copy-start | bytes 196612
  0.6 8.3 %copy-start.11 = (bf16[64,32,64]{2,1,0:T(8,128)(2,1)S(1)}, bf16[64,32,64]{2,1,0:T(8,128)(2,1)}, u32[]{:S(2)}) copy-start(bf16[64,32,64]{2,1,0:T(8,128)(2,1)} %param.12) | copy-start | bytes 786436
  0.7 8.3 %copy-start.13 = (f32[64]{0:T(128)S(1)}, f32[64]{0:T(128)}, u32[]{:S(2)}) copy-start(f32[64]{0:T(128)} %param.10) | copy-start | bytes 772
  0.7 8.3 %copy-start.14 = (f32[64]{0:T(128)S(1)}, f32[64]{0:T(128)}, u32[]{:S(2)}) copy-start(f32[64]{0:T(128)} %param.11) | copy-start | bytes 772
  0.7 8.3 %copy-start.15 = (f32[32]{0:T(128)S(1)}, f32[32]{0:T(128)}, u32[]{:S(2)}) copy-start(f32[32]{0:T(128)} %param.13) | copy-start | bytes 388
  0.7 8.3 %copy-start.16 = (f32[32]{0:T(128)S(1)}, f32[32]{0:T(128)}, u32[]{:S(2)}) copy-start(f32[32]{0:T(128)} %param.14) | copy-start | bytes 388
  0.7 8.3 %copy-start.8 = (bf16[64,64,128]{2,1,0:T(8,128)(2,1)S(1)}, bf16[64,64,128]{2,1,0:T(8,128)(2,1)}, u32[]{:S(2)}) copy-start(bf16[64,64,128]{2,1,0:T(8,128)(2,1)} %param.9) | copy-start | bytes 3145732
  2.7 18.9 %collective-permute-start = (bf16[40,4096]{1,0:T(8,128)(2,1)S(1)}, bf16[40,4096]{1,0:T(8,128)(2,1)S(1)}, u32[]{:S(2)}, u32[]{:S(2)}) collective-permute-start(bf16[40,4096]{1,0:T(8,128)(2,1)S(1)} %get-tuple-element.83), channel_id=1, source_target_pairs={{0,2},{2,4},{4,6},{6,8},{8,10},{10,12},{12,14},{1,3},{3,5},{5,7},{... | collective-permute-start | bytes 983048 | tf_op jit(solution)/shard_map/ppermute | solution.py:81
  7.6 14.0 %collective-permute-start.1 = (bf16[40,4096]{1,0:T(8,128)(2,1)S(1)}, bf16[40,4096]{1,0:T(8,128)(2,1)S(1)}, u32[]{:S(2)}, u32[]{:S(2)}) collective-permute-start(bf16[40,4096]{1,0:T(8,128)(2,1)S(1)} %get-tuple-element.82), channel_id=1, source_target_pairs={{2,0},{4,2},{6,4},{8,6},{10,8},{12,10},{14,12},{3,1},{5,3},{7,5},{... | collective-permute-start | bytes 983048 | tf_op jit(solution)/shard_map/ppermute | solution.py:86
  59.4 1.0 copy-start.9
  75.7 12.1 %copy-start.5 = (f32[2,256,256]{2,1,0:T(8,128)}, f32[2,256,256]{2,1,0:T(8,128)S(1)}, u32[]{:S(2)}) copy-start(f32[2,256,256]{2,1,0:T(8,128)S(1)} %get-tuple-element.57.g1_ref) | copy-start | bytes 1572868
  87.9 1.0 copy-start
  88.9 0.8 copy-start.2
  89.7 0.8 copy-start.4
  90.5 0.7 copy-start.12
  91.3 2.1 %collective-permute-start.11 = (bf16[1280,128]{1,0:T(8,128)(2,1)}, bf16[1280,128]{1,0:T(8,128)(2,1)}, u32[]{:S(2)}, u32[]{:S(2)}) collective-permute-start(bf16[1280,128]{1,0:T(8,128)(2,1)} %get-tuple-element.66), channel_id=1, source_target_pairs={{0,1},{1,0},{2,3},{3,2},{4,5},{5,4},{6,7},{7,6},{8,9},{9,8},{10,11... | collective-permute-start | bytes 983048 | tf_op jit(solution)/shard_map/ppermute | solution.py:37
  91.3 3.4 %copy-start.3 = (f32[1280,128]{1,0:T(8,128)S(1)}, f32[1280,128]{1,0:T(8,128)}, u32[]{:S(2)}) copy-start(f32[1280,128]{1,0:T(8,128)} %copy-done.2) | copy-start | bytes 1966084
  91.3 3.4 %collective-permute-start.4 = (bf16[1280,128]{1,0:T(8,128)(2,1)}, bf16[1280,128]{1,0:T(8,128)(2,1)S(1)}, u32[]{:S(2)}, u32[]{:S(2)}) collective-permute-start(bf16[1280,128]{1,0:T(8,128)(2,1)} %copy-done.12), channel_id=1, source_target_pairs={{0,1},{1,0},{2,3},{3,2},{4,5},{5,4},{6,7},{7,6},{8,9},{9,8},{10,11... | collective-permute-start | bytes 983048 | tf_op jit(solution)/shard_map/ppermute | solution.py:37
  94.6 6.3 %collective-permute-start.12 = (bf16[640,128]{1,0:T(8,128)(2,1)S(1)}, bf16[640,128]{1,0:T(8,128)(2,1)S(1)}, u32[]{:S(2)}, u32[]{:S(2)}) collective-permute-start(bf16[640,128]{1,0:T(8,128)(2,1)S(1)} %dynamic-slice_convert_fusion), channel_id=1, source_target_pairs={{0,4},{2,6},{4,0},{6,2},{8,12},{10,14},{12,8},{14,10},{1,5},{3,7},... | collective-permute-start | bytes 491528 | tf_op jit(solution)/shard_map/ppermute | solution.py:37
  94.8 25.7 %copy-start.6 = (f32[2,256,256]{2,1,0:T(8,128)S(1)}, f32[2,256,256]{2,1,0:T(8,128)}, u32[]{:S(2)}) copy-start(f32[2,256,256]{2,1,0:T(8,128)} %copy-done.5) | copy-start | bytes 1572868
  94.8 6.3 %collective-permute-start.5 = (bf16[640,128]{1,0:T(8,128)(2,1)S(1)}, bf16[640,128]{1,0:T(8,128)(2,1)S(1)}, u32[]{:S(2)}, u32[]{:S(2)}) collective-permute-start(bf16[640,128]{1,0:T(8,128)(2,1)S(1)} %dynamic-slice_convert_fusion.1), channel_id=1, source_target_pairs={{0,2},{2,0},{4,6},{6,4},{8,10},{10,8},{12,14},{14,12},{1,3},{3,1},... | collective-permute-start | bytes 491528 | tf_op jit(solution)/shard_map/ppermute | solution.py:37
  101.0 4.5 %collective-permute-start.13 = (bf16[320,128]{1,0:T(8,128)(2,1)S(1)}, bf16[320,128]{1,0:T(8,128)(2,1)S(1)}, u32[]{:S(2)}, u32[]{:S(2)}) collective-permute-start(bf16[320,128]{1,0:T(8,128)(2,1)S(1)} %dynamic-slice_convert_fusion.2), channel_id=1, source_target_pairs={{0,2},{2,0},{4,6},{6,4},{8,10},{10,8},{12,14},{14,12},{1,3},{3,1},... | collective-permute-start | bytes 245768 | tf_op jit(solution)/shard_map/ppermute | solution.py:37
  101.2 34.3 %copy-start.10 = (bf16[4,128,1024]{2,1,0:T(8,128)(2,1)S(1)}, bf16[4,128,1024]{2,1,0:T(8,128)(2,1)}, u32[]{:S(2)}) copy-start(bf16[4,128,1024]{2,1,0:T(8,128)(2,1)} %copy-done.9) | copy-start | bytes 3145732
  101.2 4.5 %collective-permute-start.6 = (bf16[320,128]{1,0:T(8,128)(2,1)S(1)}, bf16[320,128]{1,0:T(8,128)(2,1)S(1)}, u32[]{:S(2)}, u32[]{:S(2)}) collective-permute-start(bf16[320,128]{1,0:T(8,128)(2,1)S(1)} %dynamic-slice_convert_fusion.3), channel_id=1, source_target_pairs={{0,4},{2,6},{4,0},{6,2},{8,12},{10,14},{12,8},{14,10},{1,5},{3,7},... | collective-permute-start | bytes 245768 | tf_op jit(solution)/shard_map/ppermute | solution.py:37
  105.5 5.1 %collective-permute-start.14 = (bf16[160,128]{1,0:T(8,128)(2,1)S(1)}, bf16[160,128]{1,0:T(8,128)(2,1)S(1)}, u32[]{:S(2)}, u32[]{:S(2)}) collective-permute-start(bf16[160,128]{1,0:T(8,128)(2,1)S(1)} %dynamic-slice_convert_fusion.4), channel_id=1, source_target_pairs={{0,8},{2,10},{4,12},{6,14},{8,0},{10,2},{12,4},{14,6},{1,9},{3,11}... | collective-permute-start | bytes 122888 | tf_op jit(solution)/shard_map/ppermute | solution.py:37
  105.8 5.3 %collective-permute-start.7 = (bf16[160,128]{1,0:T(8,128)(2,1)S(1)}, bf16[160,128]{1,0:T(8,128)(2,1)S(1)}, u32[]{:S(2)}, u32[]{:S(2)}) collective-permute-start(bf16[160,128]{1,0:T(8,128)(2,1)S(1)} %dynamic-slice_convert_fusion.5), channel_id=1, source_target_pairs={{0,8},{2,10},{4,12},{6,14},{8,0},{10,2},{12,4},{14,6},{1,9},{3,11}... | collective-permute-start | bytes 122888 | tf_op jit(solution)/shard_map/ppermute | solution.py:37
  110.7 5.0 %collective-permute-start.15 = (bf16[160,128]{1,0:T(8,128)(2,1)S(1)}, bf16[160,128]{1,0:T(8,128)(2,1)S(1)}, u32[]{:S(2)}, u32[]{:S(2)}) collective-permute-start(bf16[160,128]{1,0:T(8,128)(2,1)S(1)} %add_convert_fusion), channel_id=1, source_target_pairs={{0,8},{2,10},{4,12},{6,14},{8,0},{10,2},{12,4},{14,6},{1,9},{3,11}... | collective-permute-start | bytes 122888 | tf_op jit(solution)/shard_map/ppermute | solution.py:37
  111.1 5.0 %collective-permute-start.8 = (bf16[160,128]{1,0:T(8,128)(2,1)S(1)}, bf16[160,128]{1,0:T(8,128)(2,1)S(1)}, u32[]{:S(2)}, u32[]{:S(2)}) collective-permute-start(bf16[160,128]{1,0:T(8,128)(2,1)S(1)} %add_convert_fusion.1), channel_id=1, source_target_pairs={{0,8},{2,10},{4,12},{6,14},{8,0},{10,2},{12,4},{14,6},{1,9},{3,11}... | collective-permute-start | bytes 122888 | tf_op jit(solution)/shard_map/ppermute | solution.py:37
  115.7 4.5 %collective-permute-start.16 = (bf16[320,128]{1,0:T(8,128)(2,1)S(1)}, bf16[320,128]{1,0:T(8,128)(2,1)S(1)}, u32[]{:S(2)}, u32[]{:S(2)}) collective-permute-start(bf16[320,128]{1,0:T(8,128)(2,1)S(1)} %maximum_select_fusion.5), channel_id=1, source_target_pairs={{0,2},{2,0},{4,6},{6,4},{8,10},{10,8},{12,14},{14,12},{1,3},{3,1},... | collective-permute-start | bytes 245768 | tf_op jit(solution)/shard_map/ppermute | solution.py:37
  116.1 7.9 %collective-permute-start.9 = (bf16[320,128]{1,0:T(8,128)(2,1)S(1)}, bf16[320,128]{1,0:T(8,128)(2,1)S(1)}, u32[]{:S(2)}, u32[]{:S(2)}) collective-permute-start(bf16[320,128]{1,0:T(8,128)(2,1)S(1)} %maximum_select_fusion.4), channel_id=1, source_target_pairs={{0,4},{2,6},{4,0},{6,2},{8,12},{10,14},{12,8},{14,10},{1,5},{3,7},... | collective-permute-start | bytes 245768 | tf_op jit(solution)/shard_map/ppermute | solution.py:37
  120.2 7.6 %collective-permute-start.17 = (bf16[640,128]{1,0:T(8,128)(2,1)S(1)}, bf16[640,128]{1,0:T(8,128)(2,1)S(1)}, u32[]{:S(2)}, u32[]{:S(2)}) collective-permute-start(bf16[640,128]{1,0:T(8,128)(2,1)S(1)} %maximum_select_fusion.3), channel_id=1, source_target_pairs={{0,4},{2,6},{4,0},{6,2},{8,12},{10,14},{12,8},{14,10},{1,5},{3,7},... | collective-permute-start | bytes 491528 | tf_op jit(solution)/shard_map/ppermute | solution.py:37
  120.5 19.5 %collective-permute-start.2 = (f32[256,256]{1,0:T(8,128)S(1)}, f32[256,256]{1,0:T(8,128)S(1)}, u32[]{:S(2)}, u32[]{:S(2)}) collective-permute-start(f32[256,256]{1,0:T(8,128)S(1)} %get-tuple-element.81), channel_id=1, source_target_pairs={{0,2},{2,4},{4,6},{6,8},{8,10},{10,12},{12,14},{1,3},{3,5},{5,7},{... | collective-permute-start | bytes 786440 | tf_op jit(solution)/shard_map/ppermute | solution.py:81
  122.8 17.2 %collective-permute-start.3 = (f32[256,256]{1,0:T(8,128)S(1)}, f32[256,256]{1,0:T(8,128)S(1)}, u32[]{:S(2)}, u32[]{:S(2)}) collective-permute-start(f32[256,256]{1,0:T(8,128)S(1)} %get-tuple-element.80), channel_id=1, source_target_pairs={{2,0},{4,2},{6,4},{8,6},{10,8},{12,10},{14,12},{3,1},{5,3},{7,5},{... | collective-permute-start | bytes 786440 | tf_op jit(solution)/shard_map/ppermute | solution.py:86
  124.1 11.2 %collective-permute-start.10 = (bf16[640,128]{1,0:T(8,128)(2,1)S(1)}, bf16[640,128]{1,0:T(8,128)(2,1)S(1)}, u32[]{:S(2)}, u32[]{:S(2)}) collective-permute-start(bf16[640,128]{1,0:T(8,128)(2,1)S(1)} %maximum_select_fusion.2), channel_id=1, source_target_pairs={{0,2},{2,0},{4,6},{6,4},{8,10},{10,8},{12,14},{14,12},{1,3},{3,1},... | collective-permute-start | bytes 491528 | tf_op jit(solution)/shard_map/ppermute | solution.py:37
  127.9 14.2 %collective-permute-start.19 = (bf16[1280,128]{1,0:T(8,128)(2,1)S(1)}, bf16[1280,128]{1,0:T(8,128)(2,1)S(1)}, u32[]{:S(2)}, u32[]{:S(2)}) collective-permute-start(bf16[1280,128]{1,0:T(8,128)(2,1)S(1)} %maximum_select_fusion.1.own_b_ref), channel_id=1, source_target_pairs={{0,1},{1,0},{2,3},{3,2},{4,5},{5,4},{6,7},{7,6},{8,9},{9,8},{10,11... | collective-permute-start | bytes 983048 | tf_op jit(solution)/shard_map/ppermute | solution.py:37
  135.4 6.7 %collective-permute-start.18 = (bf16[1280,128]{1,0:T(8,128)(2,1)S(1)}, bf16[1280,128]{1,0:T(8,128)(2,1)S(1)}, u32[]{:S(2)}, u32[]{:S(2)}) collective-permute-start(bf16[1280,128]{1,0:T(8,128)(2,1)S(1)} %maximum_select_fusion.own_a_ref), channel_id=1, source_target_pairs={{0,1},{1,0},{2,3},{3,2},{4,5},{5,4},{6,7},{7,6},{8,9},{9,8},{10,11... | collective-permute-start | bytes 983048 | tf_op jit(solution)/shard_map/ppermute | solution.py:37
  135.5 4.4 %copy-start.1 = (bf16[2048,256]{1,0:T(8,128)(2,1)S(1)}, bf16[2048,256]{1,0:T(8,128)(2,1)}, u32[]{:S(2)}) copy-start(bf16[2048,256]{1,0:T(8,128)(2,1)} %copy-done) | copy-start | bytes 3145732

commit v2 on v1

--- a/solution.py
+++ b/solution.py
@@ -62,36 +62,37 @@
     )
 
 
-def space_sums(parts):
-    orders = chunk_steps()
-    for step in range(len(orders[0])):
-        parts = [halve(part, *order[step]) for part, order in zip(parts, orders)]
-    parts = [part.astype(BF16) for part in parts]
-    for step in reversed(range(len(orders[0]))):
-        parts = [double(part, *order[step]) for part, order in zip(parts, orders)]
-    return parts
-
-
 def exchange(copies):
     return lax.all_to_all(copies, GROUP, 0, 0)
 
 
-def to_above(block):
+def is_even():
+    return lax.axis_index("space") % 2 == 0
+
+
+def swap_inner(block):
+    return swap(block, "space", 1)
+
+
+def swap_outer(block):
     count = lax.axis_size("space")
-    return lax.ppermute(block, "space", [(i, i + 1) for i in range(count - 1)])
-
-
-def to_below(block):
-    count = lax.axis_size("space")
-    return lax.ppermute(block, "space", [(i + 1, i) for i in range(count - 1)])
-
-
-def call(kernel, outs, args, scratch=()):
+    pairs = [(i, i + 1) for i in range(1, count - 1, 2)]
+    return lax.ppermute(block, "space", pairs + [(j, i) for i, j in pairs])
+
+
+def hold(*values):
+    return lax.optimization_barrier(values)
+
+
+def call(kernel, outs, args, scratch=(), far=(), far_args=()):
+    def spec(away):
+        return pl.BlockSpec(memory_space=pl.ANY if away else pltpu.VMEM)
+
     return pl.pallas_call(
         kernel,
         out_shape=[jax.ShapeDtypeStruct(shape, dtype) for shape, dtype in outs],
-        in_specs=[pl.BlockSpec(memory_space=pltpu.VMEM)] * len(args),
-        out_specs=[pl.BlockSpec(memory_space=pltpu.VMEM)] * len(outs),
+        in_specs=[spec(k in far_args) for k in range(len(args))],
+        out_specs=[spec(k in far) for k in range(len(outs))],
         scratch_shapes=list(scratch),
         compiler_params=pltpu.CompilerParams(vmem_limit_bytes=24 * 2**20),
         cost_estimate=pl.CostEstimate(flops=10**9, bytes_accessed=4 * 10**6, transcendentals=0),
@@ -159,8 +160,7 @@
     return 1.0 / (1.0 + jnp.exp(-values))
 
 
-def spread_planes(cot_ref, out_ref, planes):
-    matrix = spread_matrix()
+def spread_planes(cot_ref, out_ref, planes, matrix):
     for rp in range(2):
         for rp2 in range(2):
             for h in range(2):
@@ -181,9 +181,32 @@
 
 
 def prepare_kernel(
-    w1_ref, w2_ref, gain1_ref, shift1_ref, gain2_ref, shift2_ref, cot_ref,
-    a1_ref, a2_ref, b1_ref, b2_ref, sh_ref, p1_ref, p2_ref, spread_ref,
+    w1_far, w2_far, gain1_far, shift1_far, gain2_far, shift2_far, cot_ref,
+    a1_ref, a2_ref, b1_ref, b2_ref, sh_ref, p1_ref, p2_ref, spread_ref, matrix_ref,
+    w1_ref, w2_ref, gain1_ref, shift1_ref, gain2_ref, shift2_ref, sem,
 ):
+    copies = [
+        pltpu.make_async_copy(far, near, sem.at[k])
+        for k, (far, near) in enumerate(
+            (
+                (w1_far, w1_ref),
+                (w2_far, w2_ref),
+                (gain1_far, gain1_ref),
+                (shift1_far, shift1_ref),
+                (gain2_far, gain2_ref),
+                (shift2_far, shift2_ref),
+            )
+        )
+    ]
+    for copy in copies:
+        copy.start()
+    matrix_ref[...] = spread_matrix()
+    spread_planes(cot_ref, spread_ref, range(4), matrix_ref[...])
+    for dj in (-1, 0, 1):
+        for dl in (-1, 0, 1):
+            sh_ref[:, shift_slot(dj, dl)] = shift_matrix(dj, dl)
+    for copy in copies:
+        copy.wait()
     place = lax.axis_index("space")
     below = jnp.where(place > 0, 1.0, 0.0)
     above = jnp.where(place < lax.axis_size("space") - 1, 1.0, 0.0)
@@ -195,10 +218,6 @@
     p2_ref[...] = jnp.concatenate(
         [jnp.concatenate([ref[...]] * 4, axis=1) for ref in (gain2_ref, shift2_ref)] + edges + blank
     )
-    spread_planes(cot_ref, spread_ref, range(4))
-    for dj in (-1, 0, 1):
-        for dl in (-1, 0, 1):
-            sh_ref[:, shift_slot(dj, dl)] = shift_matrix(dj, dl)
     a1_ref[...] = jnp.zeros(a1_ref.shape, BF16)
     for par in range(2):
         for rp in range(2):
@@ -237,19 +256,12 @@
         )
 
 
-def halo_latent(halo_ref):
-    rows = halo_ref[C2 : C2 + 8, :].astype(F32)
-    return jnp.concatenate(
-        [rows[:, m * CELLS : (m + 1) * CELLS] for m in range(C0 // 8)], axis=0
-    ).astype(BF16)
-
-
 def first_kernel(
-    lat_ref, below_ref, above_ref, a1_ref, sh_ref,
-    pre_ref, out_ref, spread_ref, near_ref, x_ref,
+    lat_ref, inner_ref, outer_ref, a1_ref, sh_ref, pre_ref, out_ref, near_ref, x_ref
 ):
-    near_ref[0] = halo_latent(below_ref)
-    near_ref[1] = halo_latent(above_ref)
+    even = is_even()
+    near_ref[0] = jnp.where(even, outer_ref[...], inner_ref[...])
+    near_ref[1] = jnp.where(even, inner_ref[...], outer_ref[...])
     planes = jnp.concatenate([near_ref[0], lat_ref[...], near_ref[1]], axis=0)
     for k in range(9):
         moved = matmul(planes, sh_ref[:, k * CELLS : (k + 1) * CELLS]).astype(BF16)
@@ -267,8 +279,6 @@
     lower, upper = lower - wide, upper - wide
     squares = fold(jnp.sum(lower * lower + upper * upper, axis=1, keepdims=True), C1)
     emit_rows(out_ref, mean, squares)
-    spread_planes(below_ref, spread_ref, (0,))
-    spread_planes(above_ref, spread_ref, (1,))
 
 
 def second_kernel(got_ref, pre1_ref, p1_ref, a2_ref, sh_ref, pre_ref, act_ref, st_ref, out_ref, x_ref):
@@ -349,7 +359,14 @@
                     out_ref[:, at : at + 256] = moved[:, jj * 256 : (jj + 1) * 256]
 
 
-def third_kernel(got_ref, pre_ref, cot_ref, edge_ref, p2_ref, grad_ref, feat_ref, st_ref, out_ref):
+def third_kernel(
+    got_ref, pre_ref, cot_ref, inner_ref, outer_ref, matrix_ref, p2_ref,
+    grad_ref, feat_far, st_ref, out_ref, rows_ref, edge_ref, feat_ref, sem,
+):
+    even = is_even()
+    rows_ref[0:C2] = jnp.where(even, outer_ref[...], inner_ref[...])
+    rows_ref[C2:] = jnp.where(even, inner_ref[...], outer_ref[...])
+    spread_planes(rows_ref, edge_ref, range(2), matrix_ref[...])
     mean, scale = moments(got_ref[...], 64 * CELLS)
     st = jnp.concatenate([mean, scale, p2_ref[0:6]], axis=0)
     st_ref[...] = st
@@ -364,6 +381,22 @@
         grad_ref[t, :, pl.ds(lane, CELLS)] = grad
         return hat, norm, gate, grad
 
+    first = jnp.zeros((4 * C2, CELLS), F32)
+    second = jnp.zeros((4 * C2, CELLS), F32)
+    copies = []
+    for t in range(1, 5):
+
+        def body(block, carry):
+            lane = pl.multiple_of(block * CELLS, CELLS)
+            hat, norm, gate, grad = slope(t, lane, cot_ref[t - 1, :, pl.ds(lane, CELLS)])
+            feat_ref[t - 1, :, pl.ds(lane, CELLS)] = (norm * gate).astype(BF16)
+            return carry[0] + grad * hat, carry[1] + grad
+
+        first, second = lax.fori_loop(0, 4, body, (first, second))
+        copies.append(
+            pltpu.make_async_copy(feat_ref.at[t - 1], feat_far.at[t - 1], sem.at[t - 1])
+        )
+        copies[-1].start()
     for k in range(2):
 
         @pl.loop(0, 4)
@@ -371,20 +404,13 @@
             lane = pl.multiple_of(block * CELLS, CELLS)
             slope(5 * k, lane, edge_ref[k, :, pl.ds(lane, CELLS)])
 
-    def body(k, carry):
-        t = k // 4 + 1
-        lane = pl.multiple_of((k % 4) * CELLS, CELLS)
-        hat, norm, gate, grad = slope(t, lane, cot_ref[t - 1, :, pl.ds(lane, CELLS)])
-        feat_ref[t - 1, :, pl.ds(lane, CELLS)] = (norm * gate).astype(BF16)
-        return carry[0] + grad * hat, carry[1] + grad
-
-    zero = jnp.zeros((4 * C2, CELLS), F32)
-    first, second = lax.fori_loop(0, 16, body, (zero, zero))
     emit_rows(
         out_ref,
         fold(jnp.sum(first, axis=1, keepdims=True), C2),
         fold(jnp.sum(second, axis=1, keepdims=True), C2),
     )
+    for copy in copies:
+        copy.wait()
 
 
 def fourth_kernel(
@@ -454,20 +480,17 @@
         )
 
 
-def first_dpre(grad, pre, cols, keep):
+def first_dpre(grad, pre, cols):
     mean, scale, gain = (cols[0:C1, k : k + 1] for k in range(3))
     hat_part, part = cols[0:C1, 6:7], cols[0:C1, 7:8]
-    factor = gain * scale
-    if keep is not None:
-        factor = factor * keep
-    return (factor * (grad - part - (pre - mean) * scale * hat_part)).astype(BF16)
-
-
-def first_windows(x_ref, base, grad_ref, pre_ref, cols, keep, sh_ref):
+    return (gain * scale * (grad - part - (pre - mean) * scale * hat_part)).astype(BF16)
+
+
+def first_windows(x_ref, base, grad_ref, pre_ref, cols, sh_ref):
     for block in range(4):
         rp, cp = block // 2, block % 2
         rows = slice(block * C1, (block + 1) * C1)
-        dpre = first_dpre(grad_ref[rows, :].astype(F32), pre_ref[rows, :], cols, keep)
+        dpre = first_dpre(grad_ref[rows, :], pre_ref[rows, :], cols)
         for q, (trp, dj) in enumerate(TAP_PHASES):
             for r, (tcp, dl) in enumerate(TAP_PHASES):
                 if (trp, tcp) != (rp, cp):
@@ -480,17 +503,16 @@
 
 
 def fifth_kernel(
-    got_ref, g1_ref, pre1_ref, st1_ref, sh_ref, lat_ref, near_ref, dw2_ref,
-    keep_a_ref, keep_b_ref, send_a_ref, send_b_ref, sum_ref, x_ref, dw_ref,
+    got_ref, g1_ref, pre1_ref, st1_ref, sh_ref, lat_ref, near_ref, dw2_ref, b1_ref,
+    keep_a_ref, keep_b_ref, send_a_ref, send_b_ref, sum_ref, mid_ref, inner_ref, outer_ref,
+    x_ref, dw_ref, out_ref, sem,
 ):
     sums = jnp.sum(got_ref[...], axis=0)
     sum_ref[...] = sums
     total = got_ref.shape[0] * 8 * CELLS
     cols = columns(jnp.concatenate([st1_ref[0:6], sums[0:2] / total], axis=0))
     for j in range(2):
-        first_windows(
-            x_ref, j * 16 * C1, g1_ref.at[j], pre1_ref.at[j + 1], cols, None, sh_ref
-        )
+        first_windows(x_ref, j * 16 * C1, g1_ref.at[j], pre1_ref.at[j + 1], cols, sh_ref)
     fields = (near_ref[1], lat_ref[...], lat_ref[...], near_ref[0])
     for p, j, field in ((0, 1, fields[0]), (1, 0, fields[1]), (2, 1, fields[2]), (3, 0, fields[3])):
         for half in range(2):
@@ -502,10 +524,26 @@
     core = lax.axis_index("rep")
     mine = pl.multiple_of(core * (2 * chunk), 2 * chunk)
     theirs = pl.multiple_of((1 - core) * (2 * chunk), 2 * chunk)
-    keep_a_ref[...] = dw_ref[pl.ds(mine, chunk), :]
-    keep_b_ref[...] = dw_ref[pl.ds(mine + chunk, chunk), :]
-    send_a_ref[...] = dw_ref[pl.ds(theirs, chunk), :].astype(BF16)
-    send_b_ref[...] = dw_ref[pl.ds(theirs + chunk, chunk), :].astype(BF16)
+    out_ref[...] = dw_ref[pl.ds(theirs, 2 * chunk), :].astype(BF16)
+    copies = [
+        pltpu.make_async_copy(out_ref.at[0:chunk], send_a_ref, sem.at[0]),
+        pltpu.make_async_copy(out_ref.at[chunk:], send_b_ref, sem.at[1]),
+        pltpu.make_async_copy(dw_ref.at[pl.ds(mine, chunk)], keep_a_ref, sem.at[2]),
+        pltpu.make_async_copy(dw_ref.at[pl.ds(mine + chunk, chunk)], keep_b_ref, sem.at[3]),
+    ]
+    for copy in copies:
+        copy.start()
+    pieces = [
+        matmul(b1_ref[:, p * 16 * C1 : (p + 1) * 16 * C1], x_ref[j * 16 * C1 : (j + 1) * 16 * C1, :])
+        for p, j in ((0, 1), (1, 0), (2, 1), (3, 0))
+    ]
+    mid_ref[...] = pieces[1] + pieces[2]
+    up, down = pieces[0].astype(BF16), pieces[3].astype(BF16)
+    even = is_even()
+    inner_ref[...] = jnp.where(even, up, down)
+    outer_ref[...] = jnp.where(even, down, up)
+    for copy in copies:
+        copy.wait()
 
 
 def last_kernel(own_a_ref, own_b_ref, other_a_ref, other_b_ref, dw1_ref, dw2_ref, x_ref):
@@ -520,19 +558,6 @@
     dw1_ref[...] = x_ref[0 : 64 * C1, :]
     dw2_ref[0 : 32 * C2, :] = x_ref[64 * C1 :, 0:C1]
     dw2_ref[32 * C2 :, :] = x_ref[64 * C1 :, C1:]
-
-
-def sixth_kernel(
-    sum_ref, low_ref, high_ref, pre1_ref, st1_ref, sh_ref, b1_ref, own_ref, count_ref, out_ref, x_ref
-):
-    total = count_ref.shape[0] * 8 * CELLS
-    cols = columns(jnp.concatenate([st1_ref[0:6], sum_ref[0:2] / total], axis=0))
-    keeps = (cols[0:C1, 4:5], cols[0:C1, 5:6])
-    first_windows(x_ref, 0, low_ref, pre1_ref.at[0], cols, keeps[0], sh_ref)
-    first_windows(x_ref, 16 * C1, high_ref, pre1_ref.at[3], cols, keeps[1], sh_ref)
-    grad = matmul(b1_ref[:, 0 : 16 * C1], x_ref[0 : 16 * C1, :])
-    grad = grad + matmul(b1_ref[:, 16 * C1 : 48 * C1], own_ref[...])
-    out_ref[...] = grad + matmul(b1_ref[:, 48 * C1 : 64 * C1], x_ref[16 * C1 : 32 * C1, :])
 
 
 def local(
@@ -548,13 +573,15 @@
     count = group_size()
     lat = latent.reshape(C0, CELLS)
     cot = cotangent.reshape(C2, 4, 16 * CELLS)
-    low = lat.reshape(C0 // 8, 8, CELLS).transpose(1, 0, 2).reshape(8, 16 * CELLS)
-    below = to_above(jnp.concatenate([cot[:, 3], low]))
-    above = to_below(jnp.concatenate([cot[:, 0], low]))
+    top, bottom = cot[:, 3], cot[:, 0]
+    lat_inner = swap_inner(lat)
+    lat_outer = swap_outer(lat)
+    cot_inner = swap_inner(jnp.where(is_even(), top, bottom))
+    cot_outer = swap_outer(jnp.where(is_even(), bottom, top))
     planes = cot.transpose(1, 0, 2).reshape(4 * C2, 16 * CELLS)
     w1 = first_weight.reshape(64 * C1, C0)
     w2 = second_weight.reshape(64 * C2, C1)
-    a1, a2, b1, b2, sh, p1, p2, spread = call(
+    a1, a2, b1, b2, sh, p1, p2, spread, matrix = call(
         prepare_kernel,
         [
             ((8 * C1, 18 * C0), BF16),
@@ -565,6 +592,7 @@
             ((8, 128), F32),
             ((8, 128), F32),
             ((4, 4 * C2, 4 * CELLS), BF16),
+            ((512, 512), BF16),
         ],
         [
             w1,
@@ -575,17 +603,26 @@
             second_norm_shift.reshape(1, C2),
             planes,
         ],
+        [
+            pltpu.VMEM((64 * C1, C0), BF16),
+            pltpu.VMEM((64 * C2, C1), BF16),
+            pltpu.VMEM((1, C1), F32),
+            pltpu.VMEM((1, C1), F32),
+            pltpu.VMEM((1, C2), F32),
+            pltpu.VMEM((1, C2), F32),
+            pltpu.SemaphoreType.DMA((6,)),
+        ],
+        far_args=range(6),
     )
     stats = ((count, 8, 128), F32)
-    pre1, out, edge, near = call(
+    pre1, out, near = call(
         first_kernel,
         [
             ((4, 4 * C1, CELLS), F32),
             stats,
-            ((2, 4 * C2, 4 * CELLS), BF16),
             ((2, C0, CELLS), BF16),
         ],
-        [lat, below, above, a1, sh],
+        [lat, lat_inner, lat_outer, a1, sh],
         [pltpu.VMEM((27 * C0, CELLS), BF16)],
     )
     got = exchange(out)
@@ -595,6 +632,7 @@
         [got, pre1, p1, a2, sh],
         [pltpu.VMEM((36 * C1, 4 * CELLS), BF16)],
     )
+    out, cot_inner, cot_outer = hold(out, cot_inner, cot_outer)
     got = exchange(out)
     grad2, feat, st2, out = call(
         third_kernel,
@@ -604,7 +642,14 @@
             ((8, 128), F32),
             stats,
         ],
-        [got, pre2, spread, edge, p2],
+        [got, pre2, spread, cot_inner, cot_outer, matrix, p2],
+        [
+            pltpu.VMEM((2 * C2, 16 * CELLS), BF16),
+            pltpu.VMEM((2, 4 * C2, 4 * CELLS), BF16),
+            pltpu.VMEM((4, 4 * C2, 4 * CELLS), BF16),
+            pltpu.SemaphoreType.DMA((4,)),
+        ],
+        far=(1,),
     )
     got = exchange(out)
     grad1, dw2, sum2, out = call(
@@ -613,11 +658,9 @@
         [got, pre2, grad2, st2, b2, sh, act, pre1, st1],
         [pltpu.VMEM((96 * C2, 4 * CELLS), BF16)],
     )
-    grad_below = to_above(grad1[1])
-    grad_above = to_below(grad1[0])
     got = exchange(out)
     rows = (64 * C1 + 32 * C2) // 4
-    keep_a, keep_b, send_a, send_b, sum1, windows = call(
+    keep_a, keep_b, send_a, send_b, sum1, mid, lat_in, lat_out = call(
         fifth_kernel,
         [
             ((rows, C0), F32),
@@ -625,25 +668,36 @@
             ((rows, C0), BF16),
             ((rows, C0), BF16),
             ((8, 128), F32),
-            ((32 * C1, CELLS), BF16),
+            ((C0, CELLS), F32),
+            ((C0, CELLS), BF16),
+            ((C0, CELLS), BF16),
         ],
-        [got, grad1, pre1, st1, sh, lat, near, dw2],
-        [pltpu.VMEM((4 * rows, C0), F32)],
-    )
-    (latent_grad,) = call(
-        sixth_kernel,
-        [((C0, CELLS), F32)],
-        [sum1, grad_below, grad_above, pre1, st1, sh, b1, windows, got],
-        [pltpu.VMEM((32 * C1, CELLS), BF16)],
-    )
-    (features,) = call(gather_kernel, [((4 * C2, 16 * CELLS), BF16)], [feat])
-    features = features.reshape(4, C2, 16 * CELLS).transpose(1, 0, 2)
-    part_a, part_b = space_sums(
+        [got, grad1, pre1, st1, sh, lat, near, dw2, b1],
         [
-            keep_a + swap(send_a, "rep", 1).astype(F32),
-            keep_b + swap(send_b, "rep", 1).astype(F32),
-        ]
-    )
+            pltpu.VMEM((32 * C1, CELLS), BF16),
+            pltpu.VMEM((4 * rows, C0), F32),
+            pltpu.VMEM((2 * rows, C0), BF16),
+            pltpu.SemaphoreType.DMA((4,)),
+        ],
+        far=range(4),
+    )
+    parts = [
+        keep_a + swap(send_a, "rep", 1).astype(F32),
+        keep_b + swap(send_b, "rep", 1).astype(F32),
+    ]
+    orders = chunk_steps()
+    steps = len(orders[0])
+    latent_grad = mid + swap_inner(lat_in).astype(F32) + swap_outer(lat_out).astype(F32)
+    for step in range(steps):
+        parts = [halve(part, *order[step]) for part, order in zip(parts, orders)]
+    parts = [part.astype(BF16) for part in parts]
+    for step in reversed(range(steps)):
+        if step == 0:
+            feat, *parts = hold(feat, *parts)
+            (features,) = call(gather_kernel, [((4 * C2, 16 * CELLS), BF16)], [feat])
+            features = features.reshape(4, C2, 16 * CELLS).transpose(1, 0, 2)
+        parts = [double(part, *order[step]) for part, order in zip(parts, orders)]
+    features, latent_grad, part_a, part_b = hold(features, latent_grad, *parts)
     first_weight_grad, second_weight_grad = call(
         last_kernel,
         [((64 * C1, C0), F32), ((64 * C2, C1), F32)],

time: 146 us -> 125 us (0.86); the launches traced: 144 us -> 125 us
  waiting for transfers between devices: 31.9 us -> 22.5 us
  local copies, waits for them, and re-layouts: 10.2 us -> 5.66 us
  starting transfers between devices: 25.6 us -> 21.5 us
    ppermute x4 -> x3, waiting for transfers between devices: 9.18 us -> 0.04 us  [swap_outer(): return lax.ppermute(block, 'space', pairs + [(j, i) for i, j in pairs])]
    ppermute x4 -> x3, starting transfers between devices: 9.76 us -> 1.97 us  [swap_outer(): return lax.ppermute(block, 'space', pairs + [(j, i) for i, j in pairs])]
    unnamed x36 -> x16, local copies, waits for them, and re-layouts: 7.14 us -> 2.63 us
    ppermute x16 -> x19, starting transfers between devices: 15.8 us -> 19.6 us  [swap(): lax.ppermute(block, axis, [(i, i ^ bit) for i in range(lax.axis_size(axis...]
    pallas_call x9 -> x8, Pallas kernels: 31.7 us -> 30.9 us  [call(): pl.pallas_call(kernel, out_shape=[jax.ShapeDtypeStruct(shape, dtype) for...]
    ppermute x16 -> x19, waiting for transfers between devices: 22.7 us -> 22.5 us  [swap(): lax.ppermute(block, axis, [(i, i ^ bit) for i in range(lax.axis_size(axis...]
  transfers between devices with their start and end apart: 20 -> 22, of which waited for: 10 -> 13; matrix products, arithmetic and copies ran while one was open for 4% -> 6% of each run, Pallas kernels for 4% -> 11%
where the time goes in v2:
time: 125 us
  blocking collectives  41.8 us (33%)
  Pallas kernels  30.9 us (25%)
  waiting for transfers between devices  22.5 us (18%)
  starting transfers between devices  21.5 us (17%)
  local copies, waits for them, and re-layouts  5.66 us (5%)
  other arithmetic  1.57 us (1%)
    all_to_all x4, blocking collectives, exchange(): return lax.all_to_all(copies, GROUP, 0, 0)  41.8 us
    pallas_call x8, Pallas kernels, call(): pl.pallas_call(kernel, out_shape=[jax.ShapeDtypeStruct(shape, dtype) for...  30.9 us
    ppermute x19, waiting for transfers between devices, swap(): lax.ppermute(block, axis, [(i, i ^ bit) for i in range(lax.axis_size(axis...  22.5 us
    ppermute x19, starting transfers between devices, swap(): lax.ppermute(block, axis, [(i, i ^ bit) for i in range(lax.axis_size(axis...  19.6 us
    unnamed x16, local copies, waits for them, and re-layouts  2.63 us
  transfers between devices with their start and end apart: 22, of which 13 were waited for; matrix products, arithmetic and copies ran while one was open for 6% of the time, Pallas kernels for 11%

profile of v2, /device:TPU:0, one launch (start us, length us, event | category | flops | bytes accessed | tf_op | source)
XLA Modules:
  0.0 125.1 jit_solution(9679190886147762962)
XLA Ops:
  0.7 3.0 %collective-permute-start = (bf16[128,256]{1,0:T(8,128)(2,1)}, bf16[128,256]{1,0:T(8,128)(2,1)S(1)}, u32[]{:S(2)}, u32[]{:S(2)}) collective-permute-start(bf16[128,256]{1,0:T(8,128)(2,1)} %bitcast.29), channel_id=1, source_target_pairs={{0,2},{2,0},{4,6},{6,4},{8,10},{10,8},{12,14},{14,12},{1,3},{3,1},... | collective-permute-start | bytes 196616 | tf_op jit(solution)/shard_map/ppermute | solution.py:37
  3.7 0.7 collective-permute-start.1
  4.4 1.8 %copy.21 = bf16[1,32,4,4096]{3,1,2,0:T(8,128)(2,1)S(1)} copy(bf16[1,32,4,4096]{3,2,1,0:T(4,128)(2,1)} %param.15) | data formatting | bytes 2097152 | tf_op args[7]
  6.3 4.3 %collective-permute-start.2 = (bf16[32,4096]{1,0:T(8,128)(2,1)S(1)}, bf16[32,4096]{1,0:T(8,128)(2,1)S(1)}, u32[]{:S(2)}, u32[]{:S(2)}) collective-permute-start(bf16[32,4096]{1,0:T(8,128)(2,1)S(1)} %get-tuple-element.101), channel_id=1, source_target_pairs={{0,2},{2,0},{4,6},{6,4},{8,10},{10,8},{12,14},{14,12},{1,3},{3,1},... | collective-permute-start | bytes 786440 | tf_op jit(solution)/shard_map/ppermute | solution.py:37
  10.6 0.7 collective-permute-start.3
  11.4 3.9 %shard_map.127 = (bf16[512,2304]{1,0:T(8,128)(2,1)S(1)}, bf16[256,1152]{1,0:T(8,128)(2,1)S(1)}, bf16[128,4096]{1,0:T(8,128)(2,1)S(1)}, bf16[64,2048]{1,0:T(8,128...) custom-call(bf16[4096,128]{1,0:T(8,128)(2,1)S(1)} %bitcast.33, ...), custom_call_target="tpu_custom_call" | custom-call | flops 1000000000 | bytes 4000000 | tf_op jit(solution)/shard_map/pallas_call | solution.py:91
  15.3 2.2 %shard_map.128 = (f32[4,256,256]{2,1,0:T(8,128)S(1)}, f32[16,8,128]{2,1,0:T(8,128)S(1)}, bf16[2,128,256]{2,1,0:T(8,128)(2,1)S(1)}) custom-call(bf16[128,256]{1,0:T(8,128)(2,1)S(1)} %bitcast.31, bf16[128,256]{1,0:T(8,128)(2,1)S(1)} %collective-permute-done.inner_ref, bf16[128,256]{1,0:T(8,128)(2,1)S(1)} %collective-permute-done.1.outer_ref, ...), custom_call_target="tpu_custom_call" | custom-call | flops 1000000000 | bytes 4000000 | tf_op jit(solution)/shard_map/pallas_call | solution.py:91
  17.5 13.4 %all_to_all.20.got_ref = f32[16,8,128]{2,1,0:T(8,128)S(1)} all-to-all(f32[16,8,128]{2,1,0:T(8,128)S(1)} %get-tuple-element.52), channel_id=1, replica_groups=mesh['group'=2,'space'=8,'rep'=2] {'space','rep'}, dimensions={0} | all-to-all | bytes 131072 | tf_op jit(solution)/shard_map/all_to_all | solution.py:66
  30.8 6.2 %shard_map.129 = (f32[6,128,1024]{2,1,0:T(8,128)S(1)}, bf16[2,64,1024]{2,1,0:T(8,128)(2,1)S(1)}, f32[8,128]{1,0:T(8,128)S(1)}, f32[16,8,128]{2,1,0:T(8,128)S(1)}) custom-call(f32[16,8,128]{2,1,0:T(8,128)S(1)} %all_to_all.20.got_ref, f32[4,256,256]{2,1,0:T(8,128)S(1)} %get-tuple-element.53.pre1_ref, f32[8,128]{1,0:T(8,128)S(1)} %get-tuple-element.54.p1_ref, ...), custom_call_target="tpu_custom_call" | custom-call | flops 1000000000 | bytes 4000000 | tf_op jit(solution)/shard_map/pallas_call | solution.py:91
  37.1 9.5 %all_to_all.21.got_ref = f32[16,8,128]{2,1,0:T(8,128)S(1)} all-to-all(f32[16,8,128]{2,1,0:T(8,128)S(1)} %get-tuple-element.57), channel_id=1, replica_groups=mesh['group'=2,'space'=8,'rep'=2] {'space','rep'}, dimensions={0} | all-to-all | bytes 131072 | tf_op jit(solution)/shard_map/all_to_all | solution.py:66
  46.6 6.1 %shard_map.130 = (f32[6,128,1024]{2,1,0:T(8,128)S(1)}, bf16[4,128,1024]{2,1,0:T(8,128)(2,1)S(1)}, f32[8,128]{1,0:T(8,128)S(1)}, f32[16,8,128]{2,1,0:T(8,128)S(1)}) custom-call(f32[16,8,128]{2,1,0:T(8,128)S(1)} %all_to_all.21.got_ref, f32[6,128,1024]{2,1,0:T(8,128)S(1)} %get-tuple-element.58.pre_ref, bf16[4,128,1024]{2,1,0:T(8,128)(2,1)S(1)} %get-tuple-element.59.cot_ref, ...), custom_call_target="tpu_custom_call" | custom-call | flops 1000000000 | bytes 4000000 | tf_op jit(solution)/shard_map/pallas_call | solution.py:91
  52.6 9.5 %all_to_all.22.got_ref = f32[16,8,128]{2,1,0:T(8,128)S(1)} all-to-all(f32[16,8,128]{2,1,0:T(8,128)S(1)} %get-tuple-element.65), channel_id=1, replica_groups=mesh['group'=2,'space'=8,'rep'=2] {'space','rep'}, dimensions={0} | all-to-all | bytes 131072 | tf_op jit(solution)/shard_map/all_to_all | solution.py:66
  62.1 6.0 %shard_map.131 = (f32[2,256,256]{2,1,0:T(8,128)S(1)}, f32[1024,128]{1,0:T(8,128)S(1)}, f32[8,128]{1,0:T(8,128)S(1)}, f32[16,8,128]{2,1,0:T(8,128)S(1)}) custom-call(f32[16,8,128]{2,1,0:T(8,128)S(1)} %all_to_all.22.got_ref, f32[6,128,1024]{2,1,0:T(8,128)S(1)} %get-tuple-element.58.pre_ref, f32[6,128,1024]{2,1,0:T(8,128)S(1)} %get-tuple-element.66.grad_ref, ...), custom_call_target="tpu_custom_call" | custom-call | flops 1000000000 | bytes 4000000 | tf_op jit(solution)/shard_map/pallas_call | solution.py:91
  68.2 9.5 %all_to_all.23.got_ref = f32[16,8,128]{2,1,0:T(8,128)S(1)} all-to-all(f32[16,8,128]{2,1,0:T(8,128)S(1)} %get-tuple-element.71), channel_id=1, replica_groups=mesh['group'=2,'space'=8,'rep'=2] {'space','rep'}, dimensions={0} | all-to-all | bytes 131072 | tf_op jit(solution)/shard_map/all_to_all | solution.py:66
  77.6 2.9 %shard_map.132 = (f32[1280,128]{1,0:T(8,128)S(1)}, f32[1280,128]{1,0:T(8,128)S(1)}, bf16[1280,128]{1,0:T(8,128)(2,1)S(1)}, bf16[1280,128]{1,0:T(8,128)(2,1)S(1)}...) custom-call(f32[16,8,128]{2,1,0:T(8,128)S(1)} %all_to_all.23.got_ref, ...), custom_call_target="tpu_custom_call" | custom-call | flops 1000000000 | bytes 4000000 | tf_op jit(solution)/shard_map/pallas_call | solution.py:91
  80.7 0.4 collective-permute-start.4
  81.2 0.7 collective-permute-start.17
  81.9 0.5 collective-permute-done.10
  82.3 1.0 convert_add_fusion
  83.4 4.2 %collective-permute-start.11 = (bf16[640,128]{1,0:T(8,128)(2,1)S(1)}, bf16[640,128]{1,0:T(8,128)(2,1)S(1)}, u32[]{:S(2)}, u32[]{:S(2)}) collective-permute-start(bf16[640,128]{1,0:T(8,128)(2,1)S(1)} %dynamic-slice_convert_fusion), channel_id=1, source_target_pairs={{0,4},{2,6},{4,0},{6,2},{8,12},{10,14},{12,8},{14,10},{1,5},{3,7},... | collective-permute-start | bytes 491528 | tf_op jit(solution)/shard_map/ppermute | solution.py:37
  87.8 4.4 %collective-permute-done.11 = bf16[640,128]{1,0:T(8,128)(2,1)S(1)} collective-permute-done((bf16[640,128]{1,0:T(8,128)(2,1)S(1)}, bf16[640,128]{1,0:T(8,128)(2,1)S(1)}, u32[]{:S(2)}, u32[]{:S(2)}) %collective-permute-start.11) | collective-permute-done | bytes 163872 | tf_op jit(solution)/shard_map/ppermute | solution.py:37
  92.4 0.9 collective-permute-done.5
  93.3 0.4 collective-permute-start.6
  93.7 3.1 %collective-permute-done.12 = bf16[320,128]{1,0:T(8,128)(2,1)S(1)} collective-permute-done((bf16[320,128]{1,0:T(8,128)(2,1)S(1)}, bf16[320,128]{1,0:T(8,128)(2,1)S(1)}, u32[]{:S(2)}, u32[]{:S(2)}) %collective-permute-start.12) | collective-permute-done | bytes 81952 | tf_op jit(solution)/shard_map/ppermute | solution.py:37
  96.8 0.8 collective-permute-start.13
  97.6 0.2 collective-permute-done.6
  97.9 2.1 %collective-permute-start.7 = (bf16[160,128]{1,0:T(8,128)(2,1)S(1)}, bf16[160,128]{1,0:T(8,128)(2,1)S(1)}, u32[]{:S(2)}, u32[]{:S(2)}) collective-permute-start(bf16[160,128]{1,0:T(8,128)(2,1)S(1)} %dynamic-slice_convert_fusion.5), channel_id=1, source_target_pairs={{0,8},{2,10},{4,12},{6,14},{8,0},{10,2},{12,4},{14,6},{1,9},{3,11}... | collective-permute-start | bytes 122888 | tf_op jit(solution)/shard_map/ppermute | solution.py:37
  99.9 1.9 %collective-permute-done.13 = bf16[160,128]{1,0:T(8,128)(2,1)S(1)} collective-permute-done((bf16[160,128]{1,0:T(8,128)(2,1)S(1)}, bf16[160,128]{1,0:T(8,128)(2,1)S(1)}, u32[]{:S(2)}, u32[]{:S(2)}) %collective-permute-start.13) | collective-permute-done | bytes 40992 | tf_op jit(solution)/shard_map/ppermute | solution.py:37
  101.8 0.8 collective-permute-start.14
  102.6 1.9 %collective-permute-done.7 = bf16[160,128]{1,0:T(8,128)(2,1)S(1)} collective-permute-done((bf16[160,128]{1,0:T(8,128)(2,1)S(1)}, bf16[160,128]{1,0:T(8,128)(2,1)S(1)}, u32[]{:S(2)}, u32[]{:S(2)}) %collective-permute-start.7) | collective-permute-done | bytes 40992 | tf_op jit(solution)/shard_map/ppermute | solution.py:37
  104.5 0.5 collective-permute-start.8
  105.0 1.8 %collective-permute-done.14 = bf16[160,128]{1,0:T(8,128)(2,1)S(1)} collective-permute-done((bf16[160,128]{1,0:T(8,128)(2,1)S(1)}, bf16[160,128]{1,0:T(8,128)(2,1)S(1)}, u32[]{:S(2)}, u32[]{:S(2)}) %collective-permute-start.14) | collective-permute-done | bytes 40992 | tf_op jit(solution)/shard_map/ppermute | solution.py:37
  106.8 0.3 collective-permute-start.15
  107.1 2.4 %collective-permute-done.8 = bf16[160,128]{1,0:T(8,128)(2,1)S(1)} collective-permute-done((bf16[160,128]{1,0:T(8,128)(2,1)S(1)}, bf16[160,128]{1,0:T(8,128)(2,1)S(1)}, u32[]{:S(2)}, u32[]{:S(2)}) %collective-permute-start.8) | collective-permute-done | bytes 40992 | tf_op jit(solution)/shard_map/ppermute | solution.py:37
  109.5 0.1 collective-permute-start.9
  109.6 1.7 %collective-permute-done.15 = bf16[320,128]{1,0:T(8,128)(2,1)S(1)} collective-permute-done((bf16[320,128]{1,0:T(8,128)(2,1)S(1)}, bf16[320,128]{1,0:T(8,128)(2,1)S(1)}, u32[]{:S(2)}, u32[]{:S(2)}) %collective-permute-start.15) | collective-permute-done | bytes 81952 | tf_op jit(solution)/shard_map/ppermute | solution.py:37
  111.4 2.7 %collective-permute-done.9 = bf16[320,128]{1,0:T(8,128)(2,1)S(1)} collective-permute-done((bf16[320,128]{1,0:T(8,128)(2,1)S(1)}, bf16[320,128]{1,0:T(8,128)(2,1)S(1)}, u32[]{:S(2)}, u32[]{:S(2)}) %collective-permute-start.9) | collective-permute-done | bytes 81952 | tf_op jit(solution)/shard_map/ppermute | solution.py:37
  114.1 0.9 collective-permute-start.19
  115.0 0.9 collective-permute-start.18
  115.9 1.5 %shard_map.133 = bf16[128,4096]{1,0:T(8,128)(2,1)S(1)} custom-call(bf16[4,128,1024]{2,1,0:T(8,128)(2,1)S(1)} %get-tuple-element.80.feat_ref), custom_call_target="tpu_custom_call" | custom-call | flops 1000000000 | bytes 4000000 | tf_op jit(solution)/shard_map/pallas_call | solution.py:91
  117.4 1.8 %copy.20 = bf16[4,32,4096]{2,0,1:T(4,128)(2,1)} copy(bf16[4,32,4096]{2,1,0:T(8,128)(2,1)S(1)} %bitcast.28) | data formatting | bytes 2097152 | tf_op jit(solution)/shard_map/reshape | solution.py:698
  119.2 0.2 collective-permute-done.19
  119.5 0.8 collective-permute-done.18
  120.5 0.5 collective-permute-start.21
  121.0 0.6 slice.15
  121.6 0.6 slice.14
  122.2 0.8 copy.16
  123.0 2.1 %shard_map.134 = (f32[4096,128]{1,0:T(8,128)}, f32[2048,64]{1,0:T(8,128)}) custom-call(bf16[1280,128]{1,0:T(8,128)(2,1)S(1)} %maximum_select_fusion.own_a_ref, bf16[1280,128]{1,0:T(8,128)(2,1)S(1)} %maximum_select_fusion.1.own_b_ref, bf16[1280,128]{1,0:T(8,128)(2,1)S(1)} %collective-permute-done.20.other_a_ref, ...), custom_call_target="tpu_custom_call" | custom-call | flops 1000000000 | bytes 4000000 | tf_op jit(solution)/shard_map/pallas_call | solution.py:91
  (49 shorter events, 1.1 us)
Async XLA Ops:
  0.6 10.7 %copy-start.1 = (bf16[64,64,128]{2,1,0:T(8,128)(2,1)S(1)}, bf16[64,64,128]{2,1,0:T(8,128)(2,1)}, u32[]{:S(2)}) copy-start(bf16[64,64,128]{2,1,0:T(8,128)(2,1)} %param.9) | copy-start | bytes 3145732
  0.6 10.7 %copy-start.2 = (bf16[64,32,64]{2,1,0:T(8,128)(2,1)S(1)}, bf16[64,32,64]{2,1,0:T(8,128)(2,1)}, u32[]{:S(2)}) copy-start(bf16[64,32,64]{2,1,0:T(8,128)(2,1)} %param.12) | copy-start | bytes 786436
  0.7 10.7 %copy-start.3 = (f32[64]{0:T(128)S(1)}, f32[64]{0:T(128)}, u32[]{:S(2)}) copy-start(f32[64]{0:T(128)} %param.10) | copy-start | bytes 772
  0.7 10.7 %copy-start.4 = (f32[64]{0:T(128)S(1)}, f32[64]{0:T(128)}, u32[]{:S(2)}) copy-start(f32[64]{0:T(128)} %param.11) | copy-start | bytes 772
  0.7 10.7 %copy-start.5 = (f32[32]{0:T(128)S(1)}, f32[32]{0:T(128)}, u32[]{:S(2)}) copy-start(f32[32]{0:T(128)} %param.13) | copy-start | bytes 388
  0.7 10.7 %copy-start.6 = (f32[32]{0:T(128)S(1)}, f32[32]{0:T(128)}, u32[]{:S(2)}) copy-start(f32[32]{0:T(128)} %param.14) | copy-start | bytes 388
  0.7 14.5 %collective-permute-start = (bf16[128,256]{1,0:T(8,128)(2,1)}, bf16[128,256]{1,0:T(8,128)(2,1)S(1)}, u32[]{:S(2)}, u32[]{:S(2)}) collective-permute-start(bf16[128,256]{1,0:T(8,128)(2,1)} %bitcast.29), channel_id=1, source_target_pairs={{0,2},{2,0},{4,6},{6,4},{8,10},{10,8},{12,14},{14,12},{1,3},{3,1},... | collective-permute-start | bytes 196616 | tf_op jit(solution)/shard_map/ppermute | solution.py:37
  3.7 11.5 %collective-permute-start.1 = (bf16[128,256]{1,0:T(8,128)(2,1)}, bf16[128,256]{1,0:T(8,128)(2,1)S(1)}, u32[]{:S(2)}, u32[]{:S(2)}) collective-permute-start(bf16[128,256]{1,0:T(8,128)(2,1)} %bitcast.30), channel_id=1, source_target_pairs={{2,4},{6,8},{10,12},{4,2},{8,6},{12,10},{3,5},{7,9},{11,13},{5,3},... | collective-permute-start | bytes 196616 | tf_op jit(solution)/shard_map/ppermute | solution.py:80
  6.2 9.0 %copy-start = (bf16[1,128,1,256]{3,1,2,0:T(8,128)(2,1)S(1)}, bf16[1,128,1,256]{3,1,2,0:T(8,128)(2,1)}, u32[]{:S(2)}) copy-start(bf16[1,128,1,256]{3,1,2,0:T(8,128)(2,1)} %param.8) | copy-start | bytes 196612
  6.3 30.8 %collective-permute-start.2 = (bf16[32,4096]{1,0:T(8,128)(2,1)S(1)}, bf16[32,4096]{1,0:T(8,128)(2,1)S(1)}, u32[]{:S(2)}, u32[]{:S(2)}) collective-permute-start(bf16[32,4096]{1,0:T(8,128)(2,1)S(1)} %get-tuple-element.101), channel_id=1, source_target_pairs={{0,2},{2,0},{4,6},{6,4},{8,10},{10,8},{12,14},{14,12},{1,3},{3,1},... | collective-permute-start | bytes 786440 | tf_op jit(solution)/shard_map/ppermute | solution.py:37
  10.6 26.5 %collective-permute-start.3 = (bf16[32,4096]{1,0:T(8,128)(2,1)S(1)}, bf16[32,4096]{1,0:T(8,128)(2,1)S(1)}, u32[]{:S(2)}, u32[]{:S(2)}) collective-permute-start(bf16[32,4096]{1,0:T(8,128)(2,1)S(1)} %get-tuple-element.100), channel_id=1, source_target_pairs={{2,4},{6,8},{10,12},{4,2},{8,6},{12,10},{3,5},{7,9},{11,13},{5,3},... | collective-permute-start | bytes 786440 | tf_op jit(solution)/shard_map/ppermute | solution.py:80
  80.5 1.8 %collective-permute-start.10 = (bf16[1280,128]{1,0:T(8,128)(2,1)S(1)}, bf16[1280,128]{1,0:T(8,128)(2,1)}, u32[]{:S(2)}, u32[]{:S(2)}) collective-permute-start(bf16[1280,128]{1,0:T(8,128)(2,1)S(1)} %get-tuple-element.79), channel_id=1, source_target_pairs={{0,1},{1,0},{2,3},{3,2},{4,5},{5,4},{6,7},{7,6},{8,9},{9,8},{10,11... | collective-permute-start | bytes 983048 | tf_op jit(solution)/shard_map/ppermute | solution.py:37
  80.7 6.9 %collective-permute-start.4 = (bf16[1280,128]{1,0:T(8,128)(2,1)S(1)}, bf16[1280,128]{1,0:T(8,128)(2,1)S(1)}, u32[]{:S(2)}, u32[]{:S(2)}) collective-permute-start(bf16[1280,128]{1,0:T(8,128)(2,1)S(1)} %get-tuple-element.77), channel_id=1, source_target_pairs={{0,1},{1,0},{2,3},{3,2},{4,5},{5,4},{6,7},{7,6},{8,9},{9,8},{10,11... | collective-permute-start | bytes 983048 | tf_op jit(solution)/shard_map/ppermute | solution.py:37
  81.1 33.9 %collective-permute-start.16 = (bf16[128,256]{1,0:T(8,128)(2,1)S(1)}, bf16[128,256]{1,0:T(8,128)(2,1)S(1)}, u32[]{:S(2)}, u32[]{:S(2)}) collective-permute-start(bf16[128,256]{1,0:T(8,128)(2,1)S(1)} %get-tuple-element.82), channel_id=1, source_target_pairs={{0,2},{2,0},{4,6},{6,4},{8,10},{10,8},{12,14},{14,12},{1,3},{3,1},... | collective-permute-start | bytes 196616 | tf_op jit(solution)/shard_map/ppermute | solution.py:37
  81.2 33.8 %collective-permute-start.17 = (bf16[128,256]{1,0:T(8,128)(2,1)S(1)}, bf16[128,256]{1,0:T(8,128)(2,1)S(1)}, u32[]{:S(2)}, u32[]{:S(2)}) collective-permute-start(bf16[128,256]{1,0:T(8,128)(2,1)S(1)} %get-tuple-element.83), channel_id=1, source_target_pairs={{2,4},{6,8},{10,12},{4,2},{8,6},{12,10},{3,5},{7,9},{11,13},{5,3},... | collective-permute-start | bytes 196616 | tf_op jit(solution)/shard_map/ppermute | solution.py:80
  83.4 8.8 %collective-permute-start.11 = (bf16[640,128]{1,0:T(8,128)(2,1)S(1)}, bf16[640,128]{1,0:T(8,128)(2,1)S(1)}, u32[]{:S(2)}, u32[]{:S(2)}) collective-permute-start(bf16[640,128]{1,0:T(8,128)(2,1)S(1)} %dynamic-slice_convert_fusion), channel_id=1, source_target_pairs={{0,4},{2,6},{4,0},{6,2},{8,12},{10,14},{12,8},{14,10},{1,5},{3,7},... | collective-permute-start | bytes 491528 | tf_op jit(solution)/shard_map/ppermute | solution.py:37
  87.7 5.5 %collective-permute-start.5 = (bf16[640,128]{1,0:T(8,128)(2,1)S(1)}, bf16[640,128]{1,0:T(8,128)(2,1)S(1)}, u32[]{:S(2)}, u32[]{:S(2)}) collective-permute-start(bf16[640,128]{1,0:T(8,128)(2,1)S(1)} %dynamic-slice_convert_fusion.1), channel_id=1, source_target_pairs={{0,2},{2,0},{4,6},{6,4},{8,10},{10,8},{12,14},{14,12},{1,3},{3,1},... | collective-permute-start | bytes 491528 | tf_op jit(solution)/shard_map/ppermute | solution.py:37
  92.3 4.5 %collective-permute-start.12 = (bf16[320,128]{1,0:T(8,128)(2,1)S(1)}, bf16[320,128]{1,0:T(8,128)(2,1)S(1)}, u32[]{:S(2)}, u32[]{:S(2)}) collective-permute-start(bf16[320,128]{1,0:T(8,128)(2,1)S(1)} %dynamic-slice_convert_fusion.2), channel_id=1, source_target_pairs={{0,2},{2,0},{4,6},{6,4},{8,10},{10,8},{12,14},{14,12},{1,3},{3,1},... | collective-permute-start | bytes 245768 | tf_op jit(solution)/shard_map/ppermute | solution.py:37
  93.3 4.5 %collective-permute-start.6 = (bf16[320,128]{1,0:T(8,128)(2,1)S(1)}, bf16[320,128]{1,0:T(8,128)(2,1)S(1)}, u32[]{:S(2)}, u32[]{:S(2)}) collective-permute-start(bf16[320,128]{1,0:T(8,128)(2,1)S(1)} %dynamic-slice_convert_fusion.3), channel_id=1, source_target_pairs={{0,4},{2,6},{4,0},{6,2},{8,12},{10,14},{12,8},{14,10},{1,5},{3,7},... | collective-permute-start | bytes 245768 | tf_op jit(solution)/shard_map/ppermute | solution.py:37
  96.8 5.0 %collective-permute-start.13 = (bf16[160,128]{1,0:T(8,128)(2,1)S(1)}, bf16[160,128]{1,0:T(8,128)(2,1)S(1)}, u32[]{:S(2)}, u32[]{:S(2)}) collective-permute-start(bf16[160,128]{1,0:T(8,128)(2,1)S(1)} %dynamic-slice_convert_fusion.4), channel_id=1, source_target_pairs={{0,8},{2,10},{4,12},{6,14},{8,0},{10,2},{12,4},{14,6},{1,9},{3,11}... | collective-permute-start | bytes 122888 | tf_op jit(solution)/shard_map/ppermute | solution.py:37
  97.9 6.6 %collective-permute-start.7 = (bf16[160,128]{1,0:T(8,128)(2,1)S(1)}, bf16[160,128]{1,0:T(8,128)(2,1)S(1)}, u32[]{:S(2)}, u32[]{:S(2)}) collective-permute-start(bf16[160,128]{1,0:T(8,128)(2,1)S(1)} %dynamic-slice_convert_fusion.5), channel_id=1, source_target_pairs={{0,8},{2,10},{4,12},{6,14},{8,0},{10,2},{12,4},{14,6},{1,9},{3,11}... | collective-permute-start | bytes 122888 | tf_op jit(solution)/shard_map/ppermute | solution.py:37
  101.8 5.0 %collective-permute-start.14 = (bf16[160,128]{1,0:T(8,128)(2,1)S(1)}, bf16[160,128]{1,0:T(8,128)(2,1)S(1)}, u32[]{:S(2)}, u32[]{:S(2)}) collective-permute-start(bf16[160,128]{1,0:T(8,128)(2,1)S(1)} %add_convert_fusion), channel_id=1, source_target_pairs={{0,8},{2,10},{4,12},{6,14},{8,0},{10,2},{12,4},{14,6},{1,9},{3,11}... | collective-permute-start | bytes 122888 | tf_op jit(solution)/shard_map/ppermute | solution.py:37
  104.5 5.0 %collective-permute-start.8 = (bf16[160,128]{1,0:T(8,128)(2,1)S(1)}, bf16[160,128]{1,0:T(8,128)(2,1)S(1)}, u32[]{:S(2)}, u32[]{:S(2)}) collective-permute-start(bf16[160,128]{1,0:T(8,128)(2,1)S(1)} %add_convert_fusion.1), channel_id=1, source_target_pairs={{0,8},{2,10},{4,12},{6,14},{8,0},{10,2},{12,4},{14,6},{1,9},{3,11}... | collective-permute-start | bytes 122888 | tf_op jit(solution)/shard_map/ppermute | solution.py:37
  106.8 4.5 %collective-permute-start.15 = (bf16[320,128]{1,0:T(8,128)(2,1)S(1)}, bf16[320,128]{1,0:T(8,128)(2,1)S(1)}, u32[]{:S(2)}, u32[]{:S(2)}) collective-permute-start(bf16[320,128]{1,0:T(8,128)(2,1)S(1)} %maximum_select_fusion.5), channel_id=1, source_target_pairs={{0,2},{2,0},{4,6},{6,4},{8,10},{10,8},{12,14},{14,12},{1,3},{3,1},... | collective-permute-start | bytes 245768 | tf_op jit(solution)/shard_map/ppermute | solution.py:37
  109.5 4.5 %collective-permute-start.9 = (bf16[320,128]{1,0:T(8,128)(2,1)S(1)}, bf16[320,128]{1,0:T(8,128)(2,1)S(1)}, u32[]{:S(2)}, u32[]{:S(2)}) collective-permute-start(bf16[320,128]{1,0:T(8,128)(2,1)S(1)} %maximum_select_fusion.4), channel_id=1, source_target_pairs={{0,4},{2,6},{4,0},{6,2},{8,12},{10,14},{12,8},{14,10},{1,5},{3,7},... | collective-permute-start | bytes 245768 | tf_op jit(solution)/shard_map/ppermute | solution.py:37
  114.1 5.4 %collective-permute-start.19 = (bf16[640,128]{1,0:T(8,128)(2,1)S(1)}, bf16[640,128]{1,0:T(8,128)(2,1)S(1)}, u32[]{:S(2)}, u32[]{:S(2)}) collective-permute-start(bf16[640,128]{1,0:T(8,128)(2,1)S(1)} %maximum_select_fusion.3), channel_id=1, source_target_pairs={{0,4},{2,6},{4,0},{6,2},{8,12},{10,14},{12,8},{14,10},{1,5},{3,7},... | collective-permute-start | bytes 491528 | tf_op jit(solution)/shard_map/ppermute | solution.py:37
  115.0 5.4 %collective-permute-start.18 = (bf16[640,128]{1,0:T(8,128)(2,1)S(1)}, bf16[640,128]{1,0:T(8,128)(2,1)S(1)}, u32[]{:S(2)}, u32[]{:S(2)}) collective-permute-start(bf16[640,128]{1,0:T(8,128)(2,1)S(1)} %maximum_select_fusion.2), channel_id=1, source_target_pairs={{0,2},{2,0},{4,6},{6,4},{8,10},{10,8},{12,14},{14,12},{1,3},{3,1},... | collective-permute-start | bytes 491528 | tf_op jit(solution)/shard_map/ppermute | solution.py:37
  120.5 2.5 %collective-permute-start.20 = (bf16[1280,128]{1,0:T(8,128)(2,1)S(1)}, bf16[1280,128]{1,0:T(8,128)(2,1)S(1)}, u32[]{:S(2)}, u32[]{:S(2)}) collective-permute-start(bf16[1280,128]{1,0:T(8,128)(2,1)S(1)} %maximum_select_fusion.own_a_ref), channel_id=1, source_target_pairs={{0,1},{1,0},{2,3},{3,2},{4,5},{5,4},{6,7},{7,6},{8,9},{9,8},{10,11... | collective-permute-start | bytes 983048 | tf_op jit(solution)/shard_map/ppermute | solution.py:37
  120.5 2.4 %collective-permute-start.21 = (bf16[1280,128]{1,0:T(8,128)(2,1)S(1)}, bf16[1280,128]{1,0:T(8,128)(2,1)S(1)}, u32[]{:S(2)}, u32[]{:S(2)}) collective-permute-start(bf16[1280,128]{1,0:T(8,128)(2,1)S(1)} %maximum_select_fusion.1.own_b_ref), channel_id=1, source_target_pairs={{0,1},{1,0},{2,3},{3,2},{4,5},{5,4},{6,7},{7,6},{8,9},{9,8},{10,11... | collective-permute-start | bytes 983048 | tf_op jit(solution)/shard_map/ppermute | solution.py:37

commit v3 on v2

--- a/solution.py
+++ b/solution.py
@@ -157,7 +157,7 @@
 
 
 def sigmoid(values):
-    return 1.0 / (1.0 + jnp.exp(-values))
+    return 0.5 * jnp.tanh(0.5 * values) + 0.5
 
 
 def spread_planes(cot_ref, out_ref, planes, matrix):
@@ -236,24 +236,10 @@
                             ]
                             pieces[slot] = w2_ref[tap * C2 : (tap + 1) * C2, :]
                 a2_ref[row2 : row2 + C2, :] = jnp.concatenate(pieces, axis=1)
-    eye = jnp.where(
-        lax.broadcasted_iota(jnp.int32, (128, 128), 0)
-        == lax.broadcasted_iota(jnp.int32, (128, 128), 1),
-        1.0,
-        0.0,
-    ).astype(BF16)
-
-    @pl.loop(0, 8)
-    def _(k):
-        at = pl.multiple_of(k * 512, 512)
-        b1_ref[:, pl.ds(at, 512)] = matmul_nt(eye, w1_ref[pl.ds(at, 512), :]).astype(BF16)
-
-    @pl.loop(0, 4)
-    def _(k):
-        at = pl.multiple_of(k * 512, 512)
-        b2_ref[:, pl.ds(at, 512)] = matmul_nt(eye[0:C1, 0:C1], w2_ref[pl.ds(at, 512), :]).astype(
-            BF16
-        )
+    for k in range(32):
+        b1_ref[:, k * 128 : (k + 1) * 128] = jnp.transpose(w1_ref[k * 128 : (k + 1) * 128, :])
+    for k in range(16):
+        b2_ref[:, k * 128 : (k + 1) * 128] = jnp.transpose(w2_ref[k * 128 : (k + 1) * 128, :])
 
 
 def first_kernel(
@@ -281,56 +267,68 @@
     emit_rows(out_ref, mean, squares)
 
 
-def second_kernel(got_ref, pre1_ref, p1_ref, a2_ref, sh_ref, pre_ref, act_ref, st_ref, out_ref, x_ref):
+def second_kernel(got_ref, pre1_ref, p1_ref, a2_ref, sh_ref, pre_ref, act_ref, st_ref, out_ref, x_ref, all_ref):
     mean, scale = moments(got_ref[...], 8 * CELLS)
     st = jnp.concatenate([mean, scale, p1_ref[0:6]], axis=0)
     st_ref[...] = st
     cols = columns(st)
     mean, scale, gain, shift = (cols[0:C1, k : k + 1] for k in range(4))
     keeps = (cols[0:C1, 4:5], None, None, cols[0:C1, 5:6])
-    for q in range(4):
-        for block in range(4):
-            rp, cp = block // 2, block % 2
+    for block in range(4):
+        rp, cp = block // 2, block % 2
+        for q in range(4):
             norm = gain * ((pre1_ref[q, block * C1 : (block + 1) * C1, :] - mean) * scale) + shift
             act = norm * sigmoid(norm)
             if keeps[q] is not None:
                 act = act * keeps[q]
             act = act.astype(BF16)
+            all_ref[block, q * C1 : (q + 1) * C1, :] = act
             if q in (1, 2):
-                act_ref[q - 1, :, block * CELLS : (block + 1) * CELLS] = act
-            sj, sl = 1 - 2 * rp, 1 - 2 * cp
-            moved = {(0, 0): act}
-            for dj, dl in ((sj, 0), (0, sl), (sj, sl)):
-                moved[dj, dl] = matmul(act, sh_ref[:, shift_slot(dj, dl)]).astype(BF16)
-            for (trp, dr), (srp, dj) in FINE_STEPS.items():
-                if srp != rp:
+                act_ref[(q - 1) * C1 : q * C1, block * CELLS : (block + 1) * CELLS] = act
+        sj, sl = 1 - 2 * rp, 1 - 2 * cp
+        for dj, dl in ((0, 0), (sj, 0), (0, sl), (sj, sl)):
+            moved = all_ref[block]
+            if (dj, dl) != (0, 0):
+                moved = matmul(moved, sh_ref[:, shift_slot(dj, dl)]).astype(BF16)
+            for (trp, dr), source in FINE_STEPS.items():
+                if source != (rp, dj):
                     continue
-                for (tcp, dc), (scp, dl) in FINE_STEPS.items():
-                    if scp != cp:
+                for (tcp, dc), source in FINE_STEPS.items():
+                    if source != (cp, dl):
                         continue
-                    at = q * 9 * C1 + ((dr + 1) * 3 + dc + 1) * C1
                     lane = (2 * trp + tcp) * CELLS
-                    x_ref[at : at + C1, lane : lane + CELLS] = moved[dj, dl]
+                    for q in range(4):
+                        at = q * 9 * C1 + ((dr + 1) * 3 + dc + 1) * C1
+                        x_ref[at : at + C1, lane : lane + CELLS] = moved[q * C1 : (q + 1) * C1]
 
     for m in range(3):
-
-        @pl.loop(0, 4)
-        def _(block):
-            lane = pl.multiple_of(block * CELLS, CELLS)
-            both = matmul(a2_ref[...], x_ref[m * 9 * C1 : (m + 2) * 9 * C1, pl.ds(lane, CELLS)])
-            pre_ref[2 * m + 1, :, pl.ds(lane, CELLS)] = both[0 : 4 * C2]
-            pre_ref[2 * m, :, pl.ds(lane, CELLS)] = both[4 * C2 : 8 * C2]
-
-    total = pre_ref[1] + pre_ref[2] + pre_ref[3] + pre_ref[4]
-    sums = fold(jnp.sum(total, axis=1, keepdims=True), C2)
-    mean = sums / (64 * CELLS)
-    wide = jnp.concatenate([mean] * 4, axis=0)
-    squares = jnp.zeros((4 * C2, CELLS), F32)
-    for t in range(1, 5):
         for block in range(4):
-            away = pre_ref[t, :, block * CELLS : (block + 1) * CELLS] - wide
-            squares = squares + away * away
-    emit_rows(out_ref, mean, fold(jnp.sum(squares, axis=1, keepdims=True), C2))
+            lanes = slice(block * CELLS, (block + 1) * CELLS)
+            both = matmul(a2_ref[...], x_ref[m * 9 * C1 : (m + 2) * 9 * C1, lanes])
+            pre_ref[2 * m + 1, :, lanes] = both[0 : 4 * C2]
+            pre_ref[2 * m, :, lanes] = both[4 * C2 : 8 * C2]
+
+    partial = jnp.zeros((C2, CELLS), F32)
+    for phase in range(4):
+        for t in range(1, 5):
+            for block in range(4):
+                partial = partial + pre_ref[
+                    t, phase * C2 : (phase + 1) * C2, block * CELLS : (block + 1) * CELLS
+                ]
+    mean = jnp.sum(partial, axis=1, keepdims=True) / (64 * CELLS)
+    wide = jnp.broadcast_to(mean, (C2, CELLS))
+    squares = jnp.zeros((C2, CELLS), F32)
+    for phase in range(4):
+        for t in range(1, 5):
+            for block in range(4):
+                away = (
+                    pre_ref[
+                        t, phase * C2 : (phase + 1) * C2, block * CELLS : (block + 1) * CELLS
+                    ]
+                    - wide
+                )
+                squares = squares + away * away
+    emit_rows(out_ref, mean, jnp.sum(squares, axis=1, keepdims=True))
 
 
 def gather_kernel(feat_ref, out_ref):
@@ -371,84 +369,87 @@
     st = jnp.concatenate([mean, scale, p2_ref[0:6]], axis=0)
     st_ref[...] = st
     cols = columns(st)
-    mean, scale, gain, shift = (cols[:, k : k + 1] for k in range(4))
-
-    def slope(t, lane, cot):
-        hat = (pre_ref[t, :, pl.ds(lane, CELLS)] - mean) * scale
-        norm = gain * hat + shift
-        gate = sigmoid(norm)
-        grad = cot.astype(F32) * (gate * (1.0 + norm * (1.0 - gate)))
-        grad_ref[t, :, pl.ds(lane, CELLS)] = grad
-        return hat, norm, gate, grad
-
-    first = jnp.zeros((4 * C2, CELLS), F32)
-    second = jnp.zeros((4 * C2, CELLS), F32)
-    copies = []
-    for t in range(1, 5):
-
-        def body(block, carry):
-            lane = pl.multiple_of(block * CELLS, CELLS)
-            hat, norm, gate, grad = slope(t, lane, cot_ref[t - 1, :, pl.ds(lane, CELLS)])
-            feat_ref[t - 1, :, pl.ds(lane, CELLS)] = (norm * gate).astype(BF16)
+    sums = []
+    for phase in range(4):
+        rows = slice(phase * C2, (phase + 1) * C2)
+        mean, scale, gain, shift = (
+            jnp.broadcast_to(cols[rows, k : k + 1], (C2, CELLS)) for k in range(4)
+        )
+
+        def slope(t, lane, cot):
+            hat = (pre_ref[t, rows, pl.ds(lane, CELLS)] - mean) * scale
+            norm = gain * hat + shift
+            gate = sigmoid(norm)
+            grad = cot.astype(F32) * (gate * (1.0 + norm * (1.0 - gate)))
+            grad_ref[t, rows, pl.ds(lane, CELLS)] = grad
+            return hat, norm, gate, grad
+
+        def body(step, carry):
+            t = step // 4
+            lane = pl.multiple_of((step % 4) * CELLS, CELLS)
+            hat, norm, gate, grad = slope(t + 1, lane, cot_ref[t, rows, pl.ds(lane, CELLS)])
+            feat_ref[t, rows, pl.ds(lane, CELLS)] = (norm * gate).astype(BF16)
             return carry[0] + grad * hat, carry[1] + grad
 
-        first, second = lax.fori_loop(0, 4, body, (first, second))
-        copies.append(
-            pltpu.make_async_copy(feat_ref.at[t - 1], feat_far.at[t - 1], sem.at[t - 1])
-        )
-        copies[-1].start()
-    for k in range(2):
-
-        @pl.loop(0, 4)
-        def _(block):
-            lane = pl.multiple_of(block * CELLS, CELLS)
-            slope(5 * k, lane, edge_ref[k, :, pl.ds(lane, CELLS)])
-
+        zero = jnp.zeros((C2, CELLS), F32)
+        sums.append(lax.fori_loop(0, 16, body, (zero, zero), unroll=16))
+
+        for k in range(2):
+            for lane in range(0, 4 * CELLS, CELLS):
+                slope(5 * k, lane, edge_ref[k, rows, pl.ds(lane, CELLS)])
+
+    copy = pltpu.make_async_copy(feat_ref, feat_far, sem)
+    copy.start()
+    first, second = (sum(part[k] for part in sums) for k in range(2))
     emit_rows(
         out_ref,
-        fold(jnp.sum(first, axis=1, keepdims=True), C2),
-        fold(jnp.sum(second, axis=1, keepdims=True), C2),
-    )
-    for copy in copies:
-        copy.wait()
+        jnp.sum(first, axis=1, keepdims=True),
+        jnp.sum(second, axis=1, keepdims=True),
+    )
+    copy.wait()
 
 
 def fourth_kernel(
     got_ref, pre_ref, grad_ref, st2_ref, b2_ref, sh_ref, act_ref, pre1_ref, st1_ref,
-    g1_ref, dw_ref, sum_ref, out_ref, x_ref,
+    g1_ref, dw_ref, sum_ref, out_ref, x_ref, all_ref,
 ):
     sums = jnp.sum(got_ref[...], axis=0)
     sum_ref[...] = sums
     total = got_ref.shape[0] * 64 * CELLS
     cols = columns(jnp.concatenate([st2_ref[0:6], sums[0:2] / total], axis=0))
     mean, scale, gain = (cols[:, k : k + 1] for k in range(3))
-    hat_part, part = cols[:, 6:7], cols[:, 7:8]
-    keeps = {0: cols[:, 4:5], 5: cols[:, 5:6]}
-    for t in range(6):
-        factor = gain * scale
-        if t in keeps:
-            factor = factor * keeps[t]
-        for block in range(4):
-            rp, cp = block // 2, block % 2
-            lanes = slice(block * CELLS, (block + 1) * CELLS)
-            hat = (pre_ref[t, :, lanes] - mean) * scale
-            dpre = (factor * (grad_ref[t, :, lanes] - part - hat * hat_part)).astype(BF16)
-            sj, sl = 1 - 2 * rp, 1 - 2 * cp
-            moved = {(0, 0): dpre}
-            for dj, dl in ((sj, 0), (0, sl), (sj, sl)):
-                moved[dj, dl] = matmul(dpre, sh_ref[:, shift_slot(dj, dl)]).astype(BF16)
-            for q, (rp2, dr) in enumerate(TAP_PHASES):
-                for r, (cp2, dc) in enumerate(TAP_PHASES):
-                    row = (2 * rp2 + cp2) * C2
-                    for trp in range(2):
-                        for tcp in range(2):
-                            srp, dj = FINE_STEPS[trp, dr]
-                            scp, dl = FINE_STEPS[tcp, dc]
-                            if (srp, scp) != (rp, cp):
-                                continue
-                            at = t * 16 * C2 + (4 * q + r) * C2
-                            lane = (2 * trp + tcp) * CELLS
-                            x_ref[at : at + C2, lane : lane + CELLS] = moved[dj, dl][row : row + C2]
+    factor = gain * scale
+    slant, offset = factor * scale * cols[:, 6:7], factor * cols[:, 7:8]
+    for block in range(4):
+        rp, cp = block // 2, block % 2
+        lanes = slice(block * CELLS, (block + 1) * CELLS)
+        for phase in range(4):
+            rows = slice(phase * C2, (phase + 1) * C2)
+            for t in range(6):
+                away = pre_ref[t, rows, lanes] - mean[rows]
+                dpre = factor[rows] * grad_ref[t, rows, lanes] - offset[rows] - away * slant[rows]
+                if t == 0:
+                    dpre = dpre * cols[rows, 4:5]
+                if t == 5:
+                    dpre = dpre * cols[rows, 5:6]
+                all_ref[block, phase, t * C2 : (t + 1) * C2, :] = dpre.astype(BF16)
+        for q, (rp2, dr) in enumerate(TAP_PHASES):
+            for r, (cp2, dc) in enumerate(TAP_PHASES):
+                moves = {}
+                for trp in range(2):
+                    for tcp in range(2):
+                        srp, dj = FINE_STEPS[trp, dr]
+                        scp, dl = FINE_STEPS[tcp, dc]
+                        if (srp, scp) == (rp, cp):
+                            moves[trp, tcp] = (dj, dl)
+                for (trp, tcp), (dj, dl) in moves.items():
+                    moved = all_ref[block, 2 * rp2 + cp2]
+                    if (dj, dl) != (0, 0):
+                        moved = matmul(moved, sh_ref[:, shift_slot(dj, dl)]).astype(BF16)
+                    lane = (2 * trp + tcp) * CELLS
+                    for t in range(6):
+                        at = t * 16 * C2 + (4 * q + r) * C2
+                        x_ref[at : at + C2, lane : lane + CELLS] = moved[t * C2 : (t + 1) * C2]
 
     cols = columns(st1_ref[...])
     mean, scale, gain, shift = (cols[0:C1, k : k + 1] for k in range(4))
@@ -470,14 +471,15 @@
         jnp.sum(first, axis=1, keepdims=True),
         jnp.sum(second, axis=1, keepdims=True),
     )
-    parts = []
-    for p in range(4):
-        part = matmul_nt(x_ref[p * 16 * C2 : (p + 1) * 16 * C2, :], act_ref[0])
-        parts.append(part + matmul_nt(x_ref[(p + 2) * 16 * C2 : (p + 3) * 16 * C2, :], act_ref[1]))
+    parts = [
+        matmul_nt(x_ref[t * 16 * C2 : (t + 1) * 16 * C2, :], act_ref[...]) for t in range(6)
+    ]
     for p in range(2):
+        low = [parts[p + 2 * k][:, 0:C1] for k in range(2)]
+        high = [parts[p + 2 + 2 * k][:, C1:] for k in range(2)]
         dw_ref[p * 16 * C2 : (p + 1) * 16 * C2, :] = jnp.concatenate(
-            [parts[p], parts[p + 2]], axis=1
-        )
+            low, axis=1
+        ) + jnp.concatenate(high, axis=1)
 
 
 def first_dpre(grad, pre, cols):
@@ -628,9 +630,9 @@
     got = exchange(out)
     pre2, act, st1, out = call(
         second_kernel,
-        [((6, 4 * C2, 4 * CELLS), F32), ((2, C1, 4 * CELLS), BF16), ((8, 128), F32), stats],
+        [((6, 4 * C2, 4 * CELLS), F32), ((2 * C1, 4 * CELLS), BF16), ((8, 128), F32), stats],
         [got, pre1, p1, a2, sh],
-        [pltpu.VMEM((36 * C1, 4 * CELLS), BF16)],
+        [pltpu.VMEM((36 * C1, 4 * CELLS), BF16), pltpu.VMEM((4, 4 * C1, CELLS), BF16)],
     )
     out, cot_inner, cot_outer = hold(out, cot_inner, cot_outer)
     got = exchange(out)
@@ -647,7 +649,7 @@
             pltpu.VMEM((2 * C2, 16 * CELLS), BF16),
             pltpu.VMEM((2, 4 * C2, 4 * CELLS), BF16),
             pltpu.VMEM((4, 4 * C2, 4 * CELLS), BF16),
-            pltpu.SemaphoreType.DMA((4,)),
+            pltpu.SemaphoreType.DMA,
         ],
         far=(1,),
     )
@@ -656,7 +658,7 @@
         fourth_kernel,
         [((2, 4 * C1, CELLS), F32), ((32 * C2, 2 * C1), F32), ((8, 128), F32), stats],
         [got, pre2, grad2, st2, b2, sh, act, pre1, st1],
-        [pltpu.VMEM((96 * C2, 4 * CELLS), BF16)],
+        [pltpu.VMEM((96 * C2, 4 * CELLS), BF16), pltpu.VMEM((4, 4, 6 * C2, CELLS), BF16)],
     )
     got = exchange(out)
     rows = (64 * C1 + 32 * C2) // 4
@@ -687,10 +689,11 @@
     ]
     orders = chunk_steps()
     steps = len(orders[0])
-    latent_grad = mid + swap_inner(lat_in).astype(F32) + swap_outer(lat_out).astype(F32)
     for step in range(steps):
         parts = [halve(part, *order[step]) for part, order in zip(parts, orders)]
     parts = [part.astype(BF16) for part in parts]
+    lat_in, lat_out, *parts = hold(lat_in, lat_out, *parts)
+    latent_grad = mid + swap_inner(lat_in).astype(F32) + swap_outer(lat_out).astype(F32)
     for step in reversed(range(steps)):
         if step == 0:
             feat, *parts = hold(feat, *parts)

time: 125 us -> 116 us (0.928)
  Pallas kernels: 30.9 us -> 21.5 us
  waiting for transfers between devices: 22.5 us -> 15.7 us
  starting transfers between devices: 21.5 us -> 27.9 us
    pallas_call x8, Pallas kernels: 30.9 us -> 21.5 us  [call(): pl.pallas_call(kernel, out_shape=[jax.ShapeDtypeStruct(shape, dtype) for...]
    ppermute x19, waiting for transfers between devices: 22.5 us -> 15.7 us  [swap(): lax.ppermute(block, axis, [(i, i ^ bit) for i in range(lax.axis_size(axis...]
    ppermute x19, starting transfers between devices: 19.6 us -> 25.9 us  [swap(): lax.ppermute(block, axis, [(i, i ^ bit) for i in range(lax.axis_size(axis...]
  transfers between devices with their start and end apart: 22 -> 22, of which waited for: 13 -> 8; matrix products, arithmetic and copies ran while one was open for 6% -> 6% of each run, Pallas kernels for 11% -> 8%
where the time goes in v3:
time: 116 us; the launch traced here: 115 us
  blocking collectives  41.8 us (36%)
  starting transfers between devices  27.9 us (24%)
  Pallas kernels  21.5 us (19%)
  waiting for transfers between devices  15.7 us (14%)
  local copies, waits for them, and re-layouts  5.66 us (5%)
  other arithmetic  1.57 us (1%)
    all_to_all x4, blocking collectives, exchange(): return lax.all_to_all(copies, GROUP, 0, 0)  41.8 us
    ppermute x19, starting transfers between devices, swap(): lax.ppermute(block, axis, [(i, i ^ bit) for i in range(lax.axis_size(axis...  25.9 us
    pallas_call x8, Pallas kernels, call(): pl.pallas_call(kernel, out_shape=[jax.ShapeDtypeStruct(shape, dtype) for...  21.5 us
    ppermute x19, waiting for transfers between devices, swap(): lax.ppermute(block, axis, [(i, i ^ bit) for i in range(lax.axis_size(axis...  15.7 us
    unnamed x16, local copies, waits for them, and re-layouts  2.63 us
  transfers between devices with their start and end apart: 22, of which 8 were waited for; matrix products, arithmetic and copies ran while one was open for 6% of the time, Pallas kernels for 8%

profile of v3, /device:TPU:0, one launch (start us, length us, event | category | flops | bytes accessed | tf_op | source)
XLA Modules:
  0.0 115.2 jit_solution(17853084385610676930)
XLA Ops:
  0.7 3.0 %collective-permute-start = (bf16[128,256]{1,0:T(8,128)(2,1)}, bf16[128,256]{1,0:T(8,128)(2,1)S(1)}, u32[]{:S(2)}, u32[]{:S(2)}) collective-permute-start(bf16[128,256]{1,0:T(8,128)(2,1)} %bitcast.29), channel_id=1, source_target_pairs={{0,2},{2,0},{4,6},{6,4},{8,10},{10,8},{12,14},{14,12},{1,3},{3,1},... | collective-permute-start | bytes 196616 | tf_op jit(solution)/shard_map/ppermute | solution.py:37
  3.7 0.7 collective-permute-start.1
  4.4 1.8 %copy.21 = bf16[1,32,4,4096]{3,1,2,0:T(8,128)(2,1)S(1)} copy(bf16[1,32,4,4096]{3,2,1,0:T(4,128)(2,1)} %param.15) | data formatting | bytes 2097152 | tf_op args[7]
  6.3 4.3 %collective-permute-start.2 = (bf16[32,4096]{1,0:T(8,128)(2,1)S(1)}, bf16[32,4096]{1,0:T(8,128)(2,1)S(1)}, u32[]{:S(2)}, u32[]{:S(2)}) collective-permute-start(bf16[32,4096]{1,0:T(8,128)(2,1)S(1)} %get-tuple-element.109), channel_id=1, source_target_pairs={{0,2},{2,0},{4,6},{6,4},{8,10},{10,8},{12,14},{14,12},{1,3},{3,1},... | collective-permute-start | bytes 786440 | tf_op jit(solution)/shard_map/ppermute | solution.py:37
  10.6 0.7 collective-permute-start.3
  11.4 2.0 %shard_map.127 = (bf16[512,2304]{1,0:T(8,128)(2,1)S(1)}, bf16[256,1152]{1,0:T(8,128)(2,1)S(1)}, bf16[128,4096]{1,0:T(8,128)(2,1)S(1)}, bf16[64,2048]{1,0:T(8,128...) custom-call(bf16[4096,128]{1,0:T(8,128)(2,1)S(1)} %bitcast.33, ...), custom_call_target="tpu_custom_call" | custom-call | flops 1000000000 | bytes 4000000 | tf_op jit(solution)/shard_map/pallas_call | solution.py:91
  13.4 2.2 %shard_map.128 = (f32[4,256,256]{2,1,0:T(8,128)S(1)}, f32[16,8,128]{2,1,0:T(8,128)S(1)}, bf16[2,128,256]{2,1,0:T(8,128)(2,1)S(1)}) custom-call(bf16[128,256]{1,0:T(8,128)(2,1)S(1)} %bitcast.31, bf16[128,256]{1,0:T(8,128)(2,1)S(1)} %collective-permute-done.inner_ref, bf16[128,256]{1,0:T(8,128)(2,1)S(1)} %collective-permute-done.1.outer_ref, ...), custom_call_target="tpu_custom_call" | custom-call | flops 1000000000 | bytes 4000000 | tf_op jit(solution)/shard_map/pallas_call | solution.py:91
  15.6 13.4 %all_to_all.20.got_ref = f32[16,8,128]{2,1,0:T(8,128)S(1)} all-to-all(f32[16,8,128]{2,1,0:T(8,128)S(1)} %get-tuple-element.56), channel_id=1, replica_groups=mesh['group'=2,'space'=8,'rep'=2] {'space','rep'}, dimensions={0} | all-to-all | bytes 131072 | tf_op jit(solution)/shard_map/all_to_all | solution.py:66
  29.0 3.7 %shard_map.129 = (f32[6,128,1024]{2,1,0:T(8,128)S(1)}, bf16[128,1024]{1,0:T(8,128)(2,1)S(1)}, f32[8,128]{1,0:T(8,128)S(1)}, f32[16,8,128]{2,1,0:T(8,128)S(1)}) custom-call(f32[16,8,128]{2,1,0:T(8,128)S(1)} %all_to_all.20.got_ref, f32[4,256,256]{2,1,0:T(8,128)S(1)} %get-tuple-element.57.pre1_ref, f32[8,128]{1,0:T(8,128)S(1)} %get-tuple-element.58.p1_ref, ...), custom_call_target="tpu_custom_call" | custom-call | flops 1000000000 | bytes 4000000 | tf_op jit(solution)/shard_map/pallas_call | solution.py:91
  32.7 9.5 %all_to_all.21.got_ref = f32[16,8,128]{2,1,0:T(8,128)S(1)} all-to-all(f32[16,8,128]{2,1,0:T(8,128)S(1)} %get-tuple-element.61), channel_id=1, replica_groups=mesh['group'=2,'space'=8,'rep'=2] {'space','rep'}, dimensions={0} | all-to-all | bytes 131072 | tf_op jit(solution)/shard_map/all_to_all | solution.py:66
  42.1 2.7 %shard_map.130 = (f32[6,128,1024]{2,1,0:T(8,128)S(1)}, bf16[4,128,1024]{2,1,0:T(8,128)(2,1)S(1)}, f32[8,128]{1,0:T(8,128)S(1)}, f32[16,8,128]{2,1,0:T(8,128)S(1)}) custom-call(f32[16,8,128]{2,1,0:T(8,128)S(1)} %all_to_all.21.got_ref, f32[6,128,1024]{2,1,0:T(8,128)S(1)} %get-tuple-element.62.pre_ref, bf16[4,128,1024]{2,1,0:T(8,128)(2,1)S(1)} %get-tuple-element.63.cot_ref, ...), custom_call_target="tpu_custom_call" | custom-call | flops 1000000000 | bytes 4000000 | tf_op jit(solution)/shard_map/pallas_call | solution.py:91
  44.8 9.5 %all_to_all.22.got_ref = f32[16,8,128]{2,1,0:T(8,128)S(1)} all-to-all(f32[16,8,128]{2,1,0:T(8,128)S(1)} %get-tuple-element.69), channel_id=1, replica_groups=mesh['group'=2,'space'=8,'rep'=2] {'space','rep'}, dimensions={0} | all-to-all | bytes 131072 | tf_op jit(solution)/shard_map/all_to_all | solution.py:66
  54.3 4.5 %shard_map.131 = (f32[2,256,256]{2,1,0:T(8,128)S(1)}, f32[1024,128]{1,0:T(8,128)S(1)}, f32[8,128]{1,0:T(8,128)S(1)}, f32[16,8,128]{2,1,0:T(8,128)S(1)}) custom-call(f32[16,8,128]{2,1,0:T(8,128)S(1)} %all_to_all.22.got_ref, f32[6,128,1024]{2,1,0:T(8,128)S(1)} %get-tuple-element.62.pre_ref, f32[6,128,1024]{2,1,0:T(8,128)S(1)} %get-tuple-element.70.grad_ref, ...), custom_call_target="tpu_custom_call" | custom-call | flops 1000000000 | bytes 4000000 | tf_op jit(solution)/shard_map/pallas_call | solution.py:91
  58.8 9.5 %all_to_all.23.got_ref = f32[16,8,128]{2,1,0:T(8,128)S(1)} all-to-all(f32[16,8,128]{2,1,0:T(8,128)S(1)} %get-tuple-element.75), channel_id=1, replica_groups=mesh['group'=2,'space'=8,'rep'=2] {'space','rep'}, dimensions={0} | all-to-all | bytes 131072 | tf_op jit(solution)/shard_map/all_to_all | solution.py:66
  68.2 2.9 %shard_map.132 = (f32[1280,128]{1,0:T(8,128)S(1)}, f32[1280,128]{1,0:T(8,128)S(1)}, bf16[1280,128]{1,0:T(8,128)(2,1)S(1)}, bf16[1280,128]{1,0:T(8,128)(2,1)S(1)}...) custom-call(f32[16,8,128]{2,1,0:T(8,128)S(1)} %all_to_all.23.got_ref, ...), custom_call_target="tpu_custom_call" | custom-call | flops 1000000000 | bytes 4000000 | tf_op jit(solution)/shard_map/pallas_call | solution.py:91
  71.3 0.4 collective-permute-start.4
  71.7 1.2 %collective-permute-done.8 = bf16[1280,128]{1,0:T(8,128)(2,1)} collective-permute-done((bf16[1280,128]{1,0:T(8,128)(2,1)S(1)}, bf16[1280,128]{1,0:T(8,128)(2,1)}, u32[]{:S(2)}, u32[]{:S(2)}) %collective-permute-start.8) | collective-permute-done | bytes 327712 | tf_op jit(solution)/shard_map/ppermute | solution.py:37
  72.9 1.0 convert_add_fusion
  74.0 0.2 collective-permute-start.9
  74.3 0.7 collective-permute-start.5
  75.0 5.3 %collective-permute-done.9 = bf16[640,128]{1,0:T(8,128)(2,1)S(1)} collective-permute-done((bf16[640,128]{1,0:T(8,128)(2,1)S(1)}, bf16[640,128]{1,0:T(8,128)(2,1)S(1)}, u32[]{:S(2)}, u32[]{:S(2)}) %collective-permute-start.9) | collective-permute-done | bytes 163872 | tf_op jit(solution)/shard_map/ppermute | solution.py:37
  80.4 0.2 collective-permute-start.10
  80.6 1.7 %collective-permute-start.6 = (bf16[320,128]{1,0:T(8,128)(2,1)S(1)}, bf16[320,128]{1,0:T(8,128)(2,1)S(1)}, u32[]{:S(2)}, u32[]{:S(2)}) collective-permute-start(bf16[320,128]{1,0:T(8,128)(2,1)S(1)} %dynamic-slice_convert_fusion.3), channel_id=1, source_target_pairs={{0,4},{2,6},{4,0},{6,2},{8,12},{10,14},{12,8},{14,10},{1,5},{3,7},... | collective-permute-start | bytes 245768 | tf_op jit(solution)/shard_map/ppermute | solution.py:37
  82.3 2.5 %collective-permute-done.10 = bf16[320,128]{1,0:T(8,128)(2,1)S(1)} collective-permute-done((bf16[320,128]{1,0:T(8,128)(2,1)S(1)}, bf16[320,128]{1,0:T(8,128)(2,1)S(1)}, u32[]{:S(2)}, u32[]{:S(2)}) %collective-permute-start.10) | collective-permute-done | bytes 81952 | tf_op jit(solution)/shard_map/ppermute | solution.py:37
  84.9 0.3 collective-permute-start.11
  85.2 2.8 %collective-permute-start.7 = (bf16[160,128]{1,0:T(8,128)(2,1)S(1)}, bf16[160,128]{1,0:T(8,128)(2,1)S(1)}, u32[]{:S(2)}, u32[]{:S(2)}) collective-permute-start(bf16[160,128]{1,0:T(8,128)(2,1)S(1)} %dynamic-slice_convert_fusion.5), channel_id=1, source_target_pairs={{0,8},{2,10},{4,12},{6,14},{8,0},{10,2},{12,4},{14,6},{1,9},{3,11}... | collective-permute-start | bytes 122888 | tf_op jit(solution)/shard_map/ppermute | solution.py:37
  88.0 2.0 %collective-permute-done.11 = bf16[160,128]{1,0:T(8,128)(2,1)S(1)} collective-permute-done((bf16[160,128]{1,0:T(8,128)(2,1)S(1)}, bf16[160,128]{1,0:T(8,128)(2,1)S(1)}, u32[]{:S(2)}, u32[]{:S(2)}) %collective-permute-start.11) | collective-permute-done | bytes 40992 | tf_op jit(solution)/shard_map/ppermute | solution.py:37
  90.1 0.4 collective-permute-done.7
  90.5 2.6 %collective-permute-start.14 = (bf16[160,128]{1,0:T(8,128)(2,1)S(1)}, bf16[160,128]{1,0:T(8,128)(2,1)S(1)}, u32[]{:S(2)}, u32[]{:S(2)}) collective-permute-start(bf16[160,128]{1,0:T(8,128)(2,1)S(1)} %add_convert_fusion), channel_id=1, source_target_pairs={{0,8},{2,10},{4,12},{6,14},{8,0},{10,2},{12,4},{14,6},{1,9},{3,11}... | collective-permute-start | bytes 122888 | tf_op jit(solution)/shard_map/ppermute | solution.py:37
  93.1 0.4 collective-permute-start.12
  93.5 2.0 %collective-permute-start.16 = (bf16[128,256]{1,0:T(8,128)(2,1)S(1)}, bf16[128,256]{1,0:T(8,128)(2,1)S(1)}, u32[]{:S(2)}, u32[]{:S(2)}) collective-permute-start(bf16[128,256]{1,0:T(8,128)(2,1)S(1)} %get-tuple-element.90), channel_id=1, source_target_pairs={{0,2},{2,0},{4,6},{6,4},{8,10},{10,8},{12,14},{14,12},{1,3},{3,1},... | collective-permute-start | bytes 196616 | tf_op jit(solution)/shard_map/ppermute | solution.py:37
  95.5 0.7 collective-permute-start.17
  96.2 3.1 %collective-permute-start.15 = (bf16[320,128]{1,0:T(8,128)(2,1)S(1)}, bf16[320,128]{1,0:T(8,128)(2,1)S(1)}, u32[]{:S(2)}, u32[]{:S(2)}) collective-permute-start(bf16[320,128]{1,0:T(8,128)(2,1)S(1)} %maximum_select_fusion.5), channel_id=1, source_target_pairs={{0,2},{2,0},{4,6},{6,4},{8,10},{10,8},{12,14},{14,12},{1,3},{3,1},... | collective-permute-start | bytes 245768 | tf_op jit(solution)/shard_map/ppermute | solution.py:37
  99.4 0.9 collective-permute-start.13
  100.3 1.5 %collective-permute-done.15 = bf16[320,128]{1,0:T(8,128)(2,1)S(1)} collective-permute-done((bf16[320,128]{1,0:T(8,128)(2,1)S(1)}, bf16[320,128]{1,0:T(8,128)(2,1)S(1)}, u32[]{:S(2)}, u32[]{:S(2)}) %collective-permute-start.15) | collective-permute-done | bytes 81952 | tf_op jit(solution)/shard_map/ppermute | solution.py:37
  101.8 2.1 %collective-permute-done.13 = bf16[320,128]{1,0:T(8,128)(2,1)S(1)} collective-permute-done((bf16[320,128]{1,0:T(8,128)(2,1)S(1)}, bf16[320,128]{1,0:T(8,128)(2,1)S(1)}, u32[]{:S(2)}, u32[]{:S(2)}) %collective-permute-start.13) | collective-permute-done | bytes 81952 | tf_op jit(solution)/shard_map/ppermute | solution.py:37
  103.9 1.2 %collective-permute-start.19 = (bf16[640,128]{1,0:T(8,128)(2,1)S(1)}, bf16[640,128]{1,0:T(8,128)(2,1)S(1)}, u32[]{:S(2)}, u32[]{:S(2)}) collective-permute-start(bf16[640,128]{1,0:T(8,128)(2,1)S(1)} %maximum_select_fusion.3), channel_id=1, source_target_pairs={{0,4},{2,6},{4,0},{6,2},{8,12},{10,14},{12,8},{14,10},{1,5},{3,7},... | collective-permute-start | bytes 491528 | tf_op jit(solution)/shard_map/ppermute | solution.py:37
  105.2 1.5 %collective-permute-start.18 = (bf16[640,128]{1,0:T(8,128)(2,1)S(1)}, bf16[640,128]{1,0:T(8,128)(2,1)S(1)}, u32[]{:S(2)}, u32[]{:S(2)}) collective-permute-start(bf16[640,128]{1,0:T(8,128)(2,1)S(1)} %maximum_select_fusion.2), channel_id=1, source_target_pairs={{0,2},{2,0},{4,6},{6,4},{8,10},{10,8},{12,14},{14,12},{1,3},{3,1},... | collective-permute-start | bytes 491528 | tf_op jit(solution)/shard_map/ppermute | solution.py:37
  106.6 1.5 %shard_map.133 = bf16[128,4096]{1,0:T(8,128)(2,1)S(1)} custom-call(bf16[4,128,1024]{2,1,0:T(8,128)(2,1)S(1)} %get-tuple-element.88.feat_ref), custom_call_target="tpu_custom_call" | custom-call | flops 1000000000 | bytes 4000000 | tf_op jit(solution)/shard_map/pallas_call | solution.py:91
  108.1 1.8 %copy.20 = bf16[4,32,4096]{2,0,1:T(4,128)(2,1)} copy(bf16[4,32,4096]{2,1,0:T(8,128)(2,1)S(1)} %bitcast.28) | data formatting | bytes 2097152 | tf_op jit(solution)/shard_map/reshape | solution.py:701
  109.9 0.1 maximum_select_fusion.1.own_b_ref
  110.0 0.5 collective-permute-done.18
  110.5 0.1 maximum_select_fusion.own_a_ref
  110.7 0.5 collective-permute-start.21
  111.2 0.6 slice.15
  111.8 0.6 slice.14
  112.3 0.8 copy.16
  113.1 2.1 %shard_map.134 = (f32[4096,128]{1,0:T(8,128)}, f32[2048,64]{1,0:T(8,128)}) custom-call(bf16[1280,128]{1,0:T(8,128)(2,1)S(1)} %maximum_select_fusion.own_a_ref, bf16[1280,128]{1,0:T(8,128)(2,1)S(1)} %maximum_select_fusion.1.own_b_ref, bf16[1280,128]{1,0:T(8,128)(2,1)S(1)} %collective-permute-done.20.other_a_ref, ...), custom_call_target="tpu_custom_call" | custom-call | flops 1000000000 | bytes 4000000 | tf_op jit(solution)/shard_map/pallas_call | solution.py:91
  (49 shorter events, 0.7 us)
Async XLA Ops:
  0.6 10.7 %copy-start.1 = (bf16[64,64,128]{2,1,0:T(8,128)(2,1)S(1)}, bf16[64,64,128]{2,1,0:T(8,128)(2,1)}, u32[]{:S(2)}) copy-start(bf16[64,64,128]{2,1,0:T(8,128)(2,1)} %param.9) | copy-start | bytes 3145732
  0.6 10.7 %copy-start.2 = (bf16[64,32,64]{2,1,0:T(8,128)(2,1)S(1)}, bf16[64,32,64]{2,1,0:T(8,128)(2,1)}, u32[]{:S(2)}) copy-start(bf16[64,32,64]{2,1,0:T(8,128)(2,1)} %param.12) | copy-start | bytes 786436
  0.7 10.7 %copy-start.3 = (f32[64]{0:T(128)S(1)}, f32[64]{0:T(128)}, u32[]{:S(2)}) copy-start(f32[64]{0:T(128)} %param.10) | copy-start | bytes 772
  0.7 10.7 %copy-start.4 = (f32[64]{0:T(128)S(1)}, f32[64]{0:T(128)}, u32[]{:S(2)}) copy-start(f32[64]{0:T(128)} %param.11) | copy-start | bytes 772
  0.7 10.7 %copy-start.5 = (f32[32]{0:T(128)S(1)}, f32[32]{0:T(128)}, u32[]{:S(2)}) copy-start(f32[32]{0:T(128)} %param.13) | copy-start | bytes 388
  0.7 10.7 %copy-start.6 = (f32[32]{0:T(128)S(1)}, f32[32]{0:T(128)}, u32[]{:S(2)}) copy-start(f32[32]{0:T(128)} %param.14) | copy-start | bytes 388
  0.7 12.7 %collective-permute-start = (bf16[128,256]{1,0:T(8,128)(2,1)}, bf16[128,256]{1,0:T(8,128)(2,1)S(1)}, u32[]{:S(2)}, u32[]{:S(2)}) collective-permute-start(bf16[128,256]{1,0:T(8,128)(2,1)} %bitcast.29), channel_id=1, source_target_pairs={{0,2},{2,0},{4,6},{6,4},{8,10},{10,8},{12,14},{14,12},{1,3},{3,1},... | collective-permute-start | bytes 196616 | tf_op jit(solution)/shard_map/ppermute | solution.py:37
  3.7 9.6 %collective-permute-start.1 = (bf16[128,256]{1,0:T(8,128)(2,1)}, bf16[128,256]{1,0:T(8,128)(2,1)S(1)}, u32[]{:S(2)}, u32[]{:S(2)}) collective-permute-start(bf16[128,256]{1,0:T(8,128)(2,1)} %bitcast.30), channel_id=1, source_target_pairs={{2,4},{6,8},{10,12},{4,2},{8,6},{12,10},{3,5},{7,9},{11,13},{5,3},... | collective-permute-start | bytes 196616 | tf_op jit(solution)/shard_map/ppermute | solution.py:80
  6.2 7.2 %copy-start = (bf16[1,128,1,256]{3,1,2,0:T(8,128)(2,1)S(1)}, bf16[1,128,1,256]{3,1,2,0:T(8,128)(2,1)}, u32[]{:S(2)}) copy-start(bf16[1,128,1,256]{3,1,2,0:T(8,128)(2,1)} %param.8) | copy-start | bytes 196612
  6.3 26.4 %collective-permute-start.2 = (bf16[32,4096]{1,0:T(8,128)(2,1)S(1)}, bf16[32,4096]{1,0:T(8,128)(2,1)S(1)}, u32[]{:S(2)}, u32[]{:S(2)}) collective-permute-start(bf16[32,4096]{1,0:T(8,128)(2,1)S(1)} %get-tuple-element.109), channel_id=1, source_target_pairs={{0,2},{2,0},{4,6},{6,4},{8,10},{10,8},{12,14},{14,12},{1,3},{3,1},... | collective-permute-start | bytes 786440 | tf_op jit(solution)/shard_map/ppermute | solution.py:37
  10.6 22.0 %collective-permute-start.3 = (bf16[32,4096]{1,0:T(8,128)(2,1)S(1)}, bf16[32,4096]{1,0:T(8,128)(2,1)S(1)}, u32[]{:S(2)}, u32[]{:S(2)}) collective-permute-start(bf16[32,4096]{1,0:T(8,128)(2,1)S(1)} %get-tuple-element.108), channel_id=1, source_target_pairs={{2,4},{6,8},{10,12},{4,2},{8,6},{12,10},{3,5},{7,9},{11,13},{5,3},... | collective-permute-start | bytes 786440 | tf_op jit(solution)/shard_map/ppermute | solution.py:80
  71.1 1.8 %collective-permute-start.8 = (bf16[1280,128]{1,0:T(8,128)(2,1)S(1)}, bf16[1280,128]{1,0:T(8,128)(2,1)}, u32[]{:S(2)}, u32[]{:S(2)}) collective-permute-start(bf16[1280,128]{1,0:T(8,128)(2,1)S(1)} %get-tuple-element.85), channel_id=1, source_target_pairs={{0,1},{1,0},{2,3},{3,2},{4,5},{5,4},{6,7},{7,6},{8,9},{9,8},{10,11... | collective-permute-start | bytes 983048 | tf_op jit(solution)/shard_map/ppermute | solution.py:37
  71.3 2.9 %collective-permute-start.4 = (bf16[1280,128]{1,0:T(8,128)(2,1)S(1)}, bf16[1280,128]{1,0:T(8,128)(2,1)S(1)}, u32[]{:S(2)}, u32[]{:S(2)}) collective-permute-start(bf16[1280,128]{1,0:T(8,128)(2,1)S(1)} %get-tuple-element.83), channel_id=1, source_target_pairs={{0,1},{1,0},{2,3},{3,2},{4,5},{5,4},{6,7},{7,6},{8,9},{9,8},{10,11... | collective-permute-start | bytes 983048 | tf_op jit(solution)/shard_map/ppermute | solution.py:37
  74.0 6.3 %collective-permute-start.9 = (bf16[640,128]{1,0:T(8,128)(2,1)S(1)}, bf16[640,128]{1,0:T(8,128)(2,1)S(1)}, u32[]{:S(2)}, u32[]{:S(2)}) collective-permute-start(bf16[640,128]{1,0:T(8,128)(2,1)S(1)} %dynamic-slice_convert_fusion), channel_id=1, source_target_pairs={{0,4},{2,6},{4,0},{6,2},{8,12},{10,14},{12,8},{14,10},{1,5},{3,7},... | collective-permute-start | bytes 491528 | tf_op jit(solution)/shard_map/ppermute | solution.py:37
  74.3 6.3 %collective-permute-start.5 = (bf16[640,128]{1,0:T(8,128)(2,1)S(1)}, bf16[640,128]{1,0:T(8,128)(2,1)S(1)}, u32[]{:S(2)}, u32[]{:S(2)}) collective-permute-start(bf16[640,128]{1,0:T(8,128)(2,1)S(1)} %dynamic-slice_convert_fusion.1), channel_id=1, source_target_pairs={{0,2},{2,0},{4,6},{6,4},{8,10},{10,8},{12,14},{14,12},{1,3},{3,1},... | collective-permute-start | bytes 491528 | tf_op jit(solution)/shard_map/ppermute | solution.py:37
  80.4 4.5 %collective-permute-start.10 = (bf16[320,128]{1,0:T(8,128)(2,1)S(1)}, bf16[320,128]{1,0:T(8,128)(2,1)S(1)}, u32[]{:S(2)}, u32[]{:S(2)}) collective-permute-start(bf16[320,128]{1,0:T(8,128)(2,1)S(1)} %dynamic-slice_convert_fusion.2), channel_id=1, source_target_pairs={{0,2},{2,0},{4,6},{6,4},{8,10},{10,8},{12,14},{14,12},{1,3},{3,1},... | collective-permute-start | bytes 245768 | tf_op jit(solution)/shard_map/ppermute | solution.py:37
  80.6 4.6 %collective-permute-start.6 = (bf16[320,128]{1,0:T(8,128)(2,1)S(1)}, bf16[320,128]{1,0:T(8,128)(2,1)S(1)}, u32[]{:S(2)}, u32[]{:S(2)}) collective-permute-start(bf16[320,128]{1,0:T(8,128)(2,1)S(1)} %dynamic-slice_convert_fusion.3), channel_id=1, source_target_pairs={{0,4},{2,6},{4,0},{6,2},{8,12},{10,14},{12,8},{14,10},{1,5},{3,7},... | collective-permute-start | bytes 245768 | tf_op jit(solution)/shard_map/ppermute | solution.py:37
  84.9 5.1 %collective-permute-start.11 = (bf16[160,128]{1,0:T(8,128)(2,1)S(1)}, bf16[160,128]{1,0:T(8,128)(2,1)S(1)}, u32[]{:S(2)}, u32[]{:S(2)}) collective-permute-start(bf16[160,128]{1,0:T(8,128)(2,1)S(1)} %dynamic-slice_convert_fusion.4), channel_id=1, source_target_pairs={{0,8},{2,10},{4,12},{6,14},{8,0},{10,2},{12,4},{14,6},{1,9},{3,11}... | collective-permute-start | bytes 122888 | tf_op jit(solution)/shard_map/ppermute | solution.py:37
  85.2 5.2 %collective-permute-start.7 = (bf16[160,128]{1,0:T(8,128)(2,1)S(1)}, bf16[160,128]{1,0:T(8,128)(2,1)S(1)}, u32[]{:S(2)}, u32[]{:S(2)}) collective-permute-start(bf16[160,128]{1,0:T(8,128)(2,1)S(1)} %dynamic-slice_convert_fusion.5), channel_id=1, source_target_pairs={{0,8},{2,10},{4,12},{6,14},{8,0},{10,2},{12,4},{14,6},{1,9},{3,11}... | collective-permute-start | bytes 122888 | tf_op jit(solution)/shard_map/ppermute | solution.py:37
  90.5 5.7 %collective-permute-start.14 = (bf16[160,128]{1,0:T(8,128)(2,1)S(1)}, bf16[160,128]{1,0:T(8,128)(2,1)S(1)}, u32[]{:S(2)}, u32[]{:S(2)}) collective-permute-start(bf16[160,128]{1,0:T(8,128)(2,1)S(1)} %add_convert_fusion), channel_id=1, source_target_pairs={{0,8},{2,10},{4,12},{6,14},{8,0},{10,2},{12,4},{14,6},{1,9},{3,11}... | collective-permute-start | bytes 122888 | tf_op jit(solution)/shard_map/ppermute | solution.py:37
  93.1 6.2 %collective-permute-start.12 = (bf16[160,128]{1,0:T(8,128)(2,1)S(1)}, bf16[160,128]{1,0:T(8,128)(2,1)S(1)}, u32[]{:S(2)}, u32[]{:S(2)}) collective-permute-start(bf16[160,128]{1,0:T(8,128)(2,1)S(1)} %add_convert_fusion.1), channel_id=1, source_target_pairs={{0,8},{2,10},{4,12},{6,14},{8,0},{10,2},{12,4},{14,6},{1,9},{3,11}... | collective-permute-start | bytes 122888 | tf_op jit(solution)/shard_map/ppermute | solution.py:37
  93.5 11.6 %collective-permute-start.16 = (bf16[128,256]{1,0:T(8,128)(2,1)S(1)}, bf16[128,256]{1,0:T(8,128)(2,1)S(1)}, u32[]{:S(2)}, u32[]{:S(2)}) collective-permute-start(bf16[128,256]{1,0:T(8,128)(2,1)S(1)} %get-tuple-element.90), channel_id=1, source_target_pairs={{0,2},{2,0},{4,6},{6,4},{8,10},{10,8},{12,14},{14,12},{1,3},{3,1},... | collective-permute-start | bytes 196616 | tf_op jit(solution)/shard_map/ppermute | solution.py:37
  95.5 9.6 %collective-permute-start.17 = (bf16[128,256]{1,0:T(8,128)(2,1)S(1)}, bf16[128,256]{1,0:T(8,128)(2,1)S(1)}, u32[]{:S(2)}, u32[]{:S(2)}) collective-permute-start(bf16[128,256]{1,0:T(8,128)(2,1)S(1)} %get-tuple-element.91), channel_id=1, source_target_pairs={{2,4},{6,8},{10,12},{4,2},{8,6},{12,10},{3,5},{7,9},{11,13},{5,3},... | collective-permute-start | bytes 196616 | tf_op jit(solution)/shard_map/ppermute | solution.py:80
  96.2 5.6 %collective-permute-start.15 = (bf16[320,128]{1,0:T(8,128)(2,1)S(1)}, bf16[320,128]{1,0:T(8,128)(2,1)S(1)}, u32[]{:S(2)}, u32[]{:S(2)}) collective-permute-start(bf16[320,128]{1,0:T(8,128)(2,1)S(1)} %maximum_select_fusion.5), channel_id=1, source_target_pairs={{0,2},{2,0},{4,6},{6,4},{8,10},{10,8},{12,14},{14,12},{1,3},{3,1},... | collective-permute-start | bytes 245768 | tf_op jit(solution)/shard_map/ppermute | solution.py:37
  99.4 4.5 %collective-permute-start.13 = (bf16[320,128]{1,0:T(8,128)(2,1)S(1)}, bf16[320,128]{1,0:T(8,128)(2,1)S(1)}, u32[]{:S(2)}, u32[]{:S(2)}) collective-permute-start(bf16[320,128]{1,0:T(8,128)(2,1)S(1)} %maximum_select_fusion.4), channel_id=1, source_target_pairs={{0,4},{2,6},{4,0},{6,2},{8,12},{10,14},{12,8},{14,10},{1,5},{3,7},... | collective-permute-start | bytes 245768 | tf_op jit(solution)/shard_map/ppermute | solution.py:37
  103.9 6.0 %collective-permute-start.19 = (bf16[640,128]{1,0:T(8,128)(2,1)S(1)}, bf16[640,128]{1,0:T(8,128)(2,1)S(1)}, u32[]{:S(2)}, u32[]{:S(2)}) collective-permute-start(bf16[640,128]{1,0:T(8,128)(2,1)S(1)} %maximum_select_fusion.3), channel_id=1, source_target_pairs={{0,4},{2,6},{4,0},{6,2},{8,12},{10,14},{12,8},{14,10},{1,5},{3,7},... | collective-permute-start | bytes 491528 | tf_op jit(solution)/shard_map/ppermute | solution.py:37
  105.2 5.4 %collective-permute-start.18 = (bf16[640,128]{1,0:T(8,128)(2,1)S(1)}, bf16[640,128]{1,0:T(8,128)(2,1)S(1)}, u32[]{:S(2)}, u32[]{:S(2)}) collective-permute-start(bf16[640,128]{1,0:T(8,128)(2,1)S(1)} %maximum_select_fusion.2), channel_id=1, source_target_pairs={{0,2},{2,0},{4,6},{6,4},{8,10},{10,8},{12,14},{14,12},{1,3},{3,1},... | collective-permute-start | bytes 491528 | tf_op jit(solution)/shard_map/ppermute | solution.py:37
  110.6 2.5 %collective-permute-start.20 = (bf16[1280,128]{1,0:T(8,128)(2,1)S(1)}, bf16[1280,128]{1,0:T(8,128)(2,1)S(1)}, u32[]{:S(2)}, u32[]{:S(2)}) collective-permute-start(bf16[1280,128]{1,0:T(8,128)(2,1)S(1)} %maximum_select_fusion.own_a_ref), channel_id=1, source_target_pairs={{0,1},{1,0},{2,3},{3,2},{4,5},{5,4},{6,7},{7,6},{8,9},{9,8},{10,11... | collective-permute-start | bytes 983048 | tf_op jit(solution)/shard_map/ppermute | solution.py:37
  110.7 2.4 %collective-permute-start.21 = (bf16[1280,128]{1,0:T(8,128)(2,1)S(1)}, bf16[1280,128]{1,0:T(8,128)(2,1)S(1)}, u32[]{:S(2)}, u32[]{:S(2)}) collective-permute-start(bf16[1280,128]{1,0:T(8,128)(2,1)S(1)} %maximum_select_fusion.1.own_b_ref), channel_id=1, source_target_pairs={{0,1},{1,0},{2,3},{3,2},{4,5},{5,4},{6,7},{7,6},{8,9},{9,8},{10,11... | collective-permute-start | bytes 983048 | tf_op jit(solution)/shard_map/ppermute | solution.py:37

commit v4 on v3

--- a/solution.py
+++ b/solution.py
@@ -43,7 +43,7 @@
     while bit < lax.axis_size("space"):
         bits.append(("space", bit))
         bit *= 2
-    return bits, bits[1:2] + bits[0:1] + bits[2:]
+    return bits[1:2] + bits[0:1] + bits[2:], bits
 
 
 def halve(part, axis, bit):
@@ -250,7 +250,9 @@
     near_ref[1] = jnp.where(even, inner_ref[...], outer_ref[...])
     planes = jnp.concatenate([near_ref[0], lat_ref[...], near_ref[1]], axis=0)
     for k in range(9):
-        moved = matmul(planes, sh_ref[:, k * CELLS : (k + 1) * CELLS]).astype(BF16)
+        moved = planes
+        if k != 4:
+            moved = matmul(planes, sh_ref[:, k * CELLS : (k + 1) * CELLS]).astype(BF16)
         for z in range(3):
             at = (z * 9 + k) * C0
             x_ref[at : at + C0, :] = moved[z * C0 : (z + 1) * C0]
@@ -482,17 +484,24 @@
         ) + jnp.concatenate(high, axis=1)
 
 
-def first_dpre(grad, pre, cols):
+def first_windows(x_ref, grad_ref, pre_ref, cols, sh_ref):
     mean, scale, gain = (cols[0:C1, k : k + 1] for k in range(3))
-    hat_part, part = cols[0:C1, 6:7], cols[0:C1, 7:8]
-    return (gain * scale * (grad - part - (pre - mean) * scale * hat_part)).astype(BF16)
-
-
-def first_windows(x_ref, base, grad_ref, pre_ref, cols, sh_ref):
+    factor = gain * scale
+    slant, offset = factor * scale * cols[0:C1, 6:7], factor * cols[0:C1, 7:8]
     for block in range(4):
         rp, cp = block // 2, block % 2
         rows = slice(block * C1, (block + 1) * C1)
-        dpre = first_dpre(grad_ref[rows, :], pre_ref[rows, :], cols)
+        dpre = jnp.concatenate(
+            [
+                (
+                    factor * grad_ref[j, rows, :]
+                    - offset
+                    - (pre_ref[j + 1, rows, :] - mean) * slant
+                ).astype(BF16)
+                for j in range(2)
+            ],
+            axis=0,
+        )
         for q, (trp, dj) in enumerate(TAP_PHASES):
             for r, (tcp, dl) in enumerate(TAP_PHASES):
                 if (trp, tcp) != (rp, cp):
@@ -500,41 +509,40 @@
                 moved = dpre
                 if (dj, dl) != (0, 0):
                     moved = matmul(dpre, sh_ref[:, shift_slot(dj, dl)]).astype(BF16)
-                at = base + (4 * q + r) * C1
-                x_ref[at : at + C1, :] = moved
+                for j in range(2):
+                    at = (16 * j + 4 * q + r) * C1
+                    x_ref[at : at + C1, :] = moved[j * C1 : (j + 1) * C1]
+
+
+def weight_half(half, x_ref, lat_ref, near_ref, dw2_ref, a_ref, b_ref):
+    taps = 16 * C1
+    chunk = a_ref.shape[0]
+    fields = (
+        jnp.where(half == 0, near_ref[1], lat_ref[...]),
+        jnp.where(half == 0, lat_ref[...], near_ref[0]),
+    )
+    a_ref[0:taps, :] = matmul_nt(x_ref[taps:, :], fields[0]).astype(a_ref.dtype)
+    split = chunk - taps
+    a_ref[taps:, :] = matmul_nt(x_ref[0:split, :], fields[1]).astype(a_ref.dtype)
+    b_ref[0 : taps - split, :] = matmul_nt(x_ref[split:taps, :], fields[1]).astype(b_ref.dtype)
+    rest = chunk - taps + split
+    at = pl.multiple_of(half * rest, rest)
+    b_ref[taps - split :, :] = dw2_ref[pl.ds(at, rest), :].astype(b_ref.dtype)
 
 
 def fifth_kernel(
     got_ref, g1_ref, pre1_ref, st1_ref, sh_ref, lat_ref, near_ref, dw2_ref, b1_ref,
-    keep_a_ref, keep_b_ref, send_a_ref, send_b_ref, sum_ref, mid_ref, inner_ref, outer_ref,
-    x_ref, dw_ref, out_ref, sem,
+    send_a_ref, send_b_ref, keep_a_ref, keep_b_ref, sum_ref, mid_ref, inner_ref, outer_ref,
+    x_ref,
 ):
     sums = jnp.sum(got_ref[...], axis=0)
     sum_ref[...] = sums
     total = got_ref.shape[0] * 8 * CELLS
     cols = columns(jnp.concatenate([st1_ref[0:6], sums[0:2] / total], axis=0))
-    for j in range(2):
-        first_windows(x_ref, j * 16 * C1, g1_ref.at[j], pre1_ref.at[j + 1], cols, sh_ref)
-    fields = (near_ref[1], lat_ref[...], lat_ref[...], near_ref[0])
-    for p, j, field in ((0, 1, fields[0]), (1, 0, fields[1]), (2, 1, fields[2]), (3, 0, fields[3])):
-        for half in range(2):
-            at = p * 16 * C1 + half * 8 * C1
-            src = j * 16 * C1 + half * 8 * C1
-            dw_ref[at : at + 8 * C1, :] = matmul_nt(x_ref[src : src + 8 * C1, :], field)
-    dw_ref[64 * C1 :, :] = dw2_ref[...]
-    chunk = dw_ref.shape[0] // 4
+    first_windows(x_ref, g1_ref, pre1_ref, cols, sh_ref)
     core = lax.axis_index("rep")
-    mine = pl.multiple_of(core * (2 * chunk), 2 * chunk)
-    theirs = pl.multiple_of((1 - core) * (2 * chunk), 2 * chunk)
-    out_ref[...] = dw_ref[pl.ds(theirs, 2 * chunk), :].astype(BF16)
-    copies = [
-        pltpu.make_async_copy(out_ref.at[0:chunk], send_a_ref, sem.at[0]),
-        pltpu.make_async_copy(out_ref.at[chunk:], send_b_ref, sem.at[1]),
-        pltpu.make_async_copy(dw_ref.at[pl.ds(mine, chunk)], keep_a_ref, sem.at[2]),
-        pltpu.make_async_copy(dw_ref.at[pl.ds(mine + chunk, chunk)], keep_b_ref, sem.at[3]),
-    ]
-    for copy in copies:
-        copy.start()
+    weight_half(core, x_ref, lat_ref, near_ref, dw2_ref, keep_a_ref, keep_b_ref)
+    weight_half(1 - core, x_ref, lat_ref, near_ref, dw2_ref, send_a_ref, send_b_ref)
     pieces = [
         matmul(b1_ref[:, p * 16 * C1 : (p + 1) * 16 * C1], x_ref[j * 16 * C1 : (j + 1) * 16 * C1, :])
         for p, j in ((0, 1), (1, 0), (2, 1), (3, 0))
@@ -544,22 +552,38 @@
     even = is_even()
     inner_ref[...] = jnp.where(even, up, down)
     outer_ref[...] = jnp.where(even, down, up)
+
+
+def last_kernel(
+    own_a_ref, own_b_ref, other_a_ref, other_b_ref, dw1_far, dw2_far, x_ref, y_ref, sem
+):
+    core = lax.axis_index("rep")
+    chunk = own_a_ref.shape[0]
+    rest = 16 * C2
+    kept = chunk - rest
+    copies = []
+
+    def send(src, dst):
+        copies.append(pltpu.make_async_copy(src, dst, sem.at[len(copies)]))
+        copies[-1].start()
+
+    for half in range(2):
+        at = half * (chunk + kept)
+        x_ref[at : at + chunk, :] = jnp.where(
+            core == half, own_a_ref[...], other_a_ref[...]
+        ).astype(F32)
+        send(x_ref.at[at : at + chunk], dw1_far.at[at : at + chunk])
+        last = jnp.where(core == half, own_b_ref[...], other_b_ref[...]).astype(F32)
+        x_ref[at + chunk : at + chunk + kept, :] = last[0:kept]
+        send(
+            x_ref.at[at + chunk : at + chunk + kept], dw1_far.at[at + chunk : at + chunk + kept]
+        )
+        for k in range(2):
+            row = half * rest + k * 2 * rest
+            y_ref[row : row + rest, :] = last[kept:, k * C1 : (k + 1) * C1]
+            send(y_ref.at[row : row + rest], dw2_far.at[row : row + rest])
     for copy in copies:
         copy.wait()
-
-
-def last_kernel(own_a_ref, own_b_ref, other_a_ref, other_b_ref, dw1_ref, dw2_ref, x_ref):
-    core = lax.axis_index("rep")
-    chunk = own_a_ref.shape[0]
-    mine = pl.multiple_of(core * (2 * chunk), 2 * chunk)
-    theirs = pl.multiple_of((1 - core) * (2 * chunk), 2 * chunk)
-    x_ref[pl.ds(mine, chunk), :] = own_a_ref[...].astype(F32)
-    x_ref[pl.ds(mine + chunk, chunk), :] = own_b_ref[...].astype(F32)
-    x_ref[pl.ds(theirs, chunk), :] = other_a_ref[...].astype(F32)
-    x_ref[pl.ds(theirs + chunk, chunk), :] = other_b_ref[...].astype(F32)
-    dw1_ref[...] = x_ref[0 : 64 * C1, :]
-    dw2_ref[0 : 32 * C2, :] = x_ref[64 * C1 :, 0:C1]
-    dw2_ref[32 * C2 :, :] = x_ref[64 * C1 :, C1:]
 
 
 def local(
@@ -662,13 +686,13 @@
     )
     got = exchange(out)
     rows = (64 * C1 + 32 * C2) // 4
-    keep_a, keep_b, send_a, send_b, sum1, mid, lat_in, lat_out = call(
+    send_a, send_b, keep_a, keep_b, sum1, mid, lat_in, lat_out = call(
         fifth_kernel,
         [
+            ((rows, C0), BF16),
+            ((rows, C0), BF16),
             ((rows, C0), F32),
             ((rows, C0), F32),
-            ((rows, C0), BF16),
-            ((rows, C0), BF16),
             ((8, 128), F32),
             ((C0, CELLS), F32),
             ((C0, CELLS), BF16),
@@ -677,16 +701,10 @@
         [got, grad1, pre1, st1, sh, lat, near, dw2, b1],
         [
             pltpu.VMEM((32 * C1, CELLS), BF16),
-            pltpu.VMEM((4 * rows, C0), F32),
-            pltpu.VMEM((2 * rows, C0), BF16),
-            pltpu.SemaphoreType.DMA((4,)),
-        ],
-        far=range(4),
-    )
-    parts = [
-        keep_a + swap(send_a, "rep", 1).astype(F32),
-        keep_b + swap(send_b, "rep", 1).astype(F32),
-    ]
+        ],
+    )
+    sent_a, sent_b = swap(send_a, "rep", 1), swap(send_b, "rep", 1)
+    parts = [keep_a + sent_a.astype(F32), keep_b + sent_b.astype(F32)]
     orders = chunk_steps()
     steps = len(orders[0])
     for step in range(steps):
@@ -705,7 +723,12 @@
         last_kernel,
         [((64 * C1, C0), F32), ((64 * C2, C1), F32)],
         [part_a, part_b, swap(part_a, "rep", 1), swap(part_b, "rep", 1)],
-        [pltpu.VMEM((4 * rows, C0), F32)],
+        [
+            pltpu.VMEM((64 * C1, C0), F32),
+            pltpu.VMEM((64 * C2, C1), F32),
+            pltpu.SemaphoreType.DMA((8,)),
+        ],
+        far=range(2),
     )
     return (
         features[None],

time: 116 us -> 113 us (0.974)
  Pallas kernels: 21.5 us -> 19.9 us
    pallas_call x8, Pallas kernels: 21.5 us -> 19.9 us  [call(): pl.pallas_call(kernel, out_shape=[jax.ShapeDtypeStruct(shape, dtype) for...]
  transfers between devices with their start and end apart: 22 -> 22, of which waited for: 8 -> 7; matrix products, arithmetic and copies ran while one was open for 6% -> 6% of each run, Pallas kernels for 8% -> 8%
where the time goes in v4:
time: 113 us
  blocking collectives  41.8 us (37%)
  starting transfers between devices  27.7 us (25%)
  Pallas kernels  19.9 us (18%)
  waiting for transfers between devices  15.2 us (13%)
  local copies, waits for them, and re-layouts  5.66 us (5%)
  other arithmetic  1.58 us (1%)
  between operations  1.29 us (1%)
    all_to_all x4, blocking collectives, exchange(): return lax.all_to_all(copies, GROUP, 0, 0)  41.8 us
    ppermute x19, starting transfers between devices, swap(): lax.ppermute(block, axis, [(i, i ^ bit) for i in range(lax.axis_size(axis...  25.7 us
    pallas_call x8, Pallas kernels, call(): pl.pallas_call(kernel, out_shape=[jax.ShapeDtypeStruct(shape, dtype) for...  19.9 us
    ppermute x19, waiting for transfers between devices, swap(): lax.ppermute(block, axis, [(i, i ^ bit) for i in range(lax.axis_size(axis...  15.2 us
    unnamed x16, local copies, waits for them, and re-layouts  2.63 us
  transfers between devices with their start and end apart: 22, of which 7 were waited for; matrix products, arithmetic and copies ran while one was open for 6% of the time, Pallas kernels for 8%

profile of v4, /device:TPU:0, one launch (start us, length us, event | category | flops | bytes accessed | tf_op | source)
XLA Modules:
  0.0 113.1 jit_solution(11021617478527346357)
XLA Ops:
  0.7 3.0 %collective-permute-start = (bf16[128,256]{1,0:T(8,128)(2,1)}, bf16[128,256]{1,0:T(8,128)(2,1)S(1)}, u32[]{:S(2)}, u32[]{:S(2)}) collective-permute-start(bf16[128,256]{1,0:T(8,128)(2,1)} %bitcast.29), channel_id=1, source_target_pairs={{0,2},{2,0},{4,6},{6,4},{8,10},{10,8},{12,14},{14,12},{1,3},{3,1},... | collective-permute-start | bytes 196616 | tf_op jit(solution)/shard_map/ppermute | solution.py:37
  3.7 0.7 collective-permute-start.1
  4.4 1.8 %copy.21 = bf16[1,32,4,4096]{3,1,2,0:T(8,128)(2,1)S(1)} copy(bf16[1,32,4,4096]{3,2,1,0:T(4,128)(2,1)} %param.15) | data formatting | bytes 2097152 | tf_op args[7]
  6.3 4.3 %collective-permute-start.2 = (bf16[32,4096]{1,0:T(8,128)(2,1)S(1)}, bf16[32,4096]{1,0:T(8,128)(2,1)S(1)}, u32[]{:S(2)}, u32[]{:S(2)}) collective-permute-start(bf16[32,4096]{1,0:T(8,128)(2,1)S(1)} %get-tuple-element.109), channel_id=1, source_target_pairs={{0,2},{2,0},{4,6},{6,4},{8,10},{10,8},{12,14},{14,12},{1,3},{3,1},... | collective-permute-start | bytes 786440 | tf_op jit(solution)/shard_map/ppermute | solution.py:37
  10.6 0.7 collective-permute-start.3
  11.4 2.0 %shard_map.127 = (bf16[512,2304]{1,0:T(8,128)(2,1)S(1)}, bf16[256,1152]{1,0:T(8,128)(2,1)S(1)}, bf16[128,4096]{1,0:T(8,128)(2,1)S(1)}, bf16[64,2048]{1,0:T(8,128...) custom-call(bf16[4096,128]{1,0:T(8,128)(2,1)S(1)} %bitcast.33, ...), custom_call_target="tpu_custom_call" | custom-call | flops 1000000000 | bytes 4000000 | tf_op jit(solution)/shard_map/pallas_call | solution.py:91
  13.4 2.2 %shard_map.128 = (f32[4,256,256]{2,1,0:T(8,128)S(1)}, f32[16,8,128]{2,1,0:T(8,128)S(1)}, bf16[2,128,256]{2,1,0:T(8,128)(2,1)S(1)}) custom-call(bf16[128,256]{1,0:T(8,128)(2,1)S(1)} %bitcast.31, bf16[128,256]{1,0:T(8,128)(2,1)S(1)} %collective-permute-done.inner_ref, bf16[128,256]{1,0:T(8,128)(2,1)S(1)} %collective-permute-done.1.outer_ref, ...), custom_call_target="tpu_custom_call" | custom-call | flops 1000000000 | bytes 4000000 | tf_op jit(solution)/shard_map/pallas_call | solution.py:91
  15.6 13.4 %all_to_all.20.got_ref = f32[16,8,128]{2,1,0:T(8,128)S(1)} all-to-all(f32[16,8,128]{2,1,0:T(8,128)S(1)} %get-tuple-element.56), channel_id=1, replica_groups=mesh['group'=2,'space'=8,'rep'=2] {'space','rep'}, dimensions={0} | all-to-all | bytes 131072 | tf_op jit(solution)/shard_map/all_to_all | solution.py:66
  28.9 3.7 %shard_map.129 = (f32[6,128,1024]{2,1,0:T(8,128)S(1)}, bf16[128,1024]{1,0:T(8,128)(2,1)S(1)}, f32[8,128]{1,0:T(8,128)S(1)}, f32[16,8,128]{2,1,0:T(8,128)S(1)}) custom-call(f32[16,8,128]{2,1,0:T(8,128)S(1)} %all_to_all.20.got_ref, f32[4,256,256]{2,1,0:T(8,128)S(1)} %get-tuple-element.57.pre1_ref, f32[8,128]{1,0:T(8,128)S(1)} %get-tuple-element.58.p1_ref, ...), custom_call_target="tpu_custom_call" | custom-call | flops 1000000000 | bytes 4000000 | tf_op jit(solution)/shard_map/pallas_call | solution.py:91
  32.6 9.5 %all_to_all.21.got_ref = f32[16,8,128]{2,1,0:T(8,128)S(1)} all-to-all(f32[16,8,128]{2,1,0:T(8,128)S(1)} %get-tuple-element.61), channel_id=1, replica_groups=mesh['group'=2,'space'=8,'rep'=2] {'space','rep'}, dimensions={0} | all-to-all | bytes 131072 | tf_op jit(solution)/shard_map/all_to_all | solution.py:66
  42.1 2.7 %shard_map.130 = (f32[6,128,1024]{2,1,0:T(8,128)S(1)}, bf16[4,128,1024]{2,1,0:T(8,128)(2,1)S(1)}, f32[8,128]{1,0:T(8,128)S(1)}, f32[16,8,128]{2,1,0:T(8,128)S(1)}) custom-call(f32[16,8,128]{2,1,0:T(8,128)S(1)} %all_to_all.21.got_ref, f32[6,128,1024]{2,1,0:T(8,128)S(1)} %get-tuple-element.62.pre_ref, bf16[4,128,1024]{2,1,0:T(8,128)(2,1)S(1)} %get-tuple-element.63.cot_ref, ...), custom_call_target="tpu_custom_call" | custom-call | flops 1000000000 | bytes 4000000 | tf_op jit(solution)/shard_map/pallas_call | solution.py:91
  44.8 9.5 %all_to_all.22.got_ref = f32[16,8,128]{2,1,0:T(8,128)S(1)} all-to-all(f32[16,8,128]{2,1,0:T(8,128)S(1)} %get-tuple-element.69), channel_id=1, replica_groups=mesh['group'=2,'space'=8,'rep'=2] {'space','rep'}, dimensions={0} | all-to-all | bytes 131072 | tf_op jit(solution)/shard_map/all_to_all | solution.py:66
  54.3 4.5 %shard_map.131 = (f32[2,256,256]{2,1,0:T(8,128)S(1)}, f32[1024,128]{1,0:T(8,128)S(1)}, f32[8,128]{1,0:T(8,128)S(1)}, f32[16,8,128]{2,1,0:T(8,128)S(1)}) custom-call(f32[16,8,128]{2,1,0:T(8,128)S(1)} %all_to_all.22.got_ref, f32[6,128,1024]{2,1,0:T(8,128)S(1)} %get-tuple-element.62.pre_ref, f32[6,128,1024]{2,1,0:T(8,128)S(1)} %get-tuple-element.70.grad_ref, ...), custom_call_target="tpu_custom_call" | custom-call | flops 1000000000 | bytes 4000000 | tf_op jit(solution)/shard_map/pallas_call | solution.py:91
  58.7 9.5 %all_to_all.23.got_ref = f32[16,8,128]{2,1,0:T(8,128)S(1)} all-to-all(f32[16,8,128]{2,1,0:T(8,128)S(1)} %get-tuple-element.75), channel_id=1, replica_groups=mesh['group'=2,'space'=8,'rep'=2] {'space','rep'}, dimensions={0} | all-to-all | bytes 131072 | tf_op jit(solution)/shard_map/all_to_all | solution.py:66
  68.2 1.5 %shard_map.132 = (bf16[1280,128]{1,0:T(8,128)(2,1)S(1)}, bf16[1280,128]{1,0:T(8,128)(2,1)S(1)}, f32[1280,128]{1,0:T(8,128)S(1)}, f32[1280,128]{1,0:T(8,128)S(1)}...) custom-call(f32[16,8,128]{2,1,0:T(8,128)S(1)} %all_to_all.23.got_ref, ...), custom_call_target="tpu_custom_call" | custom-call | flops 1000000000 | bytes 4000000 | tf_op jit(solution)/shard_map/pallas_call | solution.py:91
  69.7 0.1 collective-permute-start.8
  69.9 0.4 collective-permute-start.4
  70.3 1.2 %collective-permute-done.8 = bf16[1280,128]{1,0:T(8,128)(2,1)} collective-permute-done((bf16[1280,128]{1,0:T(8,128)(2,1)S(1)}, bf16[1280,128]{1,0:T(8,128)(2,1)}, u32[]{:S(2)}, u32[]{:S(2)}) %collective-permute-start.8) | collective-permute-done | bytes 327712 | tf_op jit(solution)/shard_map/ppermute | solution.py:37
  71.5 1.0 convert_add_fusion
  72.6 0.2 collective-permute-start.9
  72.9 0.7 collective-permute-start.5
  73.6 5.3 %collective-permute-done.9 = bf16[640,128]{1,0:T(8,128)(2,1)S(1)} collective-permute-done((bf16[640,128]{1,0:T(8,128)(2,1)S(1)}, bf16[640,128]{1,0:T(8,128)(2,1)S(1)}, u32[]{:S(2)}, u32[]{:S(2)}) %collective-permute-start.9) | collective-permute-done | bytes 163872 | tf_op jit(solution)/shard_map/ppermute | solution.py:37
  79.0 0.2 collective-permute-start.10
  79.2 1.7 %collective-permute-start.6 = (bf16[320,128]{1,0:T(8,128)(2,1)S(1)}, bf16[320,128]{1,0:T(8,128)(2,1)S(1)}, u32[]{:S(2)}, u32[]{:S(2)}) collective-permute-start(bf16[320,128]{1,0:T(8,128)(2,1)S(1)} %dynamic-slice_convert_fusion.3), channel_id=1, source_target_pairs={{0,2},{2,0},{4,6},{6,4},{8,10},{10,8},{12,14},{14,12},{1,3},{3,1},... | collective-permute-start | bytes 245768 | tf_op jit(solution)/shard_map/ppermute | solution.py:37
  81.0 2.5 %collective-permute-done.10 = bf16[320,128]{1,0:T(8,128)(2,1)S(1)} collective-permute-done((bf16[320,128]{1,0:T(8,128)(2,1)S(1)}, bf16[320,128]{1,0:T(8,128)(2,1)S(1)}, u32[]{:S(2)}, u32[]{:S(2)}) %collective-permute-start.10) | collective-permute-done | bytes 81952 | tf_op jit(solution)/shard_map/ppermute | solution.py:37
  83.5 0.3 collective-permute-start.11
  83.9 2.8 %collective-permute-start.7 = (bf16[160,128]{1,0:T(8,128)(2,1)S(1)}, bf16[160,128]{1,0:T(8,128)(2,1)S(1)}, u32[]{:S(2)}, u32[]{:S(2)}) collective-permute-start(bf16[160,128]{1,0:T(8,128)(2,1)S(1)} %dynamic-slice_convert_fusion.5), channel_id=1, source_target_pairs={{0,8},{2,10},{4,12},{6,14},{8,0},{10,2},{12,4},{14,6},{1,9},{3,11}... | collective-permute-start | bytes 122888 | tf_op jit(solution)/shard_map/ppermute | solution.py:37
  86.6 1.9 %collective-permute-done.11 = bf16[160,128]{1,0:T(8,128)(2,1)S(1)} collective-permute-done((bf16[160,128]{1,0:T(8,128)(2,1)S(1)}, bf16[160,128]{1,0:T(8,128)(2,1)S(1)}, u32[]{:S(2)}, u32[]{:S(2)}) %collective-permute-start.11) | collective-permute-done | bytes 40992 | tf_op jit(solution)/shard_map/ppermute | solution.py:37
  88.5 0.4 collective-permute-done.7
  89.0 2.7 %collective-permute-start.12 = (bf16[160,128]{1,0:T(8,128)(2,1)S(1)}, bf16[160,128]{1,0:T(8,128)(2,1)S(1)}, u32[]{:S(2)}, u32[]{:S(2)}) collective-permute-start(bf16[160,128]{1,0:T(8,128)(2,1)S(1)} %add_convert_fusion.1), channel_id=1, source_target_pairs={{0,8},{2,10},{4,12},{6,14},{8,0},{10,2},{12,4},{14,6},{1,9},{3,11}... | collective-permute-start | bytes 122888 | tf_op jit(solution)/shard_map/ppermute | solution.py:37
  91.6 0.3 collective-permute-start.14
  91.9 1.9 %collective-permute-start.16 = (bf16[128,256]{1,0:T(8,128)(2,1)S(1)}, bf16[128,256]{1,0:T(8,128)(2,1)S(1)}, u32[]{:S(2)}, u32[]{:S(2)}) collective-permute-start(bf16[128,256]{1,0:T(8,128)(2,1)S(1)} %get-tuple-element.90), channel_id=1, source_target_pairs={{0,2},{2,0},{4,6},{6,4},{8,10},{10,8},{12,14},{14,12},{1,3},{3,1},... | collective-permute-start | bytes 196616 | tf_op jit(solution)/shard_map/ppermute | solution.py:37
  93.8 0.7 collective-permute-start.17
  94.5 2.9 %collective-permute-start.13 = (bf16[320,128]{1,0:T(8,128)(2,1)S(1)}, bf16[320,128]{1,0:T(8,128)(2,1)S(1)}, u32[]{:S(2)}, u32[]{:S(2)}) collective-permute-start(bf16[320,128]{1,0:T(8,128)(2,1)S(1)} %maximum_select_fusion.4), channel_id=1, source_target_pairs={{0,2},{2,0},{4,6},{6,4},{8,10},{10,8},{12,14},{14,12},{1,3},{3,1},... | collective-permute-start | bytes 245768 | tf_op jit(solution)/shard_map/ppermute | solution.py:37
  97.5 1.6 %collective-permute-start.15 = (bf16[320,128]{1,0:T(8,128)(2,1)S(1)}, bf16[320,128]{1,0:T(8,128)(2,1)S(1)}, u32[]{:S(2)}, u32[]{:S(2)}) collective-permute-start(bf16[320,128]{1,0:T(8,128)(2,1)S(1)} %maximum_select_fusion.5), channel_id=1, source_target_pairs={{0,4},{2,6},{4,0},{6,2},{8,12},{10,14},{12,8},{14,10},{1,5},{3,7},... | collective-permute-start | bytes 245768 | tf_op jit(solution)/shard_map/ppermute | solution.py:37
  99.1 1.3 %collective-permute-done.13 = bf16[320,128]{1,0:T(8,128)(2,1)S(1)} collective-permute-done((bf16[320,128]{1,0:T(8,128)(2,1)S(1)}, bf16[320,128]{1,0:T(8,128)(2,1)S(1)}, u32[]{:S(2)}, u32[]{:S(2)}) %collective-permute-start.13) | collective-permute-done | bytes 81952 | tf_op jit(solution)/shard_map/ppermute | solution.py:37
  100.4 2.5 %collective-permute-done.15 = bf16[320,128]{1,0:T(8,128)(2,1)S(1)} collective-permute-done((bf16[320,128]{1,0:T(8,128)(2,1)S(1)}, bf16[320,128]{1,0:T(8,128)(2,1)S(1)}, u32[]{:S(2)}, u32[]{:S(2)}) %collective-permute-start.15) | collective-permute-done | bytes 81952 | tf_op jit(solution)/shard_map/ppermute | solution.py:37
  102.9 0.1 collective-permute-start.19
  103.0 2.0 %collective-permute-start.18 = (bf16[640,128]{1,0:T(8,128)(2,1)S(1)}, bf16[640,128]{1,0:T(8,128)(2,1)S(1)}, u32[]{:S(2)}, u32[]{:S(2)}) collective-permute-start(bf16[640,128]{1,0:T(8,128)(2,1)S(1)} %maximum_select_fusion.2), channel_id=1, source_target_pairs={{0,4},{2,6},{4,0},{6,2},{8,12},{10,14},{12,8},{14,10},{1,5},{3,7},... | collective-permute-start | bytes 491528 | tf_op jit(solution)/shard_map/ppermute | solution.py:37
  105.0 1.5 %shard_map.133 = bf16[128,4096]{1,0:T(8,128)(2,1)S(1)} custom-call(bf16[4,128,1024]{2,1,0:T(8,128)(2,1)S(1)} %get-tuple-element.88.feat_ref), custom_call_target="tpu_custom_call" | custom-call | flops 1000000000 | bytes 4000000 | tf_op jit(solution)/shard_map/pallas_call | solution.py:91
  106.5 1.8 %copy.20 = bf16[4,32,4096]{2,0,1:T(4,128)(2,1)} copy(bf16[4,32,4096]{2,1,0:T(8,128)(2,1)S(1)} %bitcast.28) | data formatting | bytes 2097152 | tf_op jit(solution)/shard_map/reshape | solution.py:719
  108.3 0.1 maximum_select_fusion.1.own_b_ref
  108.4 0.1 maximum_select_fusion.own_a_ref
  108.6 0.5 collective-permute-start.21
  109.1 0.6 slice.15
  109.7 0.6 slice.14
  110.2 0.8 copy.16
  111.0 1.9 %shard_map.134 = (f32[4096,128]{1,0:T(8,128)}, f32[2048,64]{1,0:T(8,128)}) custom-call(bf16[1280,128]{1,0:T(8,128)(2,1)S(1)} %maximum_select_fusion.own_a_ref, bf16[1280,128]{1,0:T(8,128)(2,1)S(1)} %maximum_select_fusion.1.own_b_ref, bf16[1280,128]{1,0:T(8,128)(2,1)S(1)} %collective-permute-done.20.other_a_ref, ...), custom_call_target="tpu_custom_call" | custom-call | flops 1000000000 | bytes 4000000 | tf_op jit(solution)/shard_map/pallas_call | solution.py:91
  (49 shorter events, 0.7 us)
Async XLA Ops:
  0.6 10.7 %copy-start.1 = (bf16[64,64,128]{2,1,0:T(8,128)(2,1)S(1)}, bf16[64,64,128]{2,1,0:T(8,128)(2,1)}, u32[]{:S(2)}) copy-start(bf16[64,64,128]{2,1,0:T(8,128)(2,1)} %param.9) | copy-start | bytes 3145732
  0.6 10.7 %copy-start.2 = (bf16[64,32,64]{2,1,0:T(8,128)(2,1)S(1)}, bf16[64,32,64]{2,1,0:T(8,128)(2,1)}, u32[]{:S(2)}) copy-start(bf16[64,32,64]{2,1,0:T(8,128)(2,1)} %param.12) | copy-start | bytes 786436
  0.7 10.7 %copy-start.3 = (f32[64]{0:T(128)S(1)}, f32[64]{0:T(128)}, u32[]{:S(2)}) copy-start(f32[64]{0:T(128)} %param.10) | copy-start | bytes 772
  0.7 10.7 %copy-start.4 = (f32[64]{0:T(128)S(1)}, f32[64]{0:T(128)}, u32[]{:S(2)}) copy-start(f32[64]{0:T(128)} %param.11) | copy-start | bytes 772
  0.7 10.7 %copy-start.5 = (f32[32]{0:T(128)S(1)}, f32[32]{0:T(128)}, u32[]{:S(2)}) copy-start(f32[32]{0:T(128)} %param.13) | copy-start | bytes 388
  0.7 10.7 %copy-start.6 = (f32[32]{0:T(128)S(1)}, f32[32]{0:T(128)}, u32[]{:S(2)}) copy-start(f32[32]{0:T(128)} %param.14) | copy-start | bytes 388
  0.7 12.7 %collective-permute-start = (bf16[128,256]{1,0:T(8,128)(2,1)}, bf16[128,256]{1,0:T(8,128)(2,1)S(1)}, u32[]{:S(2)}, u32[]{:S(2)}) collective-permute-start(bf16[128,256]{1,0:T(8,128)(2,1)} %bitcast.29), channel_id=1, source_target_pairs={{0,2},{2,0},{4,6},{6,4},{8,10},{10,8},{12,14},{14,12},{1,3},{3,1},... | collective-permute-start | bytes 196616 | tf_op jit(solution)/shard_map/ppermute | solution.py:37
  3.7 9.6 %collective-permute-start.1 = (bf16[128,256]{1,0:T(8,128)(2,1)}, bf16[128,256]{1,0:T(8,128)(2,1)S(1)}, u32[]{:S(2)}, u32[]{:S(2)}) collective-permute-start(bf16[128,256]{1,0:T(8,128)(2,1)} %bitcast.30), channel_id=1, source_target_pairs={{2,4},{6,8},{10,12},{4,2},{8,6},{12,10},{3,5},{7,9},{11,13},{5,3},... | collective-permute-start | bytes 196616 | tf_op jit(solution)/shard_map/ppermute | solution.py:80
  6.2 7.2 %copy-start = (bf16[1,128,1,256]{3,1,2,0:T(8,128)(2,1)S(1)}, bf16[1,128,1,256]{3,1,2,0:T(8,128)(2,1)}, u32[]{:S(2)}) copy-start(bf16[1,128,1,256]{3,1,2,0:T(8,128)(2,1)} %param.8) | copy-start | bytes 196612
  6.3 26.3 %collective-permute-start.2 = (bf16[32,4096]{1,0:T(8,128)(2,1)S(1)}, bf16[32,4096]{1,0:T(8,128)(2,1)S(1)}, u32[]{:S(2)}, u32[]{:S(2)}) collective-permute-start(bf16[32,4096]{1,0:T(8,128)(2,1)S(1)} %get-tuple-element.109), channel_id=1, source_target_pairs={{0,2},{2,0},{4,6},{6,4},{8,10},{10,8},{12,14},{14,12},{1,3},{3,1},... | collective-permute-start | bytes 786440 | tf_op jit(solution)/shard_map/ppermute | solution.py:37
  10.6 22.0 %collective-permute-start.3 = (bf16[32,4096]{1,0:T(8,128)(2,1)S(1)}, bf16[32,4096]{1,0:T(8,128)(2,1)S(1)}, u32[]{:S(2)}, u32[]{:S(2)}) collective-permute-start(bf16[32,4096]{1,0:T(8,128)(2,1)S(1)} %get-tuple-element.108), channel_id=1, source_target_pairs={{2,4},{6,8},{10,12},{4,2},{8,6},{12,10},{3,5},{7,9},{11,13},{5,3},... | collective-permute-start | bytes 786440 | tf_op jit(solution)/shard_map/ppermute | solution.py:80
  69.7 1.8 %collective-permute-start.8 = (bf16[1280,128]{1,0:T(8,128)(2,1)S(1)}, bf16[1280,128]{1,0:T(8,128)(2,1)}, u32[]{:S(2)}, u32[]{:S(2)}) collective-permute-start(bf16[1280,128]{1,0:T(8,128)(2,1)S(1)} %get-tuple-element.85), channel_id=1, source_target_pairs={{0,1},{1,0},{2,3},{3,2},{4,5},{5,4},{6,7},{7,6},{8,9},{9,8},{10,11... | collective-permute-start | bytes 983048 | tf_op jit(solution)/shard_map/ppermute | solution.py:37
  69.9 2.9 %collective-permute-start.4 = (bf16[1280,128]{1,0:T(8,128)(2,1)S(1)}, bf16[1280,128]{1,0:T(8,128)(2,1)S(1)}, u32[]{:S(2)}, u32[]{:S(2)}) collective-permute-start(bf16[1280,128]{1,0:T(8,128)(2,1)S(1)} %get-tuple-element.83), channel_id=1, source_target_pairs={{0,1},{1,0},{2,3},{3,2},{4,5},{5,4},{6,7},{7,6},{8,9},{9,8},{10,11... | collective-permute-start | bytes 983048 | tf_op jit(solution)/shard_map/ppermute | solution.py:37
  72.6 6.3 %collective-permute-start.9 = (bf16[640,128]{1,0:T(8,128)(2,1)S(1)}, bf16[640,128]{1,0:T(8,128)(2,1)S(1)}, u32[]{:S(2)}, u32[]{:S(2)}) collective-permute-start(bf16[640,128]{1,0:T(8,128)(2,1)S(1)} %dynamic-slice_convert_fusion), channel_id=1, source_target_pairs={{0,2},{2,0},{4,6},{6,4},{8,10},{10,8},{12,14},{14,12},{1,3},{3,1},... | collective-permute-start | bytes 491528 | tf_op jit(solution)/shard_map/ppermute | solution.py:37
  72.9 6.3 %collective-permute-start.5 = (bf16[640,128]{1,0:T(8,128)(2,1)S(1)}, bf16[640,128]{1,0:T(8,128)(2,1)S(1)}, u32[]{:S(2)}, u32[]{:S(2)}) collective-permute-start(bf16[640,128]{1,0:T(8,128)(2,1)S(1)} %dynamic-slice_convert_fusion.1), channel_id=1, source_target_pairs={{0,4},{2,6},{4,0},{6,2},{8,12},{10,14},{12,8},{14,10},{1,5},{3,7},... | collective-permute-start | bytes 491528 | tf_op jit(solution)/shard_map/ppermute | solution.py:37
  79.0 4.5 %collective-permute-start.10 = (bf16[320,128]{1,0:T(8,128)(2,1)S(1)}, bf16[320,128]{1,0:T(8,128)(2,1)S(1)}, u32[]{:S(2)}, u32[]{:S(2)}) collective-permute-start(bf16[320,128]{1,0:T(8,128)(2,1)S(1)} %dynamic-slice_convert_fusion.2), channel_id=1, source_target_pairs={{0,4},{2,6},{4,0},{6,2},{8,12},{10,14},{12,8},{14,10},{1,5},{3,7},... | collective-permute-start | bytes 245768 | tf_op jit(solution)/shard_map/ppermute | solution.py:37
  79.2 4.6 %collective-permute-start.6 = (bf16[320,128]{1,0:T(8,128)(2,1)S(1)}, bf16[320,128]{1,0:T(8,128)(2,1)S(1)}, u32[]{:S(2)}, u32[]{:S(2)}) collective-permute-start(bf16[320,128]{1,0:T(8,128)(2,1)S(1)} %dynamic-slice_convert_fusion.3), channel_id=1, source_target_pairs={{0,2},{2,0},{4,6},{6,4},{8,10},{10,8},{12,14},{14,12},{1,3},{3,1},... | collective-permute-start | bytes 245768 | tf_op jit(solution)/shard_map/ppermute | solution.py:37
  83.5 5.0 %collective-permute-start.11 = (bf16[160,128]{1,0:T(8,128)(2,1)S(1)}, bf16[160,128]{1,0:T(8,128)(2,1)S(1)}, u32[]{:S(2)}, u32[]{:S(2)}) collective-permute-start(bf16[160,128]{1,0:T(8,128)(2,1)S(1)} %dynamic-slice_convert_fusion.4), channel_id=1, source_target_pairs={{0,8},{2,10},{4,12},{6,14},{8,0},{10,2},{12,4},{14,6},{1,9},{3,11}... | collective-permute-start | bytes 122888 | tf_op jit(solution)/shard_map/ppermute | solution.py:37
  83.9 5.1 %collective-permute-start.7 = (bf16[160,128]{1,0:T(8,128)(2,1)S(1)}, bf16[160,128]{1,0:T(8,128)(2,1)S(1)}, u32[]{:S(2)}, u32[]{:S(2)}) collective-permute-start(bf16[160,128]{1,0:T(8,128)(2,1)S(1)} %dynamic-slice_convert_fusion.5), channel_id=1, source_target_pairs={{0,8},{2,10},{4,12},{6,14},{8,0},{10,2},{12,4},{14,6},{1,9},{3,11}... | collective-permute-start | bytes 122888 | tf_op jit(solution)/shard_map/ppermute | solution.py:37
  89.0 5.5 %collective-permute-start.12 = (bf16[160,128]{1,0:T(8,128)(2,1)S(1)}, bf16[160,128]{1,0:T(8,128)(2,1)S(1)}, u32[]{:S(2)}, u32[]{:S(2)}) collective-permute-start(bf16[160,128]{1,0:T(8,128)(2,1)S(1)} %add_convert_fusion.1), channel_id=1, source_target_pairs={{0,8},{2,10},{4,12},{6,14},{8,0},{10,2},{12,4},{14,6},{1,9},{3,11}... | collective-permute-start | bytes 122888 | tf_op jit(solution)/shard_map/ppermute | solution.py:37
  91.6 5.8 %collective-permute-start.14 = (bf16[160,128]{1,0:T(8,128)(2,1)S(1)}, bf16[160,128]{1,0:T(8,128)(2,1)S(1)}, u32[]{:S(2)}, u32[]{:S(2)}) collective-permute-start(bf16[160,128]{1,0:T(8,128)(2,1)S(1)} %add_convert_fusion), channel_id=1, source_target_pairs={{0,8},{2,10},{4,12},{6,14},{8,0},{10,2},{12,4},{14,6},{1,9},{3,11}... | collective-permute-start | bytes 122888 | tf_op jit(solution)/shard_map/ppermute | solution.py:37
  91.9 11.1 %collective-permute-start.16 = (bf16[128,256]{1,0:T(8,128)(2,1)S(1)}, bf16[128,256]{1,0:T(8,128)(2,1)S(1)}, u32[]{:S(2)}, u32[]{:S(2)}) collective-permute-start(bf16[128,256]{1,0:T(8,128)(2,1)S(1)} %get-tuple-element.90), channel_id=1, source_target_pairs={{0,2},{2,0},{4,6},{6,4},{8,10},{10,8},{12,14},{14,12},{1,3},{3,1},... | collective-permute-start | bytes 196616 | tf_op jit(solution)/shard_map/ppermute | solution.py:37
  93.8 9.2 %collective-permute-start.17 = (bf16[128,256]{1,0:T(8,128)(2,1)S(1)}, bf16[128,256]{1,0:T(8,128)(2,1)S(1)}, u32[]{:S(2)}, u32[]{:S(2)}) collective-permute-start(bf16[128,256]{1,0:T(8,128)(2,1)S(1)} %get-tuple-element.91), channel_id=1, source_target_pairs={{2,4},{6,8},{10,12},{4,2},{8,6},{12,10},{3,5},{7,9},{11,13},{5,3},... | collective-permute-start | bytes 196616 | tf_op jit(solution)/shard_map/ppermute | solution.py:80
  94.5 5.8 %collective-permute-start.13 = (bf16[320,128]{1,0:T(8,128)(2,1)S(1)}, bf16[320,128]{1,0:T(8,128)(2,1)S(1)}, u32[]{:S(2)}, u32[]{:S(2)}) collective-permute-start(bf16[320,128]{1,0:T(8,128)(2,1)S(1)} %maximum_select_fusion.4), channel_id=1, source_target_pairs={{0,2},{2,0},{4,6},{6,4},{8,10},{10,8},{12,14},{14,12},{1,3},{3,1},... | collective-permute-start | bytes 245768 | tf_op jit(solution)/shard_map/ppermute | solution.py:37
  97.5 5.4 %collective-permute-start.15 = (bf16[320,128]{1,0:T(8,128)(2,1)S(1)}, bf16[320,128]{1,0:T(8,128)(2,1)S(1)}, u32[]{:S(2)}, u32[]{:S(2)}) collective-permute-start(bf16[320,128]{1,0:T(8,128)(2,1)S(1)} %maximum_select_fusion.5), channel_id=1, source_target_pairs={{0,4},{2,6},{4,0},{6,2},{8,12},{10,14},{12,8},{14,10},{1,5},{3,7},... | collective-permute-start | bytes 245768 | tf_op jit(solution)/shard_map/ppermute | solution.py:37
  102.9 5.4 %collective-permute-start.19 = (bf16[640,128]{1,0:T(8,128)(2,1)S(1)}, bf16[640,128]{1,0:T(8,128)(2,1)S(1)}, u32[]{:S(2)}, u32[]{:S(2)}) collective-permute-start(bf16[640,128]{1,0:T(8,128)(2,1)S(1)} %maximum_select_fusion.3), channel_id=1, source_target_pairs={{0,2},{2,0},{4,6},{6,4},{8,10},{10,8},{12,14},{14,12},{1,3},{3,1},... | collective-permute-start | bytes 491528 | tf_op jit(solution)/shard_map/ppermute | solution.py:37
  103.0 5.4 %collective-permute-start.18 = (bf16[640,128]{1,0:T(8,128)(2,1)S(1)}, bf16[640,128]{1,0:T(8,128)(2,1)S(1)}, u32[]{:S(2)}, u32[]{:S(2)}) collective-permute-start(bf16[640,128]{1,0:T(8,128)(2,1)S(1)} %maximum_select_fusion.2), channel_id=1, source_target_pairs={{0,4},{2,6},{4,0},{6,2},{8,12},{10,14},{12,8},{14,10},{1,5},{3,7},... | collective-permute-start | bytes 491528 | tf_op jit(solution)/shard_map/ppermute | solution.py:37
  108.5 2.5 %collective-permute-start.20 = (bf16[1280,128]{1,0:T(8,128)(2,1)S(1)}, bf16[1280,128]{1,0:T(8,128)(2,1)S(1)}, u32[]{:S(2)}, u32[]{:S(2)}) collective-permute-start(bf16[1280,128]{1,0:T(8,128)(2,1)S(1)} %maximum_select_fusion.own_a_ref), channel_id=1, source_target_pairs={{0,1},{1,0},{2,3},{3,2},{4,5},{5,4},{6,7},{7,6},{8,9},{9,8},{10,11... | collective-permute-start | bytes 983048 | tf_op jit(solution)/shard_map/ppermute | solution.py:37
  108.6 2.4 %collective-permute-start.21 = (bf16[1280,128]{1,0:T(8,128)(2,1)S(1)}, bf16[1280,128]{1,0:T(8,128)(2,1)S(1)}, u32[]{:S(2)}, u32[]{:S(2)}) collective-permute-start(bf16[1280,128]{1,0:T(8,128)(2,1)S(1)} %maximum_select_fusion.1.own_b_ref), channel_id=1, source_target_pairs={{0,1},{1,0},{2,3},{3,2},{4,5},{5,4},{6,7},{7,6},{8,9},{9,8},{10,11... | collective-permute-start | bytes 983048 | tf_op jit(solution)/shard_map/ppermute | solution.py:37

commit v5 on v4

--- a/solution.py
+++ b/solution.py
@@ -218,28 +218,33 @@
     p2_ref[...] = jnp.concatenate(
         [jnp.concatenate([ref[...]] * 4, axis=1) for ref in (gain2_ref, shift2_ref)] + edges + blank
     )
-    a1_ref[...] = jnp.zeros(a1_ref.shape, BF16)
     for par in range(2):
         for rp in range(2):
             for cp in range(2):
-                row2 = par * 4 * C2 + (2 * rp + cp) * C2
-                pieces = [jnp.zeros((C2, C1), BF16)] * 18
+                row2 = ((2 * rp + par) * 2 + cp) * C2
+                pieces = [jnp.zeros((C2, C1), BF16)] * 12
                 for p, dp in PHASE_TAPS[par]:
                     dt = dp + 1 - par
                     for q, dr in PHASE_TAPS[rp]:
                         for r, dc in PHASE_TAPS[cp]:
                             tap = 16 * p + 4 * q + r
-                            slot = dt * 9 + (dr + 1) * 3 + dc + 1
-                            row = par * 4 * C1 + (2 * rp + cp) * C1
+                            slot = 2 * ((dr + 1 - rp) * 2 + dc + 1 - cp) + dt
+                            row = ((2 * rp + cp) * 2 + par) * C1
                             a1_ref[row : row + C1, slot * C0 : (slot + 1) * C0] = w1_ref[
                                 tap * C1 : (tap + 1) * C1, :
                             ]
+                            slot = 2 * ((dr + 1 - rp) * 3 + dc + 1) + dt
                             pieces[slot] = w2_ref[tap * C2 : (tap + 1) * C2, :]
                 a2_ref[row2 : row2 + C2, :] = jnp.concatenate(pieces, axis=1)
     for k in range(32):
         b1_ref[:, k * 128 : (k + 1) * 128] = jnp.transpose(w1_ref[k * 128 : (k + 1) * 128, :])
     for k in range(16):
         b2_ref[:, k * 128 : (k + 1) * 128] = jnp.transpose(w2_ref[k * 128 : (k + 1) * 128, :])
+
+
+def window_shifts(phase):
+    rp, cp = phase // 2, phase % 2
+    return [(rp + dr) * 3 + cp + dc for dr in range(2) for dc in range(2)]
 
 
 def first_kernel(
@@ -254,12 +259,18 @@
         if k != 4:
             moved = matmul(planes, sh_ref[:, k * CELLS : (k + 1) * CELLS]).astype(BF16)
         for z in range(3):
-            at = (z * 9 + k) * C0
+            at = (k * 3 + z) * C0
             x_ref[at : at + C0, :] = moved[z * C0 : (z + 1) * C0]
     for m in range(2):
-        both = matmul(a1_ref[...], x_ref[m * 9 * C0 : (m + 2) * 9 * C0, :])
-        pre_ref[2 * m + 1] = both[0 : 4 * C1]
-        pre_ref[2 * m] = both[4 * C1 : 8 * C1]
+        for phase in range(4):
+            cells = jnp.concatenate(
+                [x_ref[(k * 3 + m) * C0 : (k * 3 + m + 2) * C0, :] for k in window_shifts(phase)],
+                axis=0,
+            )
+            both = matmul(a1_ref[phase * 2 * C1 : (phase + 1) * 2 * C1, :], cells)
+            rows = slice(phase * C1, (phase + 1) * C1)
+            pre_ref[2 * m + 1, rows, :] = both[0:C1]
+            pre_ref[2 * m, rows, :] = both[C1 : 2 * C1]
     lower, upper = pre_ref[1], pre_ref[2]
     sums = fold(jnp.sum(lower + upper, axis=1, keepdims=True), C1)
     mean = sums / (8 * CELLS)
@@ -300,15 +311,24 @@
                         continue
                     lane = (2 * trp + tcp) * CELLS
                     for q in range(4):
-                        at = q * 9 * C1 + ((dr + 1) * 3 + dc + 1) * C1
+                        at = (((dr + 1) * 3 + dc + 1) * 4 + q) * C1
                         x_ref[at : at + C1, lane : lane + CELLS] = moved[q * C1 : (q + 1) * C1]
 
     for m in range(3):
         for block in range(4):
             lanes = slice(block * CELLS, (block + 1) * CELLS)
-            both = matmul(a2_ref[...], x_ref[m * 9 * C1 : (m + 2) * 9 * C1, lanes])
-            pre_ref[2 * m + 1, :, lanes] = both[0 : 4 * C2]
-            pre_ref[2 * m, :, lanes] = both[4 * C2 : 8 * C2]
+            for rp in range(2):
+                cells = jnp.concatenate(
+                    [
+                        x_ref[(k * 4 + m) * C1 : (k * 4 + m + 2) * C1, lanes]
+                        for k in range(3 * rp, 3 * rp + 6)
+                    ],
+                    axis=0,
+                )
+                both = matmul(a2_ref[rp * 4 * C2 : (rp + 1) * 4 * C2, :], cells)
+                rows = slice(rp * 2 * C2, (rp + 1) * 2 * C2)
+                pre_ref[2 * m + 1, rows, lanes] = both[0 : 2 * C2]
+                pre_ref[2 * m, rows, lanes] = both[2 * C2 : 4 * C2]
 
     partial = jnp.zeros((C2, CELLS), F32)
     for phase in range(4):
@@ -610,8 +630,8 @@
     a1, a2, b1, b2, sh, p1, p2, spread, matrix = call(
         prepare_kernel,
         [
-            ((8 * C1, 18 * C0), BF16),
-            ((8 * C2, 18 * C1), BF16),
+            ((8 * C1, 8 * C0), BF16),
+            ((8 * C2, 12 * C1), BF16),
             ((C0, 64 * C1), BF16),
             ((C1, 64 * C2), BF16),
             ((CELLS, 9 * CELLS), BF16),

time: 113 us -> 112 us (level)
  Pallas kernels: 19.9 us -> 18.5 us
    pallas_call x8, Pallas kernels: 19.9 us -> 18.5 us  [call(): pl.pallas_call(kernel, out_shape=[jax.ShapeDtypeStruct(shape, dtype) for...]
  transfers between devices with their start and end apart: 22 -> 22, of which waited for: 7 -> 7; matrix products, arithmetic and copies ran while one was open for 6% -> 6% of each run, Pallas kernels for 8% -> 7%
where the time goes in v5:
time: 112 us
  blocking collectives  41.8 us (37%)
  starting transfers between devices  27.7 us (25%)
  Pallas kernels  18.5 us (17%)
  waiting for transfers between devices  15.2 us (14%)
  local copies, waits for them, and re-layouts  5.68 us (5%)
  other arithmetic  1.58 us (1%)
  between operations  1.29 us (1%)
    all_to_all x4, blocking collectives, exchange(): return lax.all_to_all(copies, GROUP, 0, 0)  41.8 us
    ppermute x19, starting transfers between devices, swap(): lax.ppermute(block, axis, [(i, i ^ bit) for i in range(lax.axis_size(axis...  25.7 us
    pallas_call x8, Pallas kernels, call(): pl.pallas_call(kernel, out_shape=[jax.ShapeDtypeStruct(shape, dtype) for...  18.5 us
    ppermute x19, waiting for transfers between devices, swap(): lax.ppermute(block, axis, [(i, i ^ bit) for i in range(lax.axis_size(axis...  15.2 us
    unnamed x16, local copies, waits for them, and re-layouts  2.65 us
  transfers between devices with their start and end apart: 22, of which 7 were waited for; matrix products, arithmetic and copies ran while one was open for 6% of the time, Pallas kernels for 7%

profile of v5, /device:TPU:0, one launch (start us, length us, event | category | flops | bytes accessed | tf_op | source)
XLA Modules:
  0.0 111.7 jit_solution(18230066843314564451)
XLA Ops:
  0.7 3.0 %collective-permute-start = (bf16[128,256]{1,0:T(8,128)(2,1)}, bf16[128,256]{1,0:T(8,128)(2,1)S(1)}, u32[]{:S(2)}, u32[]{:S(2)}) collective-permute-start(bf16[128,256]{1,0:T(8,128)(2,1)} %bitcast.29), channel_id=1, source_target_pairs={{0,2},{2,0},{4,6},{6,4},{8,10},{10,8},{12,14},{14,12},{1,3},{3,1},... | collective-permute-start | bytes 196616 | tf_op jit(solution)/shard_map/ppermute | solution.py:37
  3.7 0.7 collective-permute-start.1
  4.4 1.8 %copy.21 = bf16[1,32,4,4096]{3,1,2,0:T(8,128)(2,1)S(1)} copy(bf16[1,32,4,4096]{3,2,1,0:T(4,128)(2,1)} %param.15) | data formatting | bytes 2097152 | tf_op args[7]
  6.3 4.3 %collective-permute-start.2 = (bf16[32,4096]{1,0:T(8,128)(2,1)S(1)}, bf16[32,4096]{1,0:T(8,128)(2,1)S(1)}, u32[]{:S(2)}, u32[]{:S(2)}) collective-permute-start(bf16[32,4096]{1,0:T(8,128)(2,1)S(1)} %get-tuple-element.109), channel_id=1, source_target_pairs={{0,2},{2,0},{4,6},{6,4},{8,10},{10,8},{12,14},{14,12},{1,3},{3,1},... | collective-permute-start | bytes 786440 | tf_op jit(solution)/shard_map/ppermute | solution.py:37
  10.6 0.7 collective-permute-start.3
  11.4 1.9 %shard_map.127 = (bf16[512,1024]{1,0:T(8,128)(2,1)S(1)}, bf16[256,768]{1,0:T(8,128)(2,1)S(1)}, bf16[128,4096]{1,0:T(8,128)(2,1)S(1)}, bf16[64,2048]{1,0:T(8,128)...) custom-call(bf16[4096,128]{1,0:T(8,128)(2,1)S(1)} %bitcast.33, ...), custom_call_target="tpu_custom_call" | custom-call | flops 1000000000 | bytes 4000000 | tf_op jit(solution)/shard_map/pallas_call | solution.py:91
  13.3 1.5 %shard_map.128 = (f32[4,256,256]{2,1,0:T(8,128)S(1)}, f32[16,8,128]{2,1,0:T(8,128)S(1)}, bf16[2,128,256]{2,1,0:T(8,128)(2,1)S(1)}) custom-call(bf16[128,256]{1,0:T(8,128)(2,1)S(1)} %bitcast.31, bf16[128,256]{1,0:T(8,128)(2,1)S(1)} %collective-permute-done.inner_ref, bf16[128,256]{1,0:T(8,128)(2,1)S(1)} %collective-permute-done.1.outer_ref, ...), custom_call_target="tpu_custom_call" | custom-call | flops 1000000000 | bytes 4000000 | tf_op jit(solution)/shard_map/pallas_call | solution.py:91
  14.8 13.4 %all_to_all.20.got_ref = f32[16,8,128]{2,1,0:T(8,128)S(1)} all-to-all(f32[16,8,128]{2,1,0:T(8,128)S(1)} %get-tuple-element.56), channel_id=1, replica_groups=mesh['group'=2,'space'=8,'rep'=2] {'space','rep'}, dimensions={0} | all-to-all | bytes 131072 | tf_op jit(solution)/shard_map/all_to_all | solution.py:66
  28.1 3.0 %shard_map.129 = (f32[6,128,1024]{2,1,0:T(8,128)S(1)}, bf16[128,1024]{1,0:T(8,128)(2,1)S(1)}, f32[8,128]{1,0:T(8,128)S(1)}, f32[16,8,128]{2,1,0:T(8,128)S(1)}) custom-call(f32[16,8,128]{2,1,0:T(8,128)S(1)} %all_to_all.20.got_ref, f32[4,256,256]{2,1,0:T(8,128)S(1)} %get-tuple-element.57.pre1_ref, f32[8,128]{1,0:T(8,128)S(1)} %get-tuple-element.58.p1_ref, ...), custom_call_target="tpu_custom_call" | custom-call | flops 1000000000 | bytes 4000000 | tf_op jit(solution)/shard_map/pallas_call | solution.py:91
  31.2 9.5 %all_to_all.21.got_ref = f32[16,8,128]{2,1,0:T(8,128)S(1)} all-to-all(f32[16,8,128]{2,1,0:T(8,128)S(1)} %get-tuple-element.61), channel_id=1, replica_groups=mesh['group'=2,'space'=8,'rep'=2] {'space','rep'}, dimensions={0} | all-to-all | bytes 131072 | tf_op jit(solution)/shard_map/all_to_all | solution.py:66
  40.7 2.7 %shard_map.130 = (f32[6,128,1024]{2,1,0:T(8,128)S(1)}, bf16[4,128,1024]{2,1,0:T(8,128)(2,1)S(1)}, f32[8,128]{1,0:T(8,128)S(1)}, f32[16,8,128]{2,1,0:T(8,128)S(1)}) custom-call(f32[16,8,128]{2,1,0:T(8,128)S(1)} %all_to_all.21.got_ref, f32[6,128,1024]{2,1,0:T(8,128)S(1)} %get-tuple-element.62.pre_ref, bf16[4,128,1024]{2,1,0:T(8,128)(2,1)S(1)} %get-tuple-element.63.cot_ref, ...), custom_call_target="tpu_custom_call" | custom-call | flops 1000000000 | bytes 4000000 | tf_op jit(solution)/shard_map/pallas_call | solution.py:91
  43.4 9.5 %all_to_all.22.got_ref = f32[16,8,128]{2,1,0:T(8,128)S(1)} all-to-all(f32[16,8,128]{2,1,0:T(8,128)S(1)} %get-tuple-element.69), channel_id=1, replica_groups=mesh['group'=2,'space'=8,'rep'=2] {'space','rep'}, dimensions={0} | all-to-all | bytes 131072 | tf_op jit(solution)/shard_map/all_to_all | solution.py:66
  52.8 4.5 %shard_map.131 = (f32[2,256,256]{2,1,0:T(8,128)S(1)}, f32[1024,128]{1,0:T(8,128)S(1)}, f32[8,128]{1,0:T(8,128)S(1)}, f32[16,8,128]{2,1,0:T(8,128)S(1)}) custom-call(f32[16,8,128]{2,1,0:T(8,128)S(1)} %all_to_all.22.got_ref, f32[6,128,1024]{2,1,0:T(8,128)S(1)} %get-tuple-element.62.pre_ref, f32[6,128,1024]{2,1,0:T(8,128)S(1)} %get-tuple-element.70.grad_ref, ...), custom_call_target="tpu_custom_call" | custom-call | flops 1000000000 | bytes 4000000 | tf_op jit(solution)/shard_map/pallas_call | solution.py:91
  57.3 9.5 %all_to_all.23.got_ref = f32[16,8,128]{2,1,0:T(8,128)S(1)} all-to-all(f32[16,8,128]{2,1,0:T(8,128)S(1)} %get-tuple-element.75), channel_id=1, replica_groups=mesh['group'=2,'space'=8,'rep'=2] {'space','rep'}, dimensions={0} | all-to-all | bytes 131072 | tf_op jit(solution)/shard_map/all_to_all | solution.py:66
  66.8 1.5 %shard_map.132 = (bf16[1280,128]{1,0:T(8,128)(2,1)S(1)}, bf16[1280,128]{1,0:T(8,128)(2,1)S(1)}, f32[1280,128]{1,0:T(8,128)S(1)}, f32[1280,128]{1,0:T(8,128)S(1)}...) custom-call(f32[16,8,128]{2,1,0:T(8,128)S(1)} %all_to_all.23.got_ref, ...), custom_call_target="tpu_custom_call" | custom-call | flops 1000000000 | bytes 4000000 | tf_op jit(solution)/shard_map/pallas_call | solution.py:91
  68.3 0.1 collective-permute-start.8
  68.5 0.4 collective-permute-start.4
  68.9 1.2 %collective-permute-done.8 = bf16[1280,128]{1,0:T(8,128)(2,1)} collective-permute-done((bf16[1280,128]{1,0:T(8,128)(2,1)S(1)}, bf16[1280,128]{1,0:T(8,128)(2,1)}, u32[]{:S(2)}, u32[]{:S(2)}) %collective-permute-start.8) | collective-permute-done | bytes 327712 | tf_op jit(solution)/shard_map/ppermute | solution.py:37
  70.1 1.0 convert_add_fusion
  71.2 0.2 collective-permute-start.9
  71.5 0.7 collective-permute-start.5
  72.2 5.3 %collective-permute-done.9 = bf16[640,128]{1,0:T(8,128)(2,1)S(1)} collective-permute-done((bf16[640,128]{1,0:T(8,128)(2,1)S(1)}, bf16[640,128]{1,0:T(8,128)(2,1)S(1)}, u32[]{:S(2)}, u32[]{:S(2)}) %collective-permute-start.9) | collective-permute-done | bytes 163872 | tf_op jit(solution)/shard_map/ppermute | solution.py:37
  77.6 0.2 collective-permute-start.10
  77.8 1.7 %collective-permute-start.6 = (bf16[320,128]{1,0:T(8,128)(2,1)S(1)}, bf16[320,128]{1,0:T(8,128)(2,1)S(1)}, u32[]{:S(2)}, u32[]{:S(2)}) collective-permute-start(bf16[320,128]{1,0:T(8,128)(2,1)S(1)} %dynamic-slice_convert_fusion.3), channel_id=1, source_target_pairs={{0,2},{2,0},{4,6},{6,4},{8,10},{10,8},{12,14},{14,12},{1,3},{3,1},... | collective-permute-start | bytes 245768 | tf_op jit(solution)/shard_map/ppermute | solution.py:37
  79.5 2.5 %collective-permute-done.10 = bf16[320,128]{1,0:T(8,128)(2,1)S(1)} collective-permute-done((bf16[320,128]{1,0:T(8,128)(2,1)S(1)}, bf16[320,128]{1,0:T(8,128)(2,1)S(1)}, u32[]{:S(2)}, u32[]{:S(2)}) %collective-permute-start.10) | collective-permute-done | bytes 81952 | tf_op jit(solution)/shard_map/ppermute | solution.py:37
  82.1 0.3 collective-permute-start.11
  82.4 2.8 %collective-permute-start.7 = (bf16[160,128]{1,0:T(8,128)(2,1)S(1)}, bf16[160,128]{1,0:T(8,128)(2,1)S(1)}, u32[]{:S(2)}, u32[]{:S(2)}) collective-permute-start(bf16[160,128]{1,0:T(8,128)(2,1)S(1)} %dynamic-slice_convert_fusion.5), channel_id=1, source_target_pairs={{0,8},{2,10},{4,12},{6,14},{8,0},{10,2},{12,4},{14,6},{1,9},{3,11}... | collective-permute-start | bytes 122888 | tf_op jit(solution)/shard_map/ppermute | solution.py:37
  85.2 1.9 %collective-permute-done.11 = bf16[160,128]{1,0:T(8,128)(2,1)S(1)} collective-permute-done((bf16[160,128]{1,0:T(8,128)(2,1)S(1)}, bf16[160,128]{1,0:T(8,128)(2,1)S(1)}, u32[]{:S(2)}, u32[]{:S(2)}) %collective-permute-start.11) | collective-permute-done | bytes 40992 | tf_op jit(solution)/shard_map/ppermute | solution.py:37
  87.1 0.4 collective-permute-done.7
  87.5 2.7 %collective-permute-start.12 = (bf16[160,128]{1,0:T(8,128)(2,1)S(1)}, bf16[160,128]{1,0:T(8,128)(2,1)S(1)}, u32[]{:S(2)}, u32[]{:S(2)}) collective-permute-start(bf16[160,128]{1,0:T(8,128)(2,1)S(1)} %add_convert_fusion.1), channel_id=1, source_target_pairs={{0,8},{2,10},{4,12},{6,14},{8,0},{10,2},{12,4},{14,6},{1,9},{3,11}... | collective-permute-start | bytes 122888 | tf_op jit(solution)/shard_map/ppermute | solution.py:37
  90.2 0.3 collective-permute-start.14
  90.5 1.9 %collective-permute-start.16 = (bf16[128,256]{1,0:T(8,128)(2,1)S(1)}, bf16[128,256]{1,0:T(8,128)(2,1)S(1)}, u32[]{:S(2)}, u32[]{:S(2)}) collective-permute-start(bf16[128,256]{1,0:T(8,128)(2,1)S(1)} %get-tuple-element.90), channel_id=1, source_target_pairs={{0,2},{2,0},{4,6},{6,4},{8,10},{10,8},{12,14},{14,12},{1,3},{3,1},... | collective-permute-start | bytes 196616 | tf_op jit(solution)/shard_map/ppermute | solution.py:37
  92.4 0.7 collective-permute-start.17
  93.1 2.9 %collective-permute-start.13 = (bf16[320,128]{1,0:T(8,128)(2,1)S(1)}, bf16[320,128]{1,0:T(8,128)(2,1)S(1)}, u32[]{:S(2)}, u32[]{:S(2)}) collective-permute-start(bf16[320,128]{1,0:T(8,128)(2,1)S(1)} %maximum_select_fusion.4), channel_id=1, source_target_pairs={{0,2},{2,0},{4,6},{6,4},{8,10},{10,8},{12,14},{14,12},{1,3},{3,1},... | collective-permute-start | bytes 245768 | tf_op jit(solution)/shard_map/ppermute | solution.py:37
  96.1 1.6 %collective-permute-start.15 = (bf16[320,128]{1,0:T(8,128)(2,1)S(1)}, bf16[320,128]{1,0:T(8,128)(2,1)S(1)}, u32[]{:S(2)}, u32[]{:S(2)}) collective-permute-start(bf16[320,128]{1,0:T(8,128)(2,1)S(1)} %maximum_select_fusion.5), channel_id=1, source_target_pairs={{0,4},{2,6},{4,0},{6,2},{8,12},{10,14},{12,8},{14,10},{1,5},{3,7},... | collective-permute-start | bytes 245768 | tf_op jit(solution)/shard_map/ppermute | solution.py:37
  97.7 1.3 %collective-permute-done.13 = bf16[320,128]{1,0:T(8,128)(2,1)S(1)} collective-permute-done((bf16[320,128]{1,0:T(8,128)(2,1)S(1)}, bf16[320,128]{1,0:T(8,128)(2,1)S(1)}, u32[]{:S(2)}, u32[]{:S(2)}) %collective-permute-start.13) | collective-permute-done | bytes 81952 | tf_op jit(solution)/shard_map/ppermute | solution.py:37
  99.0 2.5 %collective-permute-done.15 = bf16[320,128]{1,0:T(8,128)(2,1)S(1)} collective-permute-done((bf16[320,128]{1,0:T(8,128)(2,1)S(1)}, bf16[320,128]{1,0:T(8,128)(2,1)S(1)}, u32[]{:S(2)}, u32[]{:S(2)}) %collective-permute-start.15) | collective-permute-done | bytes 81952 | tf_op jit(solution)/shard_map/ppermute | solution.py:37
  101.5 0.1 collective-permute-start.19
  101.6 2.0 %collective-permute-start.18 = (bf16[640,128]{1,0:T(8,128)(2,1)S(1)}, bf16[640,128]{1,0:T(8,128)(2,1)S(1)}, u32[]{:S(2)}, u32[]{:S(2)}) collective-permute-start(bf16[640,128]{1,0:T(8,128)(2,1)S(1)} %maximum_select_fusion.2), channel_id=1, source_target_pairs={{0,4},{2,6},{4,0},{6,2},{8,12},{10,14},{12,8},{14,10},{1,5},{3,7},... | collective-permute-start | bytes 491528 | tf_op jit(solution)/shard_map/ppermute | solution.py:37
  103.6 1.5 %shard_map.133 = bf16[128,4096]{1,0:T(8,128)(2,1)S(1)} custom-call(bf16[4,128,1024]{2,1,0:T(8,128)(2,1)S(1)} %get-tuple-element.88.feat_ref), custom_call_target="tpu_custom_call" | custom-call | flops 1000000000 | bytes 4000000 | tf_op jit(solution)/shard_map/pallas_call | solution.py:91
  105.1 1.8 %copy.20 = bf16[4,32,4096]{2,0,1:T(4,128)(2,1)} copy(bf16[4,32,4096]{2,1,0:T(8,128)(2,1)S(1)} %bitcast.28) | data formatting | bytes 2097152 | tf_op jit(solution)/shard_map/reshape | solution.py:739
  106.9 0.1 maximum_select_fusion.1.own_b_ref
  107.0 0.1 maximum_select_fusion.own_a_ref
  107.2 0.5 collective-permute-start.21
  107.7 0.6 slice.15
  108.2 0.6 slice.14
  108.8 0.8 copy.16
  109.6 1.9 %shard_map.134 = (f32[4096,128]{1,0:T(8,128)}, f32[2048,64]{1,0:T(8,128)}) custom-call(bf16[1280,128]{1,0:T(8,128)(2,1)S(1)} %maximum_select_fusion.own_a_ref, bf16[1280,128]{1,0:T(8,128)(2,1)S(1)} %maximum_select_fusion.1.own_b_ref, bf16[1280,128]{1,0:T(8,128)(2,1)S(1)} %collective-permute-done.20.other_a_ref, ...), custom_call_target="tpu_custom_call" | custom-call | flops 1000000000 | bytes 4000000 | tf_op jit(solution)/shard_map/pallas_call | solution.py:91
  (49 shorter events, 0.7 us)
Async XLA Ops:
  0.6 10.7 %copy-start.1 = (bf16[64,64,128]{2,1,0:T(8,128)(2,1)S(1)}, bf16[64,64,128]{2,1,0:T(8,128)(2,1)}, u32[]{:S(2)}) copy-start(bf16[64,64,128]{2,1,0:T(8,128)(2,1)} %param.9) | copy-start | bytes 3145732
  0.6 10.7 %copy-start.2 = (bf16[64,32,64]{2,1,0:T(8,128)(2,1)S(1)}, bf16[64,32,64]{2,1,0:T(8,128)(2,1)}, u32[]{:S(2)}) copy-start(bf16[64,32,64]{2,1,0:T(8,128)(2,1)} %param.12) | copy-start | bytes 786436
  0.7 10.7 %copy-start.3 = (f32[64]{0:T(128)S(1)}, f32[64]{0:T(128)}, u32[]{:S(2)}) copy-start(f32[64]{0:T(128)} %param.10) | copy-start | bytes 772
  0.7 10.7 %copy-start.4 = (f32[64]{0:T(128)S(1)}, f32[64]{0:T(128)}, u32[]{:S(2)}) copy-start(f32[64]{0:T(128)} %param.11) | copy-start | bytes 772
  0.7 10.7 %copy-start.5 = (f32[32]{0:T(128)S(1)}, f32[32]{0:T(128)}, u32[]{:S(2)}) copy-start(f32[32]{0:T(128)} %param.13) | copy-start | bytes 388
  0.7 10.7 %copy-start.6 = (f32[32]{0:T(128)S(1)}, f32[32]{0:T(128)}, u32[]{:S(2)}) copy-start(f32[32]{0:T(128)} %param.14) | copy-start | bytes 388
  0.7 12.6 %collective-permute-start = (bf16[128,256]{1,0:T(8,128)(2,1)}, bf16[128,256]{1,0:T(8,128)(2,1)S(1)}, u32[]{:S(2)}, u32[]{:S(2)}) collective-permute-start(bf16[128,256]{1,0:T(8,128)(2,1)} %bitcast.29), channel_id=1, source_target_pairs={{0,2},{2,0},{4,6},{6,4},{8,10},{10,8},{12,14},{14,12},{1,3},{3,1},... | collective-permute-start | bytes 196616 | tf_op jit(solution)/shard_map/ppermute | solution.py:37
  3.7 9.5 %collective-permute-start.1 = (bf16[128,256]{1,0:T(8,128)(2,1)}, bf16[128,256]{1,0:T(8,128)(2,1)S(1)}, u32[]{:S(2)}, u32[]{:S(2)}) collective-permute-start(bf16[128,256]{1,0:T(8,128)(2,1)} %bitcast.30), channel_id=1, source_target_pairs={{2,4},{6,8},{10,12},{4,2},{8,6},{12,10},{3,5},{7,9},{11,13},{5,3},... | collective-permute-start | bytes 196616 | tf_op jit(solution)/shard_map/ppermute | solution.py:80
  4.4 8.9 %copy-start = (bf16[1,128,1,256]{3,1,2,0:T(8,128)(2,1)S(1)}, bf16[1,128,1,256]{3,1,2,0:T(8,128)(2,1)}, u32[]{:S(2)}) copy-start(bf16[1,128,1,256]{3,1,2,0:T(8,128)(2,1)} %param.8) | copy-start | bytes 196612
  6.3 24.9 %collective-permute-start.2 = (bf16[32,4096]{1,0:T(8,128)(2,1)S(1)}, bf16[32,4096]{1,0:T(8,128)(2,1)S(1)}, u32[]{:S(2)}, u32[]{:S(2)}) collective-permute-start(bf16[32,4096]{1,0:T(8,128)(2,1)S(1)} %get-tuple-element.109), channel_id=1, source_target_pairs={{0,2},{2,0},{4,6},{6,4},{8,10},{10,8},{12,14},{14,12},{1,3},{3,1},... | collective-permute-start | bytes 786440 | tf_op jit(solution)/shard_map/ppermute | solution.py:37
  10.6 20.6 %collective-permute-start.3 = (bf16[32,4096]{1,0:T(8,128)(2,1)S(1)}, bf16[32,4096]{1,0:T(8,128)(2,1)S(1)}, u32[]{:S(2)}, u32[]{:S(2)}) collective-permute-start(bf16[32,4096]{1,0:T(8,128)(2,1)S(1)} %get-tuple-element.108), channel_id=1, source_target_pairs={{2,4},{6,8},{10,12},{4,2},{8,6},{12,10},{3,5},{7,9},{11,13},{5,3},... | collective-permute-start | bytes 786440 | tf_op jit(solution)/shard_map/ppermute | solution.py:80
  68.3 1.8 %collective-permute-start.8 = (bf16[1280,128]{1,0:T(8,128)(2,1)S(1)}, bf16[1280,128]{1,0:T(8,128)(2,1)}, u32[]{:S(2)}, u32[]{:S(2)}) collective-permute-start(bf16[1280,128]{1,0:T(8,128)(2,1)S(1)} %get-tuple-element.85), channel_id=1, source_target_pairs={{0,1},{1,0},{2,3},{3,2},{4,5},{5,4},{6,7},{7,6},{8,9},{9,8},{10,11... | collective-permute-start | bytes 983048 | tf_op jit(solution)/shard_map/ppermute | solution.py:37
  68.5 2.9 %collective-permute-start.4 = (bf16[1280,128]{1,0:T(8,128)(2,1)S(1)}, bf16[1280,128]{1,0:T(8,128)(2,1)S(1)}, u32[]{:S(2)}, u32[]{:S(2)}) collective-permute-start(bf16[1280,128]{1,0:T(8,128)(2,1)S(1)} %get-tuple-element.83), channel_id=1, source_target_pairs={{0,1},{1,0},{2,3},{3,2},{4,5},{5,4},{6,7},{7,6},{8,9},{9,8},{10,11... | collective-permute-start | bytes 983048 | tf_op jit(solution)/shard_map/ppermute | solution.py:37
  71.2 6.3 %collective-permute-start.9 = (bf16[640,128]{1,0:T(8,128)(2,1)S(1)}, bf16[640,128]{1,0:T(8,128)(2,1)S(1)}, u32[]{:S(2)}, u32[]{:S(2)}) collective-permute-start(bf16[640,128]{1,0:T(8,128)(2,1)S(1)} %dynamic-slice_convert_fusion), channel_id=1, source_target_pairs={{0,2},{2,0},{4,6},{6,4},{8,10},{10,8},{12,14},{14,12},{1,3},{3,1},... | collective-permute-start | bytes 491528 | tf_op jit(solution)/shard_map/ppermute | solution.py:37
  71.5 6.3 %collective-permute-start.5 = (bf16[640,128]{1,0:T(8,128)(2,1)S(1)}, bf16[640,128]{1,0:T(8,128)(2,1)S(1)}, u32[]{:S(2)}, u32[]{:S(2)}) collective-permute-start(bf16[640,128]{1,0:T(8,128)(2,1)S(1)} %dynamic-slice_convert_fusion.1), channel_id=1, source_target_pairs={{0,4},{2,6},{4,0},{6,2},{8,12},{10,14},{12,8},{14,10},{1,5},{3,7},... | collective-permute-start | bytes 491528 | tf_op jit(solution)/shard_map/ppermute | solution.py:37
  77.6 4.5 %collective-permute-start.10 = (bf16[320,128]{1,0:T(8,128)(2,1)S(1)}, bf16[320,128]{1,0:T(8,128)(2,1)S(1)}, u32[]{:S(2)}, u32[]{:S(2)}) collective-permute-start(bf16[320,128]{1,0:T(8,128)(2,1)S(1)} %dynamic-slice_convert_fusion.2), channel_id=1, source_target_pairs={{0,4},{2,6},{4,0},{6,2},{8,12},{10,14},{12,8},{14,10},{1,5},{3,7},... | collective-permute-start | bytes 245768 | tf_op jit(solution)/shard_map/ppermute | solution.py:37
  77.8 4.6 %collective-permute-start.6 = (bf16[320,128]{1,0:T(8,128)(2,1)S(1)}, bf16[320,128]{1,0:T(8,128)(2,1)S(1)}, u32[]{:S(2)}, u32[]{:S(2)}) collective-permute-start(bf16[320,128]{1,0:T(8,128)(2,1)S(1)} %dynamic-slice_convert_fusion.3), channel_id=1, source_target_pairs={{0,2},{2,0},{4,6},{6,4},{8,10},{10,8},{12,14},{14,12},{1,3},{3,1},... | collective-permute-start | bytes 245768 | tf_op jit(solution)/shard_map/ppermute | solution.py:37
  82.1 5.0 %collective-permute-start.11 = (bf16[160,128]{1,0:T(8,128)(2,1)S(1)}, bf16[160,128]{1,0:T(8,128)(2,1)S(1)}, u32[]{:S(2)}, u32[]{:S(2)}) collective-permute-start(bf16[160,128]{1,0:T(8,128)(2,1)S(1)} %dynamic-slice_convert_fusion.4), channel_id=1, source_target_pairs={{0,8},{2,10},{4,12},{6,14},{8,0},{10,2},{12,4},{14,6},{1,9},{3,11}... | collective-permute-start | bytes 122888 | tf_op jit(solution)/shard_map/ppermute | solution.py:37
  82.4 5.1 %collective-permute-start.7 = (bf16[160,128]{1,0:T(8,128)(2,1)S(1)}, bf16[160,128]{1,0:T(8,128)(2,1)S(1)}, u32[]{:S(2)}, u32[]{:S(2)}) collective-permute-start(bf16[160,128]{1,0:T(8,128)(2,1)S(1)} %dynamic-slice_convert_fusion.5), channel_id=1, source_target_pairs={{0,8},{2,10},{4,12},{6,14},{8,0},{10,2},{12,4},{14,6},{1,9},{3,11}... | collective-permute-start | bytes 122888 | tf_op jit(solution)/shard_map/ppermute | solution.py:37
  87.5 5.5 %collective-permute-start.12 = (bf16[160,128]{1,0:T(8,128)(2,1)S(1)}, bf16[160,128]{1,0:T(8,128)(2,1)S(1)}, u32[]{:S(2)}, u32[]{:S(2)}) collective-permute-start(bf16[160,128]{1,0:T(8,128)(2,1)S(1)} %add_convert_fusion.1), channel_id=1, source_target_pairs={{0,8},{2,10},{4,12},{6,14},{8,0},{10,2},{12,4},{14,6},{1,9},{3,11}... | collective-permute-start | bytes 122888 | tf_op jit(solution)/shard_map/ppermute | solution.py:37
  90.2 5.8 %collective-permute-start.14 = (bf16[160,128]{1,0:T(8,128)(2,1)S(1)}, bf16[160,128]{1,0:T(8,128)(2,1)S(1)}, u32[]{:S(2)}, u32[]{:S(2)}) collective-permute-start(bf16[160,128]{1,0:T(8,128)(2,1)S(1)} %add_convert_fusion), channel_id=1, source_target_pairs={{0,8},{2,10},{4,12},{6,14},{8,0},{10,2},{12,4},{14,6},{1,9},{3,11}... | collective-permute-start | bytes 122888 | tf_op jit(solution)/shard_map/ppermute | solution.py:37
  90.5 11.1 %collective-permute-start.16 = (bf16[128,256]{1,0:T(8,128)(2,1)S(1)}, bf16[128,256]{1,0:T(8,128)(2,1)S(1)}, u32[]{:S(2)}, u32[]{:S(2)}) collective-permute-start(bf16[128,256]{1,0:T(8,128)(2,1)S(1)} %get-tuple-element.90), channel_id=1, source_target_pairs={{0,2},{2,0},{4,6},{6,4},{8,10},{10,8},{12,14},{14,12},{1,3},{3,1},... | collective-permute-start | bytes 196616 | tf_op jit(solution)/shard_map/ppermute | solution.py:37
  92.4 9.2 %collective-permute-start.17 = (bf16[128,256]{1,0:T(8,128)(2,1)S(1)}, bf16[128,256]{1,0:T(8,128)(2,1)S(1)}, u32[]{:S(2)}, u32[]{:S(2)}) collective-permute-start(bf16[128,256]{1,0:T(8,128)(2,1)S(1)} %get-tuple-element.91), channel_id=1, source_target_pairs={{2,4},{6,8},{10,12},{4,2},{8,6},{12,10},{3,5},{7,9},{11,13},{5,3},... | collective-permute-start | bytes 196616 | tf_op jit(solution)/shard_map/ppermute | solution.py:80
  93.1 5.8 %collective-permute-start.13 = (bf16[320,128]{1,0:T(8,128)(2,1)S(1)}, bf16[320,128]{1,0:T(8,128)(2,1)S(1)}, u32[]{:S(2)}, u32[]{:S(2)}) collective-permute-start(bf16[320,128]{1,0:T(8,128)(2,1)S(1)} %maximum_select_fusion.4), channel_id=1, source_target_pairs={{0,2},{2,0},{4,6},{6,4},{8,10},{10,8},{12,14},{14,12},{1,3},{3,1},... | collective-permute-start | bytes 245768 | tf_op jit(solution)/shard_map/ppermute | solution.py:37
  96.1 5.4 %collective-permute-start.15 = (bf16[320,128]{1,0:T(8,128)(2,1)S(1)}, bf16[320,128]{1,0:T(8,128)(2,1)S(1)}, u32[]{:S(2)}, u32[]{:S(2)}) collective-permute-start(bf16[320,128]{1,0:T(8,128)(2,1)S(1)} %maximum_select_fusion.5), channel_id=1, source_target_pairs={{0,4},{2,6},{4,0},{6,2},{8,12},{10,14},{12,8},{14,10},{1,5},{3,7},... | collective-permute-start | bytes 245768 | tf_op jit(solution)/shard_map/ppermute | solution.py:37
  101.5 5.4 %collective-permute-start.19 = (bf16[640,128]{1,0:T(8,128)(2,1)S(1)}, bf16[640,128]{1,0:T(8,128)(2,1)S(1)}, u32[]{:S(2)}, u32[]{:S(2)}) collective-permute-start(bf16[640,128]{1,0:T(8,128)(2,1)S(1)} %maximum_select_fusion.3), channel_id=1, source_target_pairs={{0,2},{2,0},{4,6},{6,4},{8,10},{10,8},{12,14},{14,12},{1,3},{3,1},... | collective-permute-start | bytes 491528 | tf_op jit(solution)/shard_map/ppermute | solution.py:37
  101.6 5.4 %collective-permute-start.18 = (bf16[640,128]{1,0:T(8,128)(2,1)S(1)}, bf16[640,128]{1,0:T(8,128)(2,1)S(1)}, u32[]{:S(2)}, u32[]{:S(2)}) collective-permute-start(bf16[640,128]{1,0:T(8,128)(2,1)S(1)} %maximum_select_fusion.2), channel_id=1, source_target_pairs={{0,4},{2,6},{4,0},{6,2},{8,12},{10,14},{12,8},{14,10},{1,5},{3,7},... | collective-permute-start | bytes 491528 | tf_op jit(solution)/shard_map/ppermute | solution.py:37
  107.1 2.5 %collective-permute-start.20 = (bf16[1280,128]{1,0:T(8,128)(2,1)S(1)}, bf16[1280,128]{1,0:T(8,128)(2,1)S(1)}, u32[]{:S(2)}, u32[]{:S(2)}) collective-permute-start(bf16[1280,128]{1,0:T(8,128)(2,1)S(1)} %maximum_select_fusion.own_a_ref), channel_id=1, source_target_pairs={{0,1},{1,0},{2,3},{3,2},{4,5},{5,4},{6,7},{7,6},{8,9},{9,8},{10,11... | collective-permute-start | bytes 983048 | tf_op jit(solution)/shard_map/ppermute | solution.py:37
  107.2 2.4 %collective-permute-start.21 = (bf16[1280,128]{1,0:T(8,128)(2,1)S(1)}, bf16[1280,128]{1,0:T(8,128)(2,1)S(1)}, u32[]{:S(2)}, u32[]{:S(2)}) collective-permute-start(bf16[1280,128]{1,0:T(8,128)(2,1)S(1)} %maximum_select_fusion.1.own_b_ref), channel_id=1, source_target_pairs={{0,1},{1,0},{2,3},{3,2},{4,5},{5,4},{6,7},{7,6},{8,9},{9,8},{10,11... | collective-permute-start | bytes 983048 | tf_op jit(solution)/shard_map/ppermute | solution.py:37
